TPU v7x, 128 devices: a whole 4x4x4 slice. The times are simulated.
128 devices in a mesh: seq: 8 (over y, x_lo), tok: 16 (over x_hi, z, core).
Axes of the slice: x: 4 (x_hi: 2, x_lo: 2; x = x_hi * 2 + x_lo), y: 4, z: 4, core: 2. Of those that a mesh axis runs over, the one named last changes fastest.
Arguments:
- tokens: bfloat16 [24576, 1024], P(('seq', 'tok')), may hold values from -6 to 6
- cotangent: bfloat16 [24576, 1024], P(('seq', 'tok')), may hold values from -6 to 6
- doc_lengths: int32 [8, 4], P('seq'), may hold values from 1 to 3069, as said below
- pad_counts: int32 [8], P('seq'), may hold values from 0 to 96, as said below
- w_query: bfloat16 [1024, 1024], P(('seq', 'tok')), may hold values from -0.25 to 0.25
- b_query: bfloat16 [1024], P(('seq', 'tok')), may hold values from -3 to 3
- w_key: bfloat16 [1024, 1024], P(('seq', 'tok')), may hold values from -0.25 to 0.25
- w_value: bfloat16 [1024, 1024], P(('seq', 'tok')), may hold values from -0.1875 to 0.1875
- b_value: bfloat16 [1024], P(('seq', 'tok')), may hold values from -3 to 3
- w_out: bfloat16 [1024, 1024], P(('seq', 'tok')), may hold values from -0.375 to 0.375
- b_out: bfloat16 [1024], P(('seq', 'tok')), may hold values from -3 to 3
- gain_attn: bfloat16 [1024], P(('seq', 'tok')), may hold values from 0.5 to 1.5
- shift_attn: bfloat16 [1024], P(('seq', 'tok')), may hold values from -3 to 3
- w_in: bfloat16 [1024, 4096], P(('seq', 'tok')), may hold values from -0.1875 to 0.1875
- b_in: bfloat16 [4096], P(('seq', 'tok')), may hold values from -3 to 3
- w_back: bfloat16 [4096, 1024], P(('seq', 'tok')), may hold values from -0.09375 to 0.09375
- b_back: bfloat16 [1024], P(('seq', 'tok')), may hold values from -3 to 3
- gain_ffn: bfloat16 [1024], P(('seq', 'tok')), may hold values from 0.5 to 1.5
- shift_ffn: bfloat16 [1024], P(('seq', 'tok')), may hold values from -3 to 3
Outputs:
- output: bfloat16 [24576, 1024], P(('seq', 'tok'))
- tokens_grad: bfloat16 [24576, 1024], P(('seq', 'tok'))
- grad_w_query: float32 [1024, 1024], P(('seq', 'tok'))
- grad_b_query: float32 [1024], P(('seq', 'tok'))
- grad_w_key: float32 [1024, 1024], P(('seq', 'tok'))
- grad_w_value: float32 [1024, 1024], P(('seq', 'tok'))
- grad_b_value: float32 [1024], P(('seq', 'tok'))
- grad_w_out: float32 [1024, 1024], P(('seq', 'tok'))
- grad_b_out: float32 [1024], P(('seq', 'tok'))
- grad_gain_attn: float32 [1024], P(('seq', 'tok'))
- grad_shift_attn: float32 [1024], P(('seq', 'tok'))
- grad_w_in: float32 [1024, 4096], P(('seq', 'tok'))
- grad_b_in: float32 [4096], P(('seq', 'tok'))
- grad_w_back: float32 [4096, 1024], P(('seq', 'tok'))
- grad_b_back: float32 [1024], P(('seq', 'tok'))
- grad_gain_ffn: float32 [1024], P(('seq', 'tok'))
- grad_shift_ffn: float32 [1024], P(('seq', 'tok'))
Inputs may be any that keep to these rules, and one draw needn't show every extreme that they name: `doc_lengths`: each row sums to 3072. Of each row one document starts within the first 192 positions and ends within the last 192; the other documents have at most 24 tokens. `pad_counts`: some sequence has 96 padding positions and another none.
All inputs are finite; a program needn't handle non-finite values.
Results may differ from a plain program's by a relative error of at most 0.03.
Values may be sent and summed in bfloat16 or wider, within the bound.
A program may use at most 256 MiB of HBM per device.

v0:
```python
import math

import jax
import jax.numpy as jnp
from jax import lax
from jax.sharding import PartitionSpec as P

HEADS = 16
WINDOW = 1024


EPSILON = 1e-05
MASKED = -1e30


def passed_along(value, axis, steps):
    count = lax.axis_size(axis)
    initial, last = (max(0, -steps), min(count, count - steps))
    return lax.ppermute(value, axis, [(source, source + steps) for source in range(initial, last)])


def bfloat(tensor):
    return tensor.astype(jnp.bfloat16)


def widen(tensor):
    return tensor.astype(jnp.float32)


def product(former, latter):
    return jnp.dot(former, latter, preferred_element_type=jnp.float32)


def product_tn(former, latter):
    return lax.dot_general(
        former, latter, (((0,), (0,)), ((), ())), preferred_element_type=jnp.float32
    )


def product_nt(former, latter):
    return lax.dot_general(
        former, latter, (((1,), (1,)), ((), ())), preferred_element_type=jnp.float32
    )


def smooth(tensor):
    return jax.nn.gelu(tensor, approximate=True)


def normalize(tensor, norm_gain, norm_shift):
    centred = tensor - jnp.mean(tensor, axis=-1, keepdims=True)
    factor = lax.rsqrt(jnp.mean(centred * centred, axis=-1, keepdims=True) + EPSILON)
    normed = centred * factor
    return (normed * widen(norm_gain) + widen(norm_shift), normed, factor)


def normalize_back(grad_out, normed, factor, norm_gain):
    grad_normed = grad_out * widen(norm_gain)
    grad_input = factor * (
        grad_normed
        - jnp.mean(grad_normed, axis=-1, keepdims=True)
        - normed * jnp.mean(grad_normed * normed, axis=-1, keepdims=True)
    )
    return (grad_input, jnp.sum(grad_out * normed, axis=0), jnp.sum(grad_out, axis=0))


def segment_of(places, doc_ends, live_rows):
    inside = jnp.sum((places[:, None] >= doc_ends[None, :]).astype(jnp.int32), axis=1)
    return jnp.where(places >= live_rows, doc_ends.shape[0], inside)


def near_blocks(stacked, reach_blocks):
    earlier = [passed_along(stacked, "tok", offset) for offset in range(reach_blocks, 0, -1)]
    later_blocks = [passed_along(stacked, "tok", -offset) for offset in range(1, reach_blocks + 1)]
    return jnp.concatenate(earlier + [stacked] + later_blocks, axis=1)


def return_blocks(grad_pairs, reach_blocks):
    tok_rows = grad_pairs.shape[1] // (2 * reach_blocks + 1)

    def block_of(index):
        return grad_pairs[:, index * tok_rows : (index + 1) * tok_rows]

    from_later = [
        passed_along(block_of(reach_blocks - offset).astype(jnp.bfloat16), "tok", -offset).astype(
            jnp.float32
        )
        for offset in range(1, reach_blocks + 1)
    ]
    from_earlier = [
        passed_along(block_of(reach_blocks + offset).astype(jnp.bfloat16), "tok", offset).astype(
            jnp.float32
        )
        for offset in range(1, reach_blocks + 1)
    ]
    return sum(from_later + from_earlier, block_of(reach_blocks))


def split_heads(tensor, head_count):
    return tensor.reshape(tensor.shape[0], head_count, tensor.shape[1] // head_count)


def scores_of(queries, near_keys, allowed, head_count):
    head_size = queries.shape[1] // head_count
    scaled = jnp.einsum(
        "qhd,khd->hqk",
        split_heads(queries, head_count),
        split_heads(near_keys, head_count),
        preferred_element_type=jnp.float32,
    ) * (1.0 / math.sqrt(head_size))
    return jnp.where(allowed[None], scaled, MASKED)


def attend_forward(queries, pairs, allowed, head_count):
    scores = scores_of(queries, pairs[0], allowed, head_count)
    highest = jnp.max(scores, axis=-1, keepdims=True)
    exponentials = jnp.exp(scores - highest)
    totals = jnp.sum(exponentials, axis=-1, keepdims=True)
    weights = bfloat(exponentials / totals)
    mixed = jnp.einsum(
        "hqk,khd->qhd",
        weights,
        split_heads(pairs[1], head_count),
        preferred_element_type=jnp.float32,
    )
    return (mixed.reshape(queries.shape), highest + jnp.log(totals))


def attend_back(queries, pairs, allowed, head_count, logsum, grad_mixed):
    head_size = queries.shape[1] // head_count
    scale = 1.0 / math.sqrt(head_size)
    scores = scores_of(queries, pairs[0], allowed, head_count)
    chances = jnp.exp(scores - logsum)
    grad_heads = split_heads(grad_mixed, head_count)
    grad_weights = jnp.einsum(
        "qhd,khd->hqk",
        grad_heads,
        split_heads(pairs[1], head_count),
        preferred_element_type=jnp.float32,
    )
    inner = jnp.sum(chances * grad_weights, axis=-1, keepdims=True)
    grad_scores = bfloat(chances * (grad_weights - inner))
    grad_queries = (
        jnp.einsum(
            "hqk,khd->qhd",
            grad_scores,
            split_heads(pairs[0], head_count),
            preferred_element_type=jnp.float32,
        )
        * scale
    )
    grad_keys = (
        jnp.einsum(
            "hqk,qhd->khd",
            grad_scores,
            split_heads(queries, head_count),
            preferred_element_type=jnp.float32,
        )
        * scale
    )
    grad_values = jnp.einsum(
        "hqk,qhd->khd", bfloat(chances), grad_heads, preferred_element_type=jnp.float32
    )
    key_count = pairs.shape[1]
    grad_pairs = jnp.stack((grad_keys.reshape(key_count, -1), grad_values.reshape(key_count, -1)))
    return (grad_queries.reshape(queries.shape), grad_pairs)


def layer_forward(hidden, params, allowed, reach_blocks, head_count):
    (
        w_query,
        b_query,
        w_key,
        w_value,
        b_value,
        w_out,
        b_out,
        gain_attn,
        shift_attn,
        w_in,
        b_in,
        w_back,
        b_back,
        gain_ffn,
        shift_ffn,
    ) = params
    entry = bfloat(hidden)
    queries = bfloat(product(entry, w_query) + widen(b_query))
    stacked = jnp.stack(
        (bfloat(product(entry, w_key)), bfloat(product(entry, w_value) + widen(b_value)))
    )
    pairs = near_blocks(stacked, reach_blocks)
    mixed, logsum = attend_forward(queries, pairs, allowed, head_count)
    mixed = bfloat(mixed)
    first, normed_one, factor_one = normalize(
        hidden + product(mixed, w_out) + widen(b_out), gain_attn, shift_attn
    )
    entry_two = bfloat(first)
    before = product(entry_two, w_in) + widen(b_in)
    active = bfloat(smooth(before))
    result, normed_two, factor_two = normalize(
        first + product(active, w_back) + widen(b_back), gain_ffn, shift_ffn
    )
    saved = (
        entry,
        queries,
        pairs,
        logsum,
        mixed,
        normed_one,
        factor_one,
        entry_two,
        before,
        active,
        normed_two,
        factor_two,
    )
    return (result, saved)


def layer_backward(grad_out, params, saved, allowed, reach_blocks, head_count):
    (
        w_query,
        b_query,
        w_key,
        w_value,
        b_value,
        w_out,
        b_out,
        gain_attn,
        shift_attn,
        w_in,
        b_in,
        w_back,
        b_back,
        gain_ffn,
        shift_ffn,
    ) = params
    (
        entry,
        queries,
        pairs,
        logsum,
        mixed,
        normed_one,
        factor_one,
        entry_two,
        before,
        active,
        normed_two,
        factor_two,
    ) = saved
    d_second, grad_gain_ffn, grad_shift_ffn = normalize_back(
        grad_out, normed_two, factor_two, gain_ffn
    )
    d_branch = bfloat(d_second)
    grad_b_back = jnp.sum(widen(d_branch), axis=0)
    grad_w_back = product_tn(active, d_branch)
    d_active = product_nt(d_branch, w_back)
    d_before = bfloat(jax.vjp(smooth, before)[1](d_active)[0])
    grad_b_in = jnp.sum(widen(d_before), axis=0)
    grad_w_in = product_tn(entry_two, d_before)
    d_first = d_second + product_nt(d_before, w_in)
    d_inner, grad_gain_attn, grad_shift_attn = normalize_back(
        d_first, normed_one, factor_one, gain_attn
    )
    d_attn = bfloat(d_inner)
    grad_b_out = jnp.sum(widen(d_attn), axis=0)
    grad_w_out = product_tn(mixed, d_attn)
    d_mixed = bfloat(product_nt(d_attn, w_out))
    d_queries, d_pairs = attend_back(queries, pairs, allowed, head_count, logsum, d_mixed)
    d_owned = return_blocks(d_pairs, reach_blocks)
    d_queries = bfloat(d_queries)
    d_keys = bfloat(d_owned[0])
    d_values = bfloat(d_owned[1])
    grad_w_query = product_tn(entry, d_queries)
    grad_b_query = jnp.sum(widen(d_queries), axis=0)
    grad_w_key = product_tn(entry, d_keys)
    grad_w_value = product_tn(entry, d_values)
    grad_b_value = jnp.sum(widen(d_values), axis=0)
    d_hidden = (
        d_inner
        + product_nt(d_queries, w_query)
        + product_nt(d_keys, w_key)
        + product_nt(d_values, w_value)
    )
    gradients = (
        grad_w_query,
        grad_b_query,
        grad_w_key,
        grad_w_value,
        grad_b_value,
        grad_w_out,
        grad_b_out,
        grad_gain_attn,
        grad_shift_attn,
        grad_w_in,
        grad_b_in,
        grad_w_back,
        grad_b_back,
        grad_gain_ffn,
        grad_shift_ffn,
    )
    return (d_hidden, gradients)


def spread_layer(gradients):
    return lax.psum_scatter(gradients, ("seq", "tok"), scatter_dimension=0, tiled=True)


def on_device(
    tokens,
    cotangent,
    doc_lengths,
    pad_counts,
    w_query,
    b_query,
    w_key,
    w_value,
    b_value,
    w_out,
    b_out,
    gain_attn,
    shift_attn,
    w_in,
    b_in,
    w_back,
    b_back,
    gain_ffn,
    shift_ffn,
):
    tok_rows = tokens.shape[0]
    seq_length = tok_rows * lax.axis_size("tok")
    reach_blocks = (WINDOW // 2 + tok_rows - 2) // tok_rows
    first_row = lax.axis_index("tok") * tok_rows
    doc_ends = jnp.cumsum(doc_lengths[0])
    live_rows = seq_length - pad_counts[0]
    query_places = first_row + jnp.arange(tok_rows, dtype=jnp.int32)
    key_places = (
        first_row
        - reach_blocks * tok_rows
        + jnp.arange((2 * reach_blocks + 1) * tok_rows, dtype=jnp.int32)
    )
    query_segment = segment_of(query_places, doc_ends, live_rows)
    key_segment = segment_of(key_places, doc_ends, live_rows)
    inside_range = (key_places >= 0) & (key_places < seq_length)
    allowed = (
        (query_segment[:, None] == key_segment[None, :])
        & (jnp.abs(query_places[:, None] - key_places[None, :]) < WINDOW // 2)
        & inside_range[None, :]
    )
    head_count = HEADS
    params = (
        lax.all_gather(w_query, ("seq", "tok"), axis=0, tiled=True),
        lax.all_gather(b_query, ("seq", "tok"), axis=0, tiled=True),
        lax.all_gather(w_key, ("seq", "tok"), axis=0, tiled=True),
        lax.all_gather(w_value, ("seq", "tok"), axis=0, tiled=True),
        lax.all_gather(b_value, ("seq", "tok"), axis=0, tiled=True),
        lax.all_gather(w_out, ("seq", "tok"), axis=0, tiled=True),
        lax.all_gather(b_out, ("seq", "tok"), axis=0, tiled=True),
        lax.all_gather(gain_attn, ("seq", "tok"), axis=0, tiled=True),
        lax.all_gather(shift_attn, ("seq", "tok"), axis=0, tiled=True),
        lax.all_gather(w_in, ("seq", "tok"), axis=0, tiled=True),
        lax.all_gather(b_in, ("seq", "tok"), axis=0, tiled=True),
        lax.all_gather(w_back, ("seq", "tok"), axis=0, tiled=True),
        lax.all_gather(b_back, ("seq", "tok"), axis=0, tiled=True),
        lax.all_gather(gain_ffn, ("seq", "tok"), axis=0, tiled=True),
        lax.all_gather(shift_ffn, ("seq", "tok"), axis=0, tiled=True),
    )
    middle, saved_one = layer_forward(widen(tokens), params, allowed, reach_blocks, head_count)
    result, saved_two = layer_forward(middle, params, allowed, reach_blocks, head_count)
    d_middle, grads_two = layer_backward(
        widen(cotangent), params, saved_two, allowed, reach_blocks, head_count
    )
    owned_two = spread_layer(grads_two)
    d_tokens, grads_one = layer_backward(
        d_middle, params, saved_one, allowed, reach_blocks, head_count
    )
    owned_one = spread_layer(grads_one)
    owned = jax.tree.map(jnp.add, owned_two, owned_one)
    return (bfloat(result), bfloat(d_tokens)) + tuple(owned)


def solution(mesh):
    placed = (
        P(("seq", "tok"), None),
        P(("seq", "tok"), None),
        P("seq", None),
        P("seq"),
        P(("seq", "tok"), None),
        P(("seq", "tok")),
        P(("seq", "tok"), None),
        P(("seq", "tok"), None),
        P(("seq", "tok")),
        P(("seq", "tok"), None),
        P(("seq", "tok")),
        P(("seq", "tok")),
        P(("seq", "tok")),
        P(("seq", "tok"), None),
        P(("seq", "tok")),
        P(("seq", "tok"), None),
        P(("seq", "tok")),
        P(("seq", "tok")),
        P(("seq", "tok")),
    )
    return jax.shard_map(
        on_device,
        mesh=mesh,
        in_specs=placed,
        out_specs=(
            P(("seq", "tok"), None),
            P(("seq", "tok"), None),
            P(("seq", "tok"), None),
            P(("seq", "tok")),
            P(("seq", "tok"), None),
            P(("seq", "tok"), None),
            P(("seq", "tok")),
            P(("seq", "tok"), None),
            P(("seq", "tok")),
            P(("seq", "tok")),
            P(("seq", "tok")),
            P(("seq", "tok"), None),
            P(("seq", "tok")),
            P(("seq", "tok"), None),
            P(("seq", "tok")),
            P(("seq", "tok")),
            P(("seq", "tok")),
        ),
        check_vma=False,
    )
```

profile of v0, /device:TPU:1, one launch (start us, length us, event | category | flops | bytes accessed | tf_op | source)
XLA Modules:
  0.0 5429.5 jit_solution(11291398825576916372)
XLA Ops:
  18.8 69.2 %all-reduce.19 = (bf16[1024]{0:T(1024)(128)(2,1)S(1)}, bf16[1024]{0:T(1024)(128)(2,1)S(1)}, bf16[1024]{0:T(1024)(128)(2,1)S(1)}, bf16[1024]{0:T(1024)(128)(2,1)S...) all-reduce(bf16[1024]{0:T(1024)(128)(2,1)S(1)} %dynamic-update-slic, ...), channel_id=1, replica_groups=mesh['seq'=8,'tok'=16] {'seq','tok'}, use_global_device_ids=true, to_apply=%add | all-reduce | flops 12288 | bytes 49152
  89.7 117.4 %all-gather.7.cloned.1.call-done = bf16[1024,1024]{1,0:T(8,128)(2,1)} async-done(((bf16[8,1024]{1,0:T(8,128)(2,1)}), bf16[1024,1024]{1,0:T(8,128)(2,1)}) %all-gather.7.cloned.1.call-update) | async-done | bytes 2097168 | tf_op jit(solution)/shard_map/all_gather | solution.py:356
  209.4 192.2 %all-gather.9.cloned.1.call-done = bf16[1024,1024]{1,0:T(8,128)(2,1)} async-done(((bf16[8,1024]{1,0:T(8,128)(2,1)}), bf16[1024,1024]{1,0:T(8,128)(2,1)}) %all-gather.9.cloned.1.call-update) | async-done | bytes 2097168 | tf_op jit(solution)/shard_map/all_gather | solution.py:357
  420.8 202.5 %all-gather.11.cloned.1.call-done = bf16[1024,1024]{1,0:T(8,128)(2,1)} async-done(((bf16[8,1024]{1,0:T(8,128)(2,1)}), bf16[1024,1024]{1,0:T(8,128)(2,1)}) %all-gather.11.cloned.1.call-update) | async-done | bytes 2097168 | tf_op jit(solution)/shard_map/all_gather | solution.py:354
  632.9 8.7 collective-permute-done.5
  650.0 11.1 fusion.110
  661.2 8.6 fusion
  669.8 8.7 fusion.51
  678.6 140.2 %all-gather.13.cloned.1.call-done = bf16[1024,1024]{1,0:T(8,128)(2,1)} async-done(((bf16[8,1024]{1,0:T(8,128)(2,1)}), bf16[1024,1024]{1,0:T(8,128)(2,1)}) %all-gather.13.cloned.1.call-update) | async-done | bytes 2097168 | tf_op jit(solution)/shard_map/all_gather | solution.py:359
  821.5 200.5 %all-gather.15.cloned.1.call-done = bf16[1024,4096]{1,0:T(8,128)(2,1)} async-done(((bf16[8,4096]{1,0:T(8,128)(2,1)}), bf16[1024,4096]{1,0:T(8,128)(2,1)}) %all-gather.15.cloned.1.call-update) | async-done | bytes 8388624 | tf_op jit(solution)/shard_map/all_gather | solution.py:363
  1022.0 6.9 convolution_add_fusion.3
  1028.9 196.3 %all-gather.17.cloned.1.call-done = bf16[4096,1024]{1,0:T(8,128)(2,1)} async-done(((bf16[32,1024]{1,0:T(8,128)(2,1)}), bf16[4096,1024]{1,0:T(8,128)(2,1)}) %all-gather.17.cloned.1.call-update) | async-done | bytes 8388624 | tf_op jit(solution)/shard_map/all_gather | solution.py:365
  1225.2 6.8 fusion.112
  1260.4 12.7 collective-permute-done.7
  1274.3 7.2 collective-permute-done.8
  1298.0 11.0 fusion.113
  1309.0 8.4 fusion.1
  1317.5 8.9 fusion.50
  1338.9 8.8 convert_reduce_fusion.1
  1355.2 11.7 fusion.8
  1366.8 11.3 multiply_reduce_fusion.1
  1378.1 6.2 copy.89
  1384.4 12.1 multiply_convert_fusion.1
  1415.0 7.0 collective-permute-start.17
  1422.0 14.7 collective-permute-start.16
  1436.7 7.5 collective-permute-start.15
  1462.0 10.2 collective-permute-done.15
  1472.2 18.8 collective-permute-done.13
  1498.2 8.4 convert_reduce_fusion
  1511.4 12.0 multiply_reduce_fusion
  1523.4 12.2 multiply_convert_fusion
  1550.9 11.5 fusion.6
  1562.4 6.2 copy.92
  1568.7 7.8 convolution_multiply_fusion
  1576.5 6.3 copy.91
  1582.8 7.6 fusion.4
  1605.4 11.0 collective-permute-done.23
  1620.8 17.9 collective-permute-done.22
  1638.6 9.1 collective-permute-done.21
  1664.2 9.8 convolution_add_fusion.1
  1678.7 10.4 convolution_add_fusion
  1695.3 71.3 %all-reduce.18 = (f32[1024]{0:T(1024)S(1)}, f32[1024]{0:T(1024)S(1)}, f32[1024]{0:T(1024)S(1)}, f32[1024]{0:T(1024)S(1)}, f32[1024]{0:T(1024)S(1)}, /*index=5*/f...) all-reduce(f32[1024]{0:T(1024)S(1)} %reshape.308, ...), channel_id=18, replica_groups=mesh['seq'=8,'tok'=16] {'seq','tok'}, use_global_device_ids=true, to_apply=%region_28.29.clone | all-reduce | flops 12288 | bytes 98304
  1776.0 405.2 %reduce-scatter.7.cloned.1.call-done = f32[8,1024]{1,0:T(8,128)} async-done(((f32[1024,1024]{1,0:T(8,128)}), f32[8,1024]{1,0:T(8,128)}) %reduce-scatter.7.cloned.1.call-update) | async-done | bytes 32784 | tf_op jit(solution)/shard_map/reduce_scatter | solution.py:308
  2181.2 639.3 %reduce-scatter.13.cloned.1.call-done = f32[8,1024]{1,0:T(8,128)} async-done(((f32[1024,1024]{1,0:T(8,128)}), f32[8,1024]{1,0:T(8,128)}) %reduce-scatter.13.cloned.1.call-update) | async-done | bytes 32784 | tf_op jit(solution)/shard_map/reduce_scatter | solution.py:308
  2820.5 639.2 %reduce-scatter.9.cloned.1.call-done = f32[8,1024]{1,0:T(8,128)} async-done(((f32[1024,1024]{1,0:T(8,128)}), f32[8,1024]{1,0:T(8,128)}) %reduce-scatter.9.cloned.1.call-update) | async-done | bytes 32784 | tf_op jit(solution)/shard_map/reduce_scatter | solution.py:308
  3459.7 639.1 %reduce-scatter.11.cloned.1.call-done = f32[8,1024]{1,0:T(8,128)} async-done(((f32[1024,1024]{1,0:T(8,128)}), f32[8,1024]{1,0:T(8,128)}) %reduce-scatter.11.cloned.1.call-update) | async-done | bytes 32784 | tf_op jit(solution)/shard_map/reduce_scatter | solution.py:308
  4098.9 661.7 %reduce-scatter.15.cloned.1.call-done = f32[8,4096]{1,0:T(8,128)} async-done(((f32[1024,4096]{1,0:T(8,128)}), f32[8,4096]{1,0:T(8,128)}) %reduce-scatter.15.cloned.1.call-update) | async-done | bytes 131088 | tf_op jit(solution)/shard_map/reduce_scatter | solution.py:308
  4760.5 661.6 %reduce-scatter.17.cloned.1.call-done = f32[32,1024]{1,0:T(8,128)} async-done(((f32[4096,1024]{1,0:T(8,128)}), f32[32,1024]{1,0:T(8,128)}) %reduce-scatter.17.cloned.1.call-update) | async-done | bytes 131088 | tf_op jit(solution)/shard_map/reduce_scatter | solution.py:308
  (396 shorter events, 239.1 us)
Async XLA Ops:
  7.2 394.4 %copy-start.19 = (bf16[192,1024]{1,0:T(8,128)(2,1)S(1)}, bf16[192,1024]{1,0:T(8,128)(2,1)}, u32[]{:S(2)}) copy-start(bf16[192,1024]{1,0:T(8,128)(2,1)} %param.19) | copy-start | bytes 1179652
  7.2 199.9 %all-gather.7.cloned.1.call-start = ((), (), s32[]{:S(2)}) async-start(), calls=%async_computation.6 | async-start | bytes 2113536 | tf_op jit(solution)/shard_map/all_gather | solution.py:356
  7.9 393.7 %all-gather.9.cloned.1.call-start = ((), (), s32[]{:S(2)}) async-start(), calls=%async_computation.7 | async-start | bytes 2113536 | tf_op jit(solution)/shard_map/all_gather | solution.py:357
  8.7 614.6 %all-gather.11.cloned.1.call-start = ((), (), s32[]{:S(2)}) async-start(), calls=%async_computation.8 | async-start | bytes 2113536 | tf_op jit(solution)/shard_map/all_gather | solution.py:354
  9.4 809.3 %all-gather.13.cloned.1.call-start = ((), (), s32[]{:S(2)}) async-start(), calls=%async_computation.9 | async-start | bytes 2113536 | tf_op jit(solution)/shard_map/all_gather | solution.py:359
  10.0 1012.0 %all-gather.15.cloned.1.call-start = ((), (), s32[]{:S(2)}) async-start(), calls=%async_computation.10 | async-start | bytes 8454144 | tf_op jit(solution)/shard_map/all_gather | solution.py:363
  10.6 1214.6 %all-gather.17.cloned.1.call-start = ((), (), s32[]{:S(2)}) async-start(), calls=%async_computation.11 | async-start | bytes 8454144 | tf_op jit(solution)/shard_map/all_gather | solution.py:365
  11.2 2170.1 %reduce-scatter.7.cloned.1.call-start = ((), (), s32[]{:S(2)}) async-start(), calls=%async_computation.12 | async-start | bytes 4227072 | tf_op jit(solution)/shard_map/reduce_scatter | solution.py:308
  88.0 315.9 %copy-start.73 = (f32[1024]{0:T(1024)}, f32[1024]{0:T(1024)S(1)}, u32[]{:S(2)}) copy-start(f32[1024]{0:T(1024)S(1)} %convert_element_type.274) | copy-start | bytes 12292
  403.9 222.6 %collective-permute-start = (bf16[2,192,1024]{2,1,0:T(8,128)(2,1)S(1)}, bf16[2,192,1024]{2,1,0:T(8,128)(2,1)}, u32[]{:S(2)}, u32[]{:S(2)}) collective-permute-start(bf16[2,192,1024]{2,1,0:T(8,128)(2,1)S(1)} %pad_maximum_fusion.2), channel_id=1, source_target_pairs={{0,3},{1,4},{2,5},{3,6},{4,7},{5,8},{6,9},{7,10},{8,11},{9,12},{10... | collective-permute-start | bytes 2359304 | tf_op jit(solution)/shard_map/ppermute | solution.py:19
  409.5 219.7 %collective-permute-start.1 = (bf16[2,192,1024]{2,1,0:T(8,128)(2,1)S(1)}, bf16[2,192,1024]{2,1,0:T(8,128)(2,1)}, u32[]{:S(2)}, u32[]{:S(2)}) collective-permute-start(bf16[2,192,1024]{2,1,0:T(8,128)(2,1)S(1)} %pad_maximum_fusion.2), channel_id=1, source_target_pairs={{0,2},{1,3},{2,4},{3,5},{4,6},{5,7},{6,8},{7,9},{8,10},{9,11},{10,... | collective-permute-start | bytes 2359304 | tf_op jit(solution)/shard_map/ppermute | solution.py:19
  411.6 218.8 %collective-permute-start.2 = (bf16[2,192,1024]{2,1,0:T(8,128)(2,1)S(1)}, bf16[2,192,1024]{2,1,0:T(8,128)(2,1)S(1)}, u32[]{:S(2)}, u32[]{:S(2)}) collective-permute-start(bf16[2,192,1024]{2,1,0:T(8,128)(2,1)S(1)} %pad_maximum_fusion.2), channel_id=1, source_target_pairs={{0,1},{1,2},{2,3},{3,4},{4,5},{5,6},{6,7},{7,8},{8,9},{9,10},{10,1... | collective-permute-start | bytes 2359304 | tf_op jit(solution)/shard_map/ppermute | solution.py:19
  414.0 236.0 %copy-start.44 = (pred[192,1344]{1,0:T(8,128)(4,1)}, pred[192,1344]{1,0:T(8,128)(4,1)S(1)}, u32[]{:S(2)}) copy-start(pred[192,1344]{1,0:T(8,128)(4,1)S(1)} %fusion.67) | copy-start | bytes 774148
  415.9 214.5 %copy-start.75 = (f32[1024]{0:T(1024)}, f32[1024]{0:T(1024)S(1)}, u32[]{:S(2)}) copy-start(f32[1024]{0:T(1024)S(1)} %convert_element_type.278) | copy-start | bytes 12292
  415.9 917.6 %copy-start.53 = (f32[1024]{0:T(1024)}, f32[1024]{0:T(1024)S(1)}, u32[]{:S(2)}) copy-start(f32[1024]{0:T(1024)S(1)} %convert_element_type.286) | copy-start | bytes 12292
  417.1 213.5 %collective-permute-start.3 = (bf16[2,192,1024]{2,1,0:T(8,128)(2,1)S(1)}, bf16[2,192,1024]{2,1,0:T(8,128)(2,1)}, u32[]{:S(2)}, u32[]{:S(2)}) collective-permute-start(bf16[2,192,1024]{2,1,0:T(8,128)(2,1)S(1)} %pad_maximum_fusion.2), channel_id=1, source_target_pairs={{1,0},{2,1},{3,2},{4,3},{5,4},{6,5},{7,6},{8,7},{9,8},{10,9},{11,1... | collective-permute-start | bytes 2359304 | tf_op jit(solution)/shard_map/ppermute | solution.py:19
  419.5 212.2 %collective-permute-start.4 = (bf16[2,192,1024]{2,1,0:T(8,128)(2,1)S(1)}, bf16[2,192,1024]{2,1,0:T(8,128)(2,1)}, u32[]{:S(2)}, u32[]{:S(2)}) collective-permute-start(bf16[2,192,1024]{2,1,0:T(8,128)(2,1)S(1)} %pad_maximum_fusion.2), channel_id=1, source_target_pairs={{2,0},{3,1},{4,2},{5,3},{6,4},{7,5},{8,6},{9,7},{10,8},{11,9},{12,... | collective-permute-start | bytes 2359304 | tf_op jit(solution)/shard_map/ppermute | solution.py:19
  626.5 15.2 collective-permute-start.5
  669.8 148.9 %copy-start.58 = (f32[1024]{0:T(1024)S(1)}, f32[1024]{0:T(1024)}, u32[]{:S(2)}) copy-start(f32[1024]{0:T(1024)} %convert_element_type.284) | copy-start | bytes 12292
  678.5 343.4 %copy-start.69 = (f32[4096]{0:T(1024)S(1)}, f32[4096]{0:T(1024)}, u32[]{:S(2)}) copy-start(f32[4096]{0:T(1024)} %convert_element_type.288) | copy-start | bytes 49156
  821.2 404.0 %copy-start.9 = (f32[192,1024]{1,0:T(8,128)}, f32[192,1024]{1,0:T(8,128)S(1)}, u32[]{:S(2)}) copy-start(f32[192,1024]{1,0:T(8,128)S(1)} %get-tuple-element.79) | copy-start | bytes 2359300
  821.5 403.8 %copy-start.72 = (f32[1024]{0:T(1024)S(1)}, f32[1024]{0:T(1024)}, u32[]{:S(2)}) copy-start(f32[1024]{0:T(1024)} %convert_element_type.290) | copy-start | bytes 12292
  1028.9 203.4 %copy-start.55 = (f32[1024]{0:T(1024)S(1)}, f32[1024]{0:T(1024)}, u32[]{:S(2)}) copy-start(f32[1024]{0:T(1024)} %convert_element_type.291) | copy-start | bytes 12292
  1028.9 203.4 %copy-start.57 = (f32[1024]{0:T(1024)S(1)}, f32[1024]{0:T(1024)}, u32[]{:S(2)}) copy-start(f32[1024]{0:T(1024)} %convert_element_type.292) | copy-start | bytes 12292
  1028.9 203.6 %copy-start.74 = (f32[1024]{0:T(1024)S(1)}, f32[1024]{0:T(1024)}, u32[]{:S(2)}) copy-start(f32[1024]{0:T(1024)} %copy-done.73) | copy-start | bytes 12292
  1235.5 22.4 collective-permute-start.6
  1241.1 32.1 collective-permute-start.7
  1243.3 38.3 collective-permute-start.8
  1245.2 37.6 collective-permute-start.9
  1248.5 35.5 collective-permute-start.10
  1257.9 27.3 collective-permute-start.11
  1415.0 31.8 collective-permute-start.17
  1422.0 40.1 collective-permute-start.16
  1436.7 35.5 collective-permute-start.15
  1444.2 28.0 collective-permute-start.14
  1445.5 45.5 collective-permute-start.13
  1446.8 45.0 collective-permute-start.12
  1544.9 1275.6 %reduce-scatter.13.cloned.1.call-start = ((), (), s32[]{:S(2)}) async-start(), calls=%async_computation.15 | async-start | bytes 4227072 | tf_op jit(solution)/shard_map/reduce_scatter | solution.py:308
  1550.6 1909.1 %reduce-scatter.9.cloned.1.call-start = ((), (), s32[]{:S(2)}) async-start(), calls=%async_computation.13 | async-start | bytes 4227072 | tf_op jit(solution)/shard_map/reduce_scatter | solution.py:308
  1593.5 22.9 collective-permute-start.23
  1595.0 43.6 collective-permute-start.22
  1596.6 51.1 collective-permute-start.21
  1602.8 45.0 collective-permute-start.20
  1604.1 43.8 collective-permute-start.19
  1616.4 33.2 collective-permute-start.18
  1654.6 2444.3 %reduce-scatter.11.cloned.1.call-start = ((), (), s32[]{:S(2)}) async-start(), calls=%async_computation.14 | async-start | bytes 4227072 | tf_op jit(solution)/shard_map/reduce_scatter | solution.py:308
  1659.2 3101.3 %reduce-scatter.15.cloned.1.call-start = ((), (), s32[]{:S(2)}) async-start(), calls=%async_computation.16 | async-start | bytes 16908288 | tf_op jit(solution)/shard_map/reduce_scatter | solution.py:308
  1674.0 3748.1 %reduce-scatter.17.cloned.1.call-start = ((), (), s32[]{:S(2)}) async-start(), calls=%async_computation.17 | async-start | bytes 16908288 | tf_op jit(solution)/shard_map/reduce_scatter | solution.py:308
  (78 other events, 1118.9 us)
Sparse Core Ops, SparseCore 0:
  9.8 197.2 all-gather.6
  208.8 192.7 all-gather.8
  403.3 219.9 all-gather.10
  624.9 193.7 all-gather.12
  820.3 201.6 all-gather.14
  1023.6 201.5 all-gather.16
  1545.0 636.1 reduce-scatter.6
  2184.3 636.2 reduce-scatter.12
  2823.5 636.1 reduce-scatter.8
  3462.6 636.2 reduce-scatter.10
  4101.8 658.6 reduce-scatter.14
  4763.3 658.7 reduce-scatter.16
where the time goes:
time: 5440 us; the launch traced here: 5430 us
  waiting for transfers between devices  4800 us (88%)
  matrix products  229 us (4%)
  blocking collectives  140 us (3%)
  local copies, waits for them, and re-layouts  86.5 us (2%)
  starting transfers between devices  82.7 us (2%)
  other arithmetic  71.5 us (1%)
    reduce_scatter x6, waiting for transfers between devices, spread_layer(): lax.psum_scatter(gradients, ('seq', 'tok'), scatter_dimension=0, tiled=True)  3650 us
    all_gather x1, waiting for transfers between devices, on_device(): lax.all_gather(w_query, ('seq', 'tok'), axis=0, tiled=True)  202 us
    all_gather x1, waiting for transfers between devices, on_device(): lax.all_gather(w_in, ('seq', 'tok'), axis=0, tiled=True)  201 us
    all_gather x1, waiting for transfers between devices, on_device(): lax.all_gather(w_back, ('seq', 'tok'), axis=0, tiled=True)  196 us
    all_gather x1, waiting for transfers between devices, on_device(): lax.all_gather(w_value, ('seq', 'tok'), axis=0, tiled=True)  192 us
    unnamed x2, blocking collectives  140 us
    all_gather x1, waiting for transfers between devices, on_device(): lax.all_gather(w_out, ('seq', 'tok'), axis=0, tiled=True)  140 us
    all_gather x1, waiting for transfers between devices, on_device(): lax.all_gather(w_key, ('seq', 'tok'), axis=0, tiled=True)  117 us
  transfers between devices with their start and end apart: 36, of which 24 were waited for; matrix products, arithmetic and copies ran while one was open for 4% of the time, Pallas kernels for 0%

commit v1 on v0

v1 whole, which is shorter than its diff:
```python
import functools
import math

import jax
import jax.numpy as jnp
from jax import lax
from jax.experimental import pallas as pl
from jax.experimental.pallas import tpu as pltpu
from jax.sharding import PartitionSpec as P

HEADS = 16
WINDOW = 1024
D = 1024
FF = 4096
HEAD = 64
CHIPS = 8
ROWS = 192
CHIP_ROWS = 2 * ROWS
LENGTH = CHIP_ROWS * CHIPS
HALF = 512
EPSILON = 1e-05
MASKED = -1e30
SCALE = 1.0 / math.sqrt(HEAD)
LOG2E = 1.4426950408889634
MESH = pl.DeviceIdType.MESH
BF = jnp.bfloat16
F32 = jnp.float32
CUBE = (4, 2, 2, 4)


def bfloat(tensor):
    return tensor.astype(BF)


def widen(tensor):
    return tensor.astype(F32)


def place():
    seq, tok = lax.axis_index("seq"), lax.axis_index("tok")
    x = (tok // 8) * 2 + seq % 2
    return {"x": x, "y": seq // 2, "z": (tok // 2) % 4, "core": tok % 2}


def device(x, y, z, core):
    return (y * 2 + x % 2, (x // 2) * 8 + z * 2 + core)


def moved(here, axis, steps):
    there = dict(here)
    there[axis] = lax.rem(here[axis] + steps + 4, 4)
    return device(**there)


def partner(here):
    return device(here["x"], here["y"], here["z"], 1 - here["core"])


def cube_index(here, whole, axis, value):
    index = []
    for name in ("y", "x", "z"):
        if name in whole:
            index += [slice(None)] * (2 if name == "x" else 1)
        else:
            at = value if name == axis else here[name]
            index += [at % 2, at // 2] if name == "x" else [at]
    return tuple(index)


def greet(targets):
    barrier = pltpu.get_barrier_semaphore()
    for target in targets:
        pl.semaphore_signal(barrier, inc=1, device_id=target, device_id_type=MESH)
    pl.semaphore_wait(barrier, len(targets))


def neighbours(here):
    return [moved(here, axis, step) for axis in ("x", "y", "z") for step in (1, -1)] + [
        partner(here)
    ]


def remote(source, target, sems, number, to):
    return pltpu.make_async_remote_copy(
        src_ref=source,
        dst_ref=target,
        send_sem=sems[0].at[number],
        recv_sem=sems[1].at[number],
        device_id=to,
        device_id_type=MESH,
    )


GATHER_ORDERS = (("x", "y", "z"), ("z", "x", "y"), ("y", "z", "x"), ("x", "y", "z"))


def gather_kernel(
    pack, small, ga, gb, gc, gs, wo, wb, theirs, small_theirs, stage, small_stage, send, recv, local
):
    here = place()
    core = here["core"]
    other = partner(here)
    sems = (send, recv)
    greet(neighbours(here))
    first = remote(pack.at[1 - core], theirs, sems, 0, other)
    second = remote(small, small_theirs, sems, 1, other)
    first.start()
    second.start()
    first.wait()
    second.wait()

    def build(low, high):
        low, high = widen(low), widen(high)
        for piece in range(8):
            rows = slice(8 * piece, 8 * piece + 8)
            both = bfloat(jnp.concatenate([low[rows], high[rows]], axis=0))
            stage[piece // 4, (piece % 4) * 16 : (piece % 4) * 16 + 16, :] = both
        stage[2, 0:32, :] = bfloat(low[64:96])
        stage[2, 32:64, :] = bfloat(high[64:96])

    @pl.when(core == 0)
    def _():
        build(pack[0], theirs[...])

    @pl.when(core == 1)
    def _():
        build(theirs[...], pack[1])

    small_stage[...] = small[...] + small_theirs[...]
    whole = (ga, gb, gc, gs)
    own = cube_index(here, (), None, None)
    kept = []
    for part in range(4):
        source = small_stage if part == 3 else stage.at[part]
        copy = pltpu.make_async_copy(source, whole[part].at[own], local.at[part])
        copy.start()
        kept.append(copy)

    number = 2
    sent = []
    for phase in range(3):
        one, two = [], []
        for part in range(4):
            axis = GATHER_ORDERS[part][phase]
            done = GATHER_ORDERS[part][:phase]
            index = cube_index(here, done, axis, here[axis])
            if phase == 0:
                source = small_stage if part == 3 else stage.at[part]
            else:
                source = whole[part].at[index]
            pair = []
            for step in (1, -1):
                copy = remote(source, whole[part].at[index], sems, number, moved(here, axis, step))
                number += 1
                copy.start()
                pair.append(copy)
            one.append(pair)
            sent += pair
        for part in range(4):
            axis = GATHER_ORDERS[part][phase]
            done = GATHER_ORDERS[part][:phase]
            for side, step in enumerate((1, -1)):
                one[part][side].wait_recv()
                if part == 3 and side == 1:
                    continue
                come = lax.rem(here[axis] - step + 4, 4)
                index = cube_index(here, done, axis, come)
                block = whole[part].at[index]
                if part < 3:
                    rows = pl.ds(32 * side, 32)
                    block = whole[part].at[index + (rows,)]
                copy = remote(block, block, sems, number, moved(here, axis, step))
                number += 1
                copy.start()
                two.append(copy)
        for copy in two:
            copy.wait_recv()
        sent += two
        if phase == 0:
            for copy in kept:
                copy.wait()

    mine, yours = pl.ds(2 * core, 2), pl.ds(2 * (1 - core), 2)
    out_rows = pl.ds(48, 16)
    every = slice(None)
    last = [
        remote(gc.at[yours], wb.at[core], sems, number, other),
        remote(ga.at[yours, every, every, every, out_rows], wo.at[core], sems, number + 1, other),
    ]
    for copy in last:
        copy.start()
    kept = [
        pltpu.make_async_copy(gc.at[mine], wb.at[core], local.at[4]),
        pltpu.make_async_copy(
            ga.at[mine, every, every, every, out_rows], wo.at[core], local.at[5]
        ),
    ]
    for copy in kept:
        copy.start()
    for copy in kept + last:
        copy.wait()
    for copy in sent:
        copy.wait_send()


GATHER_COPIES = 2 + 3 * (8 + 7) + 2


def gather_weights(pack, small):
    any_space = pl.BlockSpec(memory_space=pl.ANY)
    vmem = pl.BlockSpec(memory_space=pltpu.VMEM)
    big = jax.ShapeDtypeStruct(CUBE + (64, HALF), BF)
    return pl.pallas_call(
        gather_kernel,
        out_shape=(
            big,
            big,
            big,
            jax.ShapeDtypeStruct(CUBE + (16, 128), BF),
            jax.ShapeDtypeStruct((2, 2, 2, 2, 4, 16, HALF), BF),
            jax.ShapeDtypeStruct((2, 2, 2, 2, 4, 64, HALF), BF),
        ),
        in_specs=[vmem, vmem],
        out_specs=(any_space,) * 6,
        scratch_shapes=[
            pltpu.VMEM((96, HALF), BF),
            pltpu.VMEM((16, 128), BF),
            pltpu.VMEM((3, 64, HALF), BF),
            pltpu.VMEM((16, 128), BF),
            pltpu.SemaphoreType.DMA((GATHER_COPIES,)),
            pltpu.SemaphoreType.DMA((GATHER_COPIES,)),
            pltpu.SemaphoreType.DMA((6,)),
        ],
        name="gather_weights",
        compiler_params=pltpu.CompilerParams(collective_id=0, has_side_effects=True),
    )(pack, small)


SCATTER_ORDERS = (("z", "y", "x"), ("y", "x", "z"), ("x", "z", "y"), ("z", "y", "x"))
SIZES = {"y": (4,), "x": (2, 2), "z": (4,)}


def lengths_of(full):
    return tuple(n for name in ("y", "x", "z") if name in full for n in SIZES[name])


def digits_of(i, lengths):
    digits = []
    for length in reversed(lengths):
        digits.append(lax.rem(i, length))
        i = lax.div(i, length)
    return tuple(digits[::-1])


def one_chip(here, full, axis, value, digits):
    digits, index = list(digits), []
    for name in ("y", "x", "z"):
        if name in full:
            index += [digits.pop(0) for _ in SIZES[name]]
        else:
            at = value if name == axis else here[name]
            index += [at % 2, at // 2] if name == "x" else [at]
    return tuple(index)


def scatter_kernel(
    da, do, db, dc, ds,
    o_query, o_key, o_value, o_out, o_in, o_back, o_small,
    *scratch,
):
    whole, slots = scratch[:4], scratch[4:28]
    final, landed, small_out, send, recv, local = scratch[28:]
    wa, wb, wc, ws = whole
    here = place()
    core = here["core"]
    other = partner(here)
    sems = (send, recv)
    every = slice(None)
    mine = pl.ds(2 * core, 2)
    out_rows = pl.ds(48, 16)
    kept = [
        pltpu.make_async_copy(da, wa.at[every, every, every, every, pl.ds(0, 48)], local.at[0]),
        pltpu.make_async_copy(db, wb, local.at[1]),
        pltpu.make_async_copy(dc.at[core], wc.at[mine], local.at[2]),
        pltpu.make_async_copy(do.at[core], wa.at[mine, every, every, every, out_rows], local.at[3]),
        pltpu.make_async_copy(ds, ws, local.at[4]),
    ]
    for copy in kept:
        copy.start()
    greet(neighbours(here))
    swaps = [
        remote(do.at[1 - core], wa.at[mine, every, every, every, out_rows], sems, 0, other),
        remote(dc.at[1 - core], wc.at[mine], sems, 1, other),
    ]
    for copy in swaps:
        copy.start()
    for copy in kept:
        copy.wait()
    for copy in swaps:
        copy.wait()

    number = 2
    sent = []
    for phase in range(3):
        ahead, arriving = {}, {}
        for part in range(4):
            axis, full = SCATTER_ORDERS[part][phase], SCATTER_ORDERS[part][phase + 1 :]
            far = cube_index(here, full, axis, lax.rem(here[axis] + 2, 4))
            for side, step in enumerate((1, -1)):
                if part == 3 and side == 1:
                    continue
                rows = () if part == 3 else (pl.ds(32 * side, 32),)
                copy = ahead[part, side] = remote(
                    whole[part].at[far + rows],
                    slots[part * 6 + phase * 2].at[side],
                    sems,
                    number,
                    moved(here, axis, step),
                )
                number += 1
                copy.start()
                sent.append(copy)
        for part in range(4):
            axis, full = SCATTER_ORDERS[part][phase], SCATTER_ORDERS[part][phase + 1 :]
            lengths = lengths_of(full)
            half, whole_slot = slots[part * 6 + phase * 2 : part * 6 + phase * 2 + 2]
            for side, step in enumerate((1, -1)):
                value = lax.rem(here[axis] + step + 4, 4)
                if not (part == 3 and side == 1):
                    ahead[part, side].wait_recv()
                    rows = (every,) if part == 3 else (pl.ds(32 * side, 32),)

                    def add(i, _, part=part, side=side, half=half, value=value, rows=rows):
                        digits = digits_of(i, lengths_of(SCATTER_ORDERS[part][phase + 1 :]))
                        at = one_chip(
                            here,
                            SCATTER_ORDERS[part][phase + 1 :],
                            SCATTER_ORDERS[part][phase],
                            value,
                            digits,
                        )
                        ref = whole[part]
                        ref[at + rows] = bfloat(
                            widen(ref[at + rows]) + widen(half[(side,) + digits])
                        )
                        return 0

                    lax.fori_loop(0, math.prod(lengths), add, 0)
                copy = arriving[part, side] = remote(
                    whole[part].at[cube_index(here, full, axis, value)],
                    whole_slot.at[side],
                    sems,
                    number,
                    moved(here, axis, step),
                )
                number += 1
                copy.start()
                sent.append(copy)
        for part in range(4):
            axis, full = SCATTER_ORDERS[part][phase], SCATTER_ORDERS[part][phase + 1 :]
            lengths = lengths_of(full)
            whole_slot = slots[part * 6 + phase * 2 + 1]
            arriving[part, 0].wait_recv()
            arriving[part, 1].wait_recv()

            def total(i, _, part=part, whole_slot=whole_slot, axis=axis, full=full):
                digits = digits_of(i, lengths_of(full))
                at = one_chip(here, full, axis, here[axis], digits)
                ref = whole[part]
                value = (
                    widen(ref[at])
                    + widen(whole_slot[(0,) + digits])
                    + widen(whole_slot[(1,) + digits])
                )
                if phase < 2:
                    ref[at] = bfloat(value)
                elif part == 3:
                    small_out[...] = value
                else:
                    final[part] = value
                return 0

            lax.fori_loop(0, math.prod(lengths), total, 0)

    o_small[...] = small_out[...]

    def finish(own):
        rows = []
        for piece in range(8):
            part, low = piece // 4, (piece % 4) * 16 + 8 * own
            rows.append(final[part, low : low + 8, :])
        rows.append(final[2, 32 * own : 32 * own + 32, :])
        return jnp.concatenate(rows, axis=0)

    @pl.when(core == 0)
    def _():
        landed[2] = finish(1)
        landed[0] = finish(0)

    @pl.when(core == 1)
    def _():
        landed[2] = finish(0)
        landed[1] = finish(1)

    last = remote(landed.at[2], landed.at[core], sems, number, other)
    last.start()
    last.wait()
    for column in (0, 1):
        span = slice(column * HALF, column * HALF + HALF)
        for piece, ref in enumerate((o_query, o_key, o_value, o_out)):
            ref[:, span] = landed[column, 8 * piece : 8 * piece + 8, :]
        for chunk in range(4):
            low = column * 2048 + chunk * HALF
            o_in[:, low : low + HALF] = landed[column, 32 + 8 * chunk : 40 + 8 * chunk, :]
        o_back[:, span] = landed[column, 64:96, :]
    for copy in sent:
        copy.wait_send()


SCATTER_COPIES = 2 + 3 * (7 + 8) + 1


def scatter_gradients(da, do, db, dc, ds):
    any_space = pl.BlockSpec(memory_space=pl.ANY)
    vmem = pl.BlockSpec(memory_space=pltpu.VMEM)
    slots = []
    for part in range(4):
        for phase in range(3):
            dims = lengths_of(SCATTER_ORDERS[part][phase + 1 :])
            ends = ((16, 128), (16, 128)) if part == 3 else ((32, HALF), (64, HALF))
            slots += [pltpu.VMEM((2,) + dims + end, BF) for end in ends]
    return pl.pallas_call(
        scatter_kernel,
        out_shape=(
            jax.ShapeDtypeStruct((8, D), F32),
            jax.ShapeDtypeStruct((8, D), F32),
            jax.ShapeDtypeStruct((8, D), F32),
            jax.ShapeDtypeStruct((8, D), F32),
            jax.ShapeDtypeStruct((8, FF), F32),
            jax.ShapeDtypeStruct((32, D), F32),
            jax.ShapeDtypeStruct((16, 128), F32),
        ),
        in_specs=[any_space] * 5,
        out_specs=(vmem,) * 7,
        scratch_shapes=[
            pltpu.VMEM(CUBE + (64, HALF), BF),
            pltpu.VMEM(CUBE + (64, HALF), BF),
            pltpu.VMEM(CUBE + (64, HALF), BF),
            pltpu.VMEM(CUBE + (16, 128), BF),
        ]
        + slots
        + [
            pltpu.VMEM((3, 64, HALF), F32),
            pltpu.VMEM((3, 96, HALF), F32),
            pltpu.VMEM((16, 128), F32),
            pltpu.SemaphoreType.DMA((SCATTER_COPIES,)),
            pltpu.SemaphoreType.DMA((SCATTER_COPIES,)),
            pltpu.SemaphoreType.DMA((5,)),
        ],
        name="scatter_gradients",
        compiler_params=pltpu.CompilerParams(
            collective_id=1, has_side_effects=True, vmem_limit_bytes=60 * 2**20
        ),
    )(da, do, db, dc, ds)


def group_device(here, number):
    seq = lax.axis_index("seq")
    return (seq, (number // 4) * 8 + (number % 4) * 2 + here["core"])


def exchange_kernel(outward, value, result, send, recv, local):
    here = place()
    me = (here["x"] // 2) * 4 + here["z"]
    targets = [group_device(here, lax.rem(me + k, CHIPS)) for k in range(1, CHIPS)]
    greet(targets)

    def spot(ref, number, grouped):
        if grouped:
            return ref.at[:, number]
        start = pl.multiple_of(number * CHIP_ROWS, CHIP_ROWS)
        return ref.at[:, :, pl.ds(start, CHIP_ROWS)]

    copies = []
    for k in range(1, CHIPS):
        to = lax.rem(me + k, CHIPS)
        copies.append(
            remote(
                spot(value, to, outward),
                spot(result, me, not outward),
                (send, recv),
                k - 1,
                group_device(here, to),
            )
        )
    for copy in copies:
        copy.start()
    own = pltpu.make_async_copy(
        spot(value, me, outward), spot(result, me, not outward), local.at[0]
    )
    own.start()
    own.wait()
    for copy in copies:
        copy.wait()


def exchange(value, outward, number):
    count = value.shape[0]
    grouped, flat = (count, CHIPS, HEAD, CHIP_ROWS), (count, HEAD, LENGTH)
    vmem = pl.BlockSpec(memory_space=pltpu.VMEM)
    return pl.pallas_call(
        functools.partial(exchange_kernel, outward),
        out_shape=jax.ShapeDtypeStruct(flat if outward else grouped, BF),
        in_specs=[vmem],
        out_specs=vmem,
        scratch_shapes=[
            pltpu.SemaphoreType.DMA((CHIPS - 1,)),
            pltpu.SemaphoreType.DMA((CHIPS - 1,)),
            pltpu.SemaphoreType.DMA((1,)),
        ],
        name="exchange_%d" % number,
        compiler_params=pltpu.CompilerParams(
            collective_id=number, has_side_effects=True, vmem_limit_bytes=40 * 2**20
        ),
    )(value)


BLOCK = 256
SPAN = 1280
STEPS = LENGTH // BLOCK


def limits(bounds, first, count):
    places = first + lax.broadcasted_iota(jnp.int32, (1, count), 1)
    low = jnp.maximum(places - (WINDOW // 2 - 1), 0)
    high = jnp.minimum(places + WINDOW // 2, LENGTH)
    for k in range(4):
        bound = bounds[k]
        low = jnp.maximum(low, jnp.where(bound <= places, bound, 0))
        high = jnp.minimum(high, jnp.where(bound > places, bound, LENGTH))
    return low, high


def dot(former, latter):
    return jnp.dot(former, latter, preferred_element_type=F32)


def block_scores(bounds, qkv, kv, i):
    first = pl.multiple_of(i * BLOCK, BLOCK)
    start = pl.multiple_of(jnp.clip(first - 512, 0, LENGTH - SPAN), BLOCK)
    queries = qkv[0, :, pl.ds(first, BLOCK)]
    padded = jnp.concatenate([queries, jnp.zeros_like(queries)], axis=0)
    keys = kv[pl.ds(start, SPAN), :]
    scores = dot(keys, padded)
    low, high = limits(bounds, first, BLOCK)
    places = start + lax.broadcasted_iota(jnp.int32, (SPAN, BLOCK), 0)
    allowed = (places >= low) & (places < high)
    return first, start, queries, keys, jnp.where(allowed, scores, MASKED)


def attend_kernel(bounds, qkv, mixed, logsum, kv, kv_t):
    kv_t[...] = jnp.concatenate([qkv[1], qkv[2]], axis=0)
    kv[...] = kv_t[...].T

    def step(i, _):
        first, start, _, _, scores = block_scores(bounds, qkv, kv, i)
        highest = jnp.max(scores, axis=0, keepdims=True)
        chances = jnp.exp2((scores - highest) * (SCALE * LOG2E))
        totals = jnp.sum(chances, axis=0, keepdims=True)
        out = dot(kv_t[:, pl.ds(start, SPAN)], bfloat(chances))
        mixed[:, pl.ds(first, BLOCK)] = bfloat(out[HEAD:] / totals)
        logsum[:, pl.ds(first, BLOCK)] = highest * (SCALE * LOG2E) + jnp.log2(totals)
        return 0

    lax.fori_loop(0, STEPS, step, 0)


def attend(bounds, qkv):
    vmem = pl.BlockSpec(memory_space=pltpu.VMEM)
    return pl.pallas_call(
        attend_kernel,
        out_shape=(
            jax.ShapeDtypeStruct((HEAD, LENGTH), BF),
            jax.ShapeDtypeStruct((1, LENGTH), F32),
        ),
        in_specs=[pl.BlockSpec(memory_space=pltpu.SMEM), vmem],
        out_specs=(vmem, vmem),
        scratch_shapes=[
            pltpu.VMEM((LENGTH, 2 * HEAD), BF),
            pltpu.VMEM((2 * HEAD, LENGTH), BF),
        ],
        name="attend",
        compiler_params=pltpu.CompilerParams(vmem_limit_bytes=50 * 2**20),
    )(bounds, qkv)


def attend_back_kernel(bounds, qkv, logsum, grad_mixed, grads, kv, kv_t, total):
    kv_t[...] = jnp.concatenate([qkv[1], qkv[2]], axis=0)
    kv[...] = kv_t[...].T
    total[...] = jnp.zeros_like(total)
    left = lax.broadcasted_iota(jnp.int32, (BLOCK, 2 * HEAD), 1) < HEAD

    def step(i, _):
        first, start, queries, keys, scores = block_scores(bounds, qkv, kv, i)
        grad = grad_mixed[:, pl.ds(first, BLOCK)]
        chances = jnp.exp2(scores * (SCALE * LOG2E) - logsum[:, pl.ds(first, BLOCK)])
        grad_weights = dot(keys, jnp.concatenate([jnp.zeros_like(grad), grad], axis=0))
        inner = jnp.sum(chances * grad_weights, axis=0, keepdims=True)
        grad_scores = bfloat(chances * (grad_weights - inner))
        weights = bfloat(chances)
        grad_queries = dot(kv_t[:, pl.ds(start, SPAN)], grad_scores)
        grads[0, :, pl.ds(first, BLOCK)] = bfloat(grad_queries[:HEAD] * SCALE)
        both = jnp.concatenate([queries, grad], axis=0).T
        none = jnp.zeros_like(both)
        total[pl.ds(start, SPAN), :] += dot(weights, jnp.where(left, none, both)) + dot(
            grad_scores, jnp.where(left, both, none)
        )
        return 0

    lax.fori_loop(0, STEPS, step, 0)

    def last(i, _):
        first = pl.multiple_of(i * BLOCK, BLOCK)
        turned = total[pl.ds(first, BLOCK), :].T
        grads[1, :, pl.ds(first, BLOCK)] = bfloat(turned[:HEAD] * SCALE)
        grads[2, :, pl.ds(first, BLOCK)] = bfloat(turned[HEAD:])
        return 0

    lax.fori_loop(0, STEPS, last, 0)


def attend_back(bounds, qkv, logsum, grad_mixed):
    vmem = pl.BlockSpec(memory_space=pltpu.VMEM)
    return pl.pallas_call(
        attend_back_kernel,
        out_shape=jax.ShapeDtypeStruct((3, HEAD, LENGTH), BF),
        in_specs=[pl.BlockSpec(memory_space=pltpu.SMEM), vmem, vmem, vmem],
        out_specs=vmem,
        scratch_shapes=[
            pltpu.VMEM((LENGTH, 2 * HEAD), BF),
            pltpu.VMEM((2 * HEAD, LENGTH), BF),
            pltpu.VMEM((LENGTH, 2 * HEAD), F32),
        ],
        name="attend_back",
        compiler_params=pltpu.CompilerParams(vmem_limit_bytes=50 * 2**20),
    )(bounds, qkv, logsum, grad_mixed)


def product(former, latter):
    return jnp.dot(former, latter, preferred_element_type=F32)


def product_tn(former, latter):
    return lax.dot_general(former, latter, (((0,), (0,)), ((), ())), preferred_element_type=F32)


def product_nt(former, latter):
    return lax.dot_general(former, latter, (((1,), (1,)), ((), ())), preferred_element_type=F32)


def smooth(tensor):
    return jax.nn.gelu(tensor, approximate=True)


def swap(value):
    return lax.ppermute(value, "tok", [(t, t ^ 1) for t in range(16)])


def both_cores(core, value):
    other = swap(value)
    return jnp.where(
        core == 0,
        jnp.concatenate([value, other], axis=0),
        jnp.concatenate([other, value], axis=0),
    )


def own_rows(core, partial):
    mine = lax.dynamic_slice_in_dim(partial, core * ROWS, ROWS, 0)
    yours = lax.dynamic_slice_in_dim(partial, (1 - core) * ROWS, ROWS, 0)
    return mine + swap(yours)


def normalize(tensor, norm_gain, norm_shift):
    centred = tensor - jnp.mean(tensor, axis=-1, keepdims=True)
    factor = lax.rsqrt(jnp.mean(centred * centred, axis=-1, keepdims=True) + EPSILON)
    normed = centred * factor
    return (normed * norm_gain + norm_shift, normed, factor)


def normalize_back(grad_out, normed, factor, norm_gain):
    grad_normed = grad_out * norm_gain
    grad_input = factor * (
        grad_normed
        - jnp.mean(grad_normed, axis=-1, keepdims=True)
        - normed * jnp.mean(grad_normed * normed, axis=-1, keepdims=True)
    )
    return (grad_input, jnp.sum(grad_out * normed, axis=0), jnp.sum(grad_out, axis=0))


def layer_forward(hidden, w, core, bounds, number):
    entry = both_cores(core, bfloat(hidden))
    queries = bfloat(product(entry, w["query"]) + w["b_query"])
    keys = bfloat(product(entry, w["key"]))
    values = bfloat(product(entry, w["value"]) + w["b_value"])
    stacked = jnp.stack([queries.T, keys.T, values.T]).reshape(3, CHIPS, HEAD, CHIP_ROWS)
    qkv = exchange(stacked, True, number)
    mixed_head, logsum = attend(bounds, qkv)
    mixed = exchange(mixed_head[None], False, number + 1).reshape(HALF, CHIP_ROWS).T
    branch = own_rows(core, product(mixed, w["out"]))
    first, normed_one, factor_one = normalize(
        hidden + branch + w["b_out"], w["gain_attn"], w["shift_attn"]
    )
    entry_two = both_cores(core, bfloat(first))
    before = product(entry_two, w["in"]) + w["b_in"]
    active = bfloat(smooth(before))
    second = own_rows(core, product(active, w["back"]))
    result, normed_two, factor_two = normalize(
        first + second + w["b_back"], w["gain_ffn"], w["shift_ffn"]
    )
    saved = (
        entry, qkv, logsum, mixed, normed_one, factor_one, entry_two, before, active, normed_two,
        factor_two,
    )
    return result, saved


def layer_backward(grad_out, w, saved, core, bounds, number):
    (
        entry, qkv, logsum, mixed, normed_one, factor_one, entry_two, before, active, normed_two,
        factor_two,
    ) = saved
    d_second, g_gain_ffn, g_shift_ffn = normalize_back(
        grad_out, normed_two, factor_two, w["gain_ffn"]
    )
    d_branch = bfloat(d_second)
    g_b_back = jnp.sum(widen(d_branch), axis=0)
    d_branch = both_cores(core, d_branch)
    d_active = product_nt(d_branch, w["back"])
    d_before = bfloat(jax.vjp(smooth, before)[1](d_active)[0])
    g_b_in = jnp.sum(widen(d_before), axis=0)
    d_first = d_second + own_rows(core, product_nt(d_before, w["in"]))
    d_inner, g_gain_attn, g_shift_attn = normalize_back(
        d_first, normed_one, factor_one, w["gain_attn"]
    )
    d_attn = bfloat(d_inner)
    g_b_out = jnp.sum(widen(d_attn), axis=0)
    d_attn = both_cores(core, d_attn)
    d_mixed = bfloat(product_nt(d_attn, w["out"]))
    grad_head = exchange(d_mixed.T.reshape(1, CHIPS, HEAD, CHIP_ROWS), True, number)[0]
    d_qkv = exchange(attend_back(bounds, qkv, logsum, grad_head), False, number + 1)
    d_queries, d_keys, d_values = [d_qkv[k].reshape(HALF, CHIP_ROWS).T for k in range(3)]
    g_b_query = jnp.sum(widen(d_queries), axis=0)
    g_b_value = jnp.sum(widen(d_values), axis=0)
    d_hidden = d_inner + own_rows(
        core,
        product_nt(d_queries, w["query"])
        + product_nt(d_keys, w["key"])
        + product_nt(d_values, w["value"]),
    )
    vectors = (
        g_b_query, g_b_value, g_b_out, g_gain_attn, g_shift_attn, g_b_back, g_gain_ffn,
        g_shift_ffn, g_b_in,
    )
    pairs = (
        (entry, d_queries), (entry, d_keys), (entry, d_values), (mixed, d_attn),
        (entry_two, d_before), (active, d_branch),
    )
    return d_hidden, vectors, pairs


def on_device(
    tokens, cotangent, doc_lengths, pad_counts, w_query, b_query, w_key, w_value, b_value, w_out,
    b_out, gain_attn, shift_attn, w_in, b_in, w_back, b_back, gain_ffn, shift_ffn,
):
    tok = lax.axis_index("tok")
    core = tok % 2
    live = LENGTH - pad_counts[0]
    ends = jnp.cumsum(doc_lengths[0])
    bounds = jnp.minimum(ends, live).astype(jnp.int32)

    pack = jnp.stack(
        [
            jnp.concatenate(
                [w[:, HALF * half : HALF * half + HALF] for w in (w_query, w_key, w_value, w_out)]
                + [w_in[:, 2048 * half + HALF * k : 2048 * half + HALF * k + HALF] for k in range(4)]
                + [w_back[:, HALF * half : HALF * half + HALF]],
                axis=0,
            )
            for half in range(2)
        ]
    )
    eight = jnp.stack(
        [b_query, b_value, b_out, gain_attn, shift_attn, b_back, gain_ffn, shift_ffn]
    )
    small = lax.dynamic_update_slice(jnp.zeros((16, 128), BF), eight, (0, tok * 8))
    small = lax.dynamic_update_slice(small, b_in[None], (8 + tok // 4, (tok % 4) * 32))
    ga, gb, _, gs, wo, wb = gather_weights(pack, small)
    ga, gb = ga.reshape(64, 4, 16, HALF), gb.reshape(64, 4, 16, HALF)
    lines = jnp.sum(widen(gs.reshape(8, 8, 16, 128)), axis=1)
    vectors = [lines[:, k].reshape(D) for k in range(8)]

    def half_of(vector):
        return lax.dynamic_slice_in_dim(vector, core * (vector.shape[0] // 2), vector.shape[0] // 2)

    w = {
        "query": ga[:, 0].reshape(D, HALF),
        "key": ga[:, 1].reshape(D, HALF),
        "value": ga[:, 2].reshape(D, HALF),
        "out": jnp.concatenate([wo[0].reshape(HALF, HALF), wo[1].reshape(HALF, HALF)], axis=1),
        "in": jnp.concatenate([gb[:, k].reshape(D, HALF) for k in range(4)], axis=1),
        "back": jnp.concatenate([wb[0].reshape(2048, HALF), wb[1].reshape(2048, HALF)], axis=1),
        "b_query": half_of(vectors[0]),
        "b_value": half_of(vectors[1]),
        "b_out": vectors[2],
        "gain_attn": vectors[3],
        "shift_attn": vectors[4],
        "b_back": vectors[5],
        "gain_ffn": vectors[6],
        "shift_ffn": vectors[7],
        "b_in": half_of(lines[:, 8:12].reshape(FF)),
    }
    middle, saved_one = layer_forward(widen(tokens), w, core, bounds, 2)
    result, saved_two = layer_forward(middle, w, core, bounds, 4)
    d_middle, vectors_two, pairs_two = layer_backward(
        widen(cotangent), w, saved_two, core, bounds, 6
    )
    d_tokens, vectors_one, pairs_one = layer_backward(d_middle, w, saved_one, core, bounds, 8)

    def gradient(k):
        former = jnp.concatenate([pairs_one[k][0], pairs_two[k][0]], axis=0)
        latter = jnp.concatenate([pairs_one[k][1], pairs_two[k][1]], axis=0)
        return bfloat(product_tn(former, latter))

    da = jnp.stack([gradient(k).reshape(64, 16, HALF) for k in range(3)], axis=1)
    do = gradient(3).reshape(32, 16, 2, HALF).transpose(2, 0, 1, 3)
    db = gradient(4).reshape(64, 16, 4, HALF).transpose(0, 2, 1, 3)
    dc = gradient(5).reshape(32, 64, 2, HALF).transpose(2, 0, 1, 3)
    sums = [a + b for a, b in zip(vectors_one, vectors_two)]

    def placed(vector):
        zeros = jnp.zeros((2 * vector.shape[0],), F32)
        return lax.dynamic_update_slice_in_dim(zeros, vector, core * vector.shape[0], 0)

    sums = [placed(sums[0]), placed(sums[1])] + sums[2:8] + [placed(sums[8])]
    lines = jnp.concatenate(
        [
            jnp.stack(sums[:8]).reshape(8, 8, 128).transpose(1, 0, 2),
            sums[8].reshape(8, 4, 128),
            jnp.zeros((8, 4, 128), F32),
        ],
        axis=1,
    )
    lines = lines + swap(lines)
    ds = jnp.broadcast_to(bfloat(lines)[:, None], (8, 8, 16, 128)).reshape(CUBE + (16, 128))
    grads = scatter_gradients(
        da.reshape(CUBE + (48, HALF)),
        do.reshape(2, 2, 2, 2, 4, 16, HALF),
        db.reshape(CUBE + (64, HALF)),
        dc.reshape(2, 2, 2, 2, 4, 64, HALF),
        ds,
    )
    g_query, g_key, g_value, g_out, g_in, g_back, tiny = grads
    eight = lax.dynamic_slice(tiny, (0, tok * 8), (8, 8))
    g_b_in = lax.dynamic_slice(tiny, (8 + tok // 4, (tok % 4) * 32), (1, 32))[0]
    (
        g_b_query, g_b_value, g_b_out, g_gain_attn, g_shift_attn, g_b_back, g_gain_ffn, g_shift_ffn,
    ) = [eight[k] for k in range(8)]
    return (
        bfloat(result), bfloat(d_tokens), g_query, g_b_query, g_key, g_value, g_b_value, g_out,
        g_b_out, g_gain_attn, g_shift_attn, g_in, g_b_in, g_back, g_b_back, g_gain_ffn, g_shift_ffn,
    )


def solution(mesh):
    both = ("seq", "tok")
    rows, vector = P(both, None), P(both)
    ins = (
        rows, rows, P("seq", None), P("seq"), rows, vector, rows, rows, vector, rows, vector, vector,
        vector, rows, vector, rows, vector, vector, vector,
    )
    outs = (
        rows, rows, rows, vector, rows, rows, vector, rows, vector, vector, vector, rows, vector,
        rows, vector, vector, vector,
    )
    return jax.shard_map(on_device, mesh=mesh, in_specs=ins, out_specs=outs, check_vma=False)
```

time: 5440 us -> 579 us (0.11)
  waiting for transfers between devices: 4800 us -> 18.8 us
  Pallas kernels: 0 us -> 392 us
  matrix products: 229 us -> 52.2 us
  blocking collectives: 140 us -> 0 us
  starting transfers between devices: 82.7 us -> 17.6 us
    reduce_scatter x6 -> x0, waiting for transfers between devices: 3650 us -> none  [spread_layer(): lax.psum_scatter(gradients, ('seq', 'tok'), scatter_dimension=0, tiled=True)]
    all_gather x6 -> x0, waiting for transfers between devices: 1050 us -> none  [the longest x1 202 us: on_device(): lax.all_gather(w_query, ('seq', 'tok'), axis=0, tiled=True)]
    pallas_call x0 -> x14, Pallas kernels: none -> 392 us  [the longest x1 143 us: gather_weights(): pl.pallas_call(gather_kernel, out_shape=(big, big, big, jax.ShapeDtypeStr...]
    unnamed x2 -> x0, blocking collectives: 140 us -> none
    dot_general x24 -> x12, matrix products: 142 us -> 17 us  [product(): return jnp.dot(former, latter, preferred_element_type=F32)]
    ppermute x24 -> x17, waiting for transfers between devices: 103 us -> 18.8 us  [swap(): return lax.ppermute(value, 'tok', [(t, t ^ 1) for t in range(16)])]
    ppermute x24 -> x17, starting transfers between devices: 81.7 us -> 17.6 us  [swap(): return lax.ppermute(value, 'tok', [(t, t ^ 1) for t in range(16)])]
  transfers between devices with their start and end apart: 36 -> 17, of which waited for: 24 -> 11; matrix products, arithmetic and copies ran while one was open for 4% -> 14% of each run, Pallas kernels for 0% -> 38%
where the time goes in v1:
time: 579 us; the launch traced here: 571 us
  Pallas kernels  392 us (68%)
  local copies, waits for them, and re-layouts  64 us (11%)
  matrix products  52.2 us (9%)
  other arithmetic  23.8 us (4%)
  waiting for transfers between devices  18.8 us (3%)
  starting transfers between devices  17.6 us (3%)
    pallas_call x1, Pallas kernels, gather_weights(): pl.pallas_call(gather_kernel, out_shape=(big, big, big, jax.ShapeDtypeStr...  143 us
    pallas_call x8, Pallas kernels, exchange(): pl.pallas_call(functools.partial(exchange_kernel, outward), out_shape=jax...  114 us
    pallas_call x1, Pallas kernels, scatter_gradients(): pl.pallas_call(scatter_kernel, out_shape=(jax.ShapeDtypeStruct((8, D), F3...  74.9 us
    pallas_call x2, Pallas kernels, attend_back(): pl.pallas_call(attend_back_kernel, out_shape=jax.ShapeDtypeStruct((3, HEA...  37.5 us
    pallas_call x2, Pallas kernels, attend(): pl.pallas_call(attend_kernel, out_shape=(jax.ShapeDtypeStruct((HEAD, LENG...  22.2 us
    dot_general x12, matrix products, product_nt(): lax.dot_general(former, latter, (((1,), (1,)), ((), ())), preferred_eleme...  19.9 us
    ppermute x17, waiting for transfers between devices, swap(): return lax.ppermute(value, 'tok', [(t, t ^ 1) for t in range(16)])  18.8 us
    ppermute x17, starting transfers between devices, swap(): return lax.ppermute(value, 'tok', [(t, t ^ 1) for t in range(16)])  17.6 us
  transfers between devices with their start and end apart: 17, of which 11 were waited for; matrix products, arithmetic and copies ran while one was open for 14% of the time, Pallas kernels for 38%

profile of v1, /device:TPU:1, one launch (start us, length us, event | category | flops | bytes accessed | tf_op | source)
XLA Modules:
  0.0 571.2 jit_solution(17666613806573999110)
XLA Ops:
  13.5 142.5 %gather_weights.1 = (bf16[4,2,2,4,64,512]{5,4,3,2,1,0:T(8,128)(2,1)}, bf16[4,2,2,4,64,512]{5,4,3,2,1,0:T(8,128)(2,1)}, bf16[4,2,2,4,64,512]{5,4,3,2,1,0:T(8,128)...) custom-call(bf16[2,96,512]{2,1,0:T(8,128)(2,1)} %pad_maximum_fusion., ...), custom_call_target="tpu_custom_call" | custom-call | tf_op jit(solution)/shard_map/gather_weights/pallas_call | solution.py:213
  160.0 2.2 fusion.81
  165.1 19.1 %exchange_2.1.qkv = bf16[3,64,3072]{2,1,0:T(8,128)(2,1)S(1)} custom-call(bf16[3,8,64,384]{3,2,1,0:T(8,128)(2,1)S(1)} %pad_maximum_fusion.4.value), custom_call_target="tpu_custom_call" | custom-call | tf_op jit(solution)/shard_map/exchange_2/pallas_call | solution.py:511
  184.2 11.1 %attend.2 = (bf16[64,3072]{1,0:T(8,128)(2,1)S(1)}, f32[1,3072]{1,0:T(1,128)S(1)}) custom-call(s32[4]{0:T(128)S(1)} %minimum_bitcast_fusion.bounds, bf16[3,64,3072]{2,1,0:T(8,128)(2,1)S(1)} %exchange_2.1.qkv), custom_call_target="tpu_custom_call" | custom-call | tf_op jit(solution)/shard_map/attend/pallas_call | solution.py:580
  195.3 7.4 %exchange_3.1 = bf16[1,8,64,384]{3,2,1,0:T(8,128)(2,1)S(1)} custom-call(bf16[1,64,3072]{2,1,0:T(8,128)(2,1)S(1)} %bitcast.170), custom_call_target="tpu_custom_call" | custom-call | tf_op jit(solution)/shard_map/exchange_3/pallas_call | solution.py:511
  204.6 3.8 collective-permute-start.1
  208.3 2.0 collective-permute-done.1
  210.4 1.7 fusion.78
  213.2 2.2 fusion.80
  215.4 2.7 fusion.79
  218.1 2.0 maximum_select_fusion.1
  220.2 5.4 multiply_convert_fusion.1
  225.6 1.8 fusion.70
  227.6 2.1 collective-permute-done.3
  235.3 19.8 %exchange_4.1.qkv = bf16[3,64,3072]{2,1,0:T(8,128)(2,1)S(1)} custom-call(bf16[3,8,64,384]{3,2,1,0:T(8,128)(2,1)S(1)} %pad_maximum_fusion.5.value), custom_call_target="tpu_custom_call" | custom-call | tf_op jit(solution)/shard_map/exchange_4/pallas_call | solution.py:511
  255.2 11.1 %attend.3 = (bf16[64,3072]{1,0:T(8,128)(2,1)S(1)}, f32[1,3072]{1,0:T(1,128)S(1)}) custom-call(s32[4]{0:T(128)S(1)} %minimum_bitcast_fusion.bounds, bf16[3,64,3072]{2,1,0:T(8,128)(2,1)S(1)} %exchange_4.1.qkv), custom_call_target="tpu_custom_call" | custom-call | tf_op jit(solution)/shard_map/attend/pallas_call | solution.py:580
  266.2 11.0 %exchange_5.1 = bf16[1,8,64,384]{3,2,1,0:T(8,128)(2,1)S(1)} custom-call(bf16[1,64,3072]{2,1,0:T(8,128)(2,1)S(1)} %bitcast.171), custom_call_target="tpu_custom_call" | custom-call | tf_op jit(solution)/shard_map/exchange_5/pallas_call | solution.py:511
  278.0 2.7 collective-permute-start.5
  280.7 1.9 collective-permute-done.5
  286.0 2.3 multiply_convert_fusion
  288.4 1.8 fusion.69
  290.7 1.9 collective-permute-done.7
  296.2 3.7 convert_reduce_fusion
  299.9 2.6 fusion.73
  303.0 1.9 collective-permute-done.9
  309.8 9.9 %exchange_6.1 = bf16[1,64,3072]{2,1,0:T(8,128)(2,1)S(1)} custom-call(bf16[1,8,64,384]{3,2,1,0:T(8,128)(2,1)S(1)} %bitcast.173), custom_call_target="tpu_custom_call" | custom-call | tf_op jit(solution)/shard_map/exchange_6/pallas_call | solution.py:511
  319.7 18.8 %attend_back.2.value = bf16[3,64,3072]{2,1,0:T(8,128)(2,1)S(1)} custom-call(s32[4]{0:T(128)S(1)} %minimum_bitcast_fusion.bounds, bf16[3,64,3072]{2,1,0:T(8,128)(2,1)S(1)} %exchange_4.1.qkv, f32[1,3072]{1,0:T(1,128)S(1)} %get-tuple-element.40.logsum, bf16[64,3072]{1,0:T(8,128)(2,1)S(1)} %bitcast.169), custom_call_target="tpu_custom_call" | custom-call | tf_op jit(solution)/shard_map/attend_back/pallas_call | solution.py:634
  338.5 17.8 %exchange_7.1 = bf16[3,8,64,384]{3,2,1,0:T(8,128)(2,1)S(1)} custom-call(bf16[3,64,3072]{2,1,0:T(8,128)(2,1)S(1)} %attend_back.2.value), custom_call_target="tpu_custom_call" | custom-call | tf_op jit(solution)/shard_map/exchange_7/pallas_call | solution.py:511
  358.6 2.1 collective-permute-start.11
  360.7 1.9 collective-permute-done.11
  365.9 3.7 convert_reduce_fusion.1
  369.6 2.6 fusion.72
  373.3 5.1 convolution_convert_fusion
  380.6 5.1 convolution_convert_fusion.1
  385.7 7.9 %reshape.387 = bf16[32,64,2,512]{3,2,1,0:T(2,128)(2,1)} reshape(bf16[2048,1024]{1,0:T(8,128)(2,1)} %convolution_convert_fusion) | data formatting | bytes 8388608 | tf_op jit(solution)/shard_map/reshape | solution.py:838
  393.5 5.2 copy.41
  398.7 7.8 %reshape.385 = bf16[64,16,4,512]{3,2,1,0:T(4,128)(2,1)} reshape(bf16[1024,2048]{1,0:T(8,128)(2,1)} %convolution_convert_fusion.1) | data formatting | bytes 8388608 | tf_op jit(solution)/shard_map/reshape | solution.py:837
  406.5 5.6 copy.40
  414.6 11.5 %exchange_8.1 = bf16[1,64,3072]{2,1,0:T(8,128)(2,1)S(1)} custom-call(bf16[1,8,64,384]{3,2,1,0:T(8,128)(2,1)S(1)} %bitcast.172), custom_call_target="tpu_custom_call" | custom-call | tf_op jit(solution)/shard_map/exchange_8/pallas_call | solution.py:511
  426.1 18.8 %attend_back.3.value = bf16[3,64,3072]{2,1,0:T(8,128)(2,1)S(1)} custom-call(s32[4]{0:T(128)S(1)} %minimum_bitcast_fusion.bounds, bf16[3,64,3072]{2,1,0:T(8,128)(2,1)S(1)} %exchange_2.1.qkv, f32[1,3072]{1,0:T(1,128)S(1)} %get-tuple-element.41.logsum, bf16[64,3072]{1,0:T(8,128)(2,1)S(1)} %bitcast.168), custom_call_target="tpu_custom_call" | custom-call | tf_op jit(solution)/shard_map/attend_back/pallas_call | solution.py:634
  444.9 17.8 %exchange_9.1 = bf16[3,8,64,384]{3,2,1,0:T(8,128)(2,1)S(1)} custom-call(bf16[3,64,3072]{2,1,0:T(8,128)(2,1)S(1)} %attend_back.3.value), custom_call_target="tpu_custom_call" | custom-call | tf_op jit(solution)/shard_map/exchange_9/pallas_call | solution.py:511
  464.8 2.0 collective-permute-start.16
  469.1 1.8 add_add_fusion
  475.5 2.0 pad_maximum_fusion.2
  477.5 2.0 fusion.30
  479.5 1.9 reshape.383
  484.3 74.9 %scatter_gradients.1 = (f32[8,1024]{1,0:T(8,128)}, f32[8,1024]{1,0:T(8,128)}, f32[8,1024]{1,0:T(8,128)}, f32[8,1024]{1,0:T(8,128)}, f32[8,4096]{1,0:T(8,128)}, /*index=5*/f32[32,1024]{1,0:T(8,128)}, f32[16,128]{1,0:T(8,128)}) custom-call(bf16[4,2,2,4,48,512]{5,4,3,2,1,0:T(8,128)(2,1)} %bitcast.176, bf16[2,2,2,2,4,16,512]{6,5,4,3,2,1,0:T(8,128)(2,1)} %bitcast.197, ...), custom_call_target="tpu_custom_call" | custom-call | tf_op jit(solution)/shard_map/scatter_gradients/pallas_call | solution.py:432
  561.9 2.1 add_convert_fusion
  (299 shorter events, 73.1 us)
Async XLA Ops:
  0.7 161.6 %collective-permute-start = (bf16[192,1024]{1,0:T(8,128)(2,1)}, bf16[192,1024]{1,0:T(8,128)(2,1)S(1)}, u32[]{:S(2)}, u32[]{:S(2)}) collective-permute-start(bf16[192,1024]{1,0:T(8,128)(2,1)} %param.19), channel_id=1, source_target_pairs={{0,1},{1,0},{2,3},{3,2},{4,5},{5,4},{6,7},{7,6},{8,9},{9,8},{10,11... | collective-permute-start | bytes 1179656 | tf_op jit(solution)/shard_map/ppermute | solution.py:666
  159.8 42.9 %copy-start.10 = (bf16[1,2,2,2,4,16,512]{6,5,4,3,2,1,0:T(8,128)(2,1)}, bf16[1,2,2,2,4,16,512]{6,5,4,3,2,1,0:T(8,128)(2,1)S(1)}, u32[]{:S(2)}) copy-start(bf16[1,2,2,2,4,16,512]{6,5,4,3,2,1,0:T(8,128)(2,1)S(1)} %get-tuple-element.103) | copy-start | bytes 1572868
  204.6 5.8 %collective-permute-start.1 = (f32[192,1024]{1,0:T(8,128)S(1)}, f32[192,1024]{1,0:T(8,128)}, u32[]{:S(2)}, u32[]{:S(2)}) collective-permute-start(f32[192,1024]{1,0:T(8,128)S(1)} %constant_dynamic-slice_fusion.8), channel_id=1, source_target_pairs={{0,1},{1,0},{2,3},{3,2},{4,5},{5,4},{6,7},{7,6},{8,9},{9,8},{10,11... | collective-permute-start | bytes 2359304 | tf_op jit(solution)/shard_map/ppermute | solution.py:666
  208.3 4.9 copy-start.13
  212.5 5.6 collective-permute-start.2
  215.4 4.7 copy-start.33
  215.4 4.7 copy-start.36
  215.4 4.7 copy-start.39
  215.4 4.7 copy-start.42
  218.1 7.5 %copy-start.26 = (bf16[1,2,2,2,4,64,512]{6,5,4,3,2,1,0:T(8,128)(2,1)}, bf16[1,2,2,2,4,64,512]{6,5,4,3,2,1,0:T(8,128)(2,1)S(1)}, u32[]{:S(2)}) copy-start(bf16[1,2,2,2,4,64,512]{6,5,4,3,2,1,0:T(8,128)(2,1)S(1)} %get-tuple-element.88) | copy-start | bytes 6291460
  218.1 78.1 %copy-start.24 = (bf16[1,2,2,2,4,64,512]{6,5,4,3,2,1,0:T(8,128)(2,1)}, bf16[1,2,2,2,4,64,512]{6,5,4,3,2,1,0:T(8,128)(2,1)S(1)}, u32[]{:S(2)}) copy-start(bf16[1,2,2,2,4,64,512]{6,5,4,3,2,1,0:T(8,128)(2,1)S(1)} %get-tuple-element.87) | copy-start | bytes 6291460
  220.1 5.4 copy-start.49
  227.4 2.4 collective-permute-start.3
  230.7 1.8 collective-permute-start.4
  235.2 42.1 %copy-start.11 = (bf16[1,2,2,2,4,16,512]{6,5,4,3,2,1,0:T(8,128)(2,1)S(1)}, bf16[1,2,2,2,4,16,512]{6,5,4,3,2,1,0:T(8,128)(2,1)}, u32[]{:S(2)}) copy-start(bf16[1,2,2,2,4,16,512]{6,5,4,3,2,1,0:T(8,128)(2,1)} %copy-done.10) | copy-start | bytes 1572868
  277.9 8.1 %copy-start.34 = (bf16[64,1,16,512]{3,2,1,0:T(8,128)(2,1)S(1)}, bf16[64,1,16,512]{3,2,1,0:T(8,128)(2,1)}, u32[]{:S(2)}) copy-start(bf16[64,1,16,512]{3,2,1,0:T(8,128)(2,1)} %get-tuple-element.89) | copy-start | bytes 3145732
  277.9 8.1 %copy-start.37 = (bf16[64,1,16,512]{3,2,1,0:T(8,128)(2,1)S(1)}, bf16[64,1,16,512]{3,2,1,0:T(8,128)(2,1)}, u32[]{:S(2)}) copy-start(bf16[64,1,16,512]{3,2,1,0:T(8,128)(2,1)} %get-tuple-element.90) | copy-start | bytes 3145732
  277.9 8.1 %copy-start.40 = (bf16[64,1,16,512]{3,2,1,0:T(8,128)(2,1)S(1)}, bf16[64,1,16,512]{3,2,1,0:T(8,128)(2,1)}, u32[]{:S(2)}) copy-start(bf16[64,1,16,512]{3,2,1,0:T(8,128)(2,1)} %get-tuple-element.91) | copy-start | bytes 3145732
  278.0 8.1 %copy-start.43 = (bf16[64,1,16,512]{3,2,1,0:T(8,128)(2,1)S(1)}, bf16[64,1,16,512]{3,2,1,0:T(8,128)(2,1)}, u32[]{:S(2)}) copy-start(bf16[64,1,16,512]{3,2,1,0:T(8,128)(2,1)} %get-tuple-element.92) | copy-start | bytes 3145732
  278.0 4.6 collective-permute-start.5
  283.5 2.2 collective-permute-start.6
  290.3 2.4 collective-permute-start.7
  294.1 1.8 collective-permute-start.8
  302.6 2.4 collective-permute-start.9
  306.8 2.0 collective-permute-start.10
  309.1 29.5 %copy-start.51 = (bf16[384,1024]{1,0:T(8,128)(2,1)}, bf16[384,1024]{1,0:T(8,128)(2,1)S(1)}, u32[]{:S(2)}) copy-start(bf16[384,1024]{1,0:T(8,128)(2,1)S(1)} %maximum_select_fusion.5) | copy-start | bytes 2359300
  356.5 16.3 %copy-start.14 = (bf16[1,8,64,384]{3,2,1,0:T(8,128)(2,1)}, bf16[1,8,64,384]{3,2,1,0:T(8,128)(2,1)S(1)}, u32[]{:S(2)}) copy-start(bf16[1,8,64,384]{3,2,1,0:T(8,128)(2,1)S(1)} %get-tuple-element.99) | copy-start | bytes 1179652
  356.5 16.5 %copy-start.19 = (bf16[1,8,64,384]{3,2,1,0:T(8,128)(2,1)}, bf16[1,8,64,384]{3,2,1,0:T(8,128)(2,1)S(1)}, u32[]{:S(2)}) copy-start(bf16[1,8,64,384]{3,2,1,0:T(8,128)(2,1)S(1)} %get-tuple-element.101) | copy-start | bytes 1179652
  358.6 4.0 collective-permute-start.11
  363.5 1.8 collective-permute-start.12
  365.9 3.7 copy-start.41
  365.9 3.7 copy-start.44
  372.3 6.0 %collective-permute-start.13 = (f32[192,1024]{1,0:T(8,128)S(1)}, f32[192,1024]{1,0:T(8,128)S(1)}, u32[]{:S(2)}, u32[]{:S(2)}) collective-permute-start(f32[192,1024]{1,0:T(8,128)S(1)} %constant_dynamic-slice_fusion.2), channel_id=1, source_target_pairs={{0,1},{1,0},{2,3},{3,2},{4,5},{5,4},{6,7},{7,6},{8,9},{9,8},{10,11... | collective-permute-start | bytes 2359304 | tf_op jit(solution)/shard_map/ppermute | solution.py:666
  372.8 91.8 %copy-start.64 = (f32[16]{0:T(128)}, f32[16]{0:T(128)S(1)}, u32[]{:S(2)}) copy-start(f32[16]{0:T(128)S(1)} %pad.2.clone) | copy-start | bytes 196
  380.2 32.0 %collective-permute-start.14 = (bf16[192,1024]{1,0:T(8,128)(2,1)}, bf16[192,1024]{1,0:T(8,128)(2,1)}, u32[]{:S(2)}, u32[]{:S(2)}) collective-permute-start(bf16[192,1024]{1,0:T(8,128)(2,1)} %get-tuple-element.74), channel_id=1, source_target_pairs={{0,1},{1,0},{2,3},{3,2},{4,5},{5,4},{6,7},{7,6},{8,9},{9,8},{10,11... | collective-permute-start | bytes 1179656 | tf_op jit(solution)/shard_map/ppermute | solution.py:666
  406.5 7.3 %copy-start.12 = (bf16[1,2,2,2,4,16,512]{6,5,4,3,2,1,0:T(8,128)(2,1)S(1)}, bf16[1,2,2,2,4,16,512]{6,5,4,3,2,1,0:T(8,128)(2,1)}, u32[]{:S(2)}) copy-start(bf16[1,2,2,2,4,16,512]{6,5,4,3,2,1,0:T(8,128)(2,1)} %copy-done.10) | copy-start | bytes 1572868
  412.1 52.6 %copy-start.59 = (f32[4096]{0:T(1024)}, f32[4096]{0:T(1024)S(1)}, u32[]{:S(2)}) copy-start(f32[4096]{0:T(1024)S(1)} %add_dynamic-update-slice_fusion) | copy-start | bytes 49156
  413.8 12.2 %copy-start.57 = (bf16[384,1024]{1,0:T(8,128)(2,1)}, bf16[384,1024]{1,0:T(8,128)(2,1)S(1)}, u32[]{:S(2)}) copy-start(bf16[384,1024]{1,0:T(8,128)(2,1)S(1)} %maximum_select_fusion.7) | copy-start | bytes 2359300
  444.9 21.9 %copy-start.5 = (bf16[64,1,16,512]{3,2,1,0:T(8,128)(2,1)S(1)}, bf16[64,1,16,512]{3,2,1,0:T(8,128)(2,1)}, u32[]{:S(2)}) copy-start(bf16[64,1,16,512]{3,2,1,0:T(8,128)(2,1)} %copy-done.3) | copy-start | bytes 3145732
  462.7 5.7 copy-start.2
  463.6 5.5 copy-start.16
  464.7 3.8 copy-start.22
  464.7 4.4 copy-start.8
  464.8 17.8 %collective-permute-start.16 = (f32[8,16,128]{2,1,0:T(8,128)S(1)}, f32[8,16,128]{2,1,0:T(8,128)}, u32[]{:S(2)}, u32[]{:S(2)}) collective-permute-start(f32[8,16,128]{2,1,0:T(8,128)S(1)} %maximum_maximum_fusion), channel_id=1, source_target_pairs={{0,1},{1,0},{2,3},{3,2},{4,5},{5,4},{6,7},{7,6},{8,9},{9,8},{10,11... | collective-permute-start | bytes 196616 | tf_op jit(solution)/shard_map/ppermute | solution.py:666
  471.9 90.0 %collective-permute-start.15 = (f32[192,1024]{1,0:T(8,128)}, f32[192,1024]{1,0:T(8,128)}, u32[]{:S(2)}, u32[]{:S(2)}) collective-permute-start(f32[192,1024]{1,0:T(8,128)} %constant_dynamic-slice_fusion.1), channel_id=1, source_target_pairs={{0,1},{1,0},{2,3},{3,2},{4,5},{5,4},{6,7},{7,6},{8,9},{9,8},{10,11... | collective-permute-start | bytes 2359304 | tf_op jit(solution)/shard_map/ppermute | solution.py:666
  484.3 77.6 %copy-start.23 = (f32[192,1024]{1,0:T(8,128)S(1)}, f32[192,1024]{1,0:T(8,128)}, u32[]{:S(2)}) copy-start(f32[192,1024]{1,0:T(8,128)} %get-tuple-element.75) | copy-start | bytes 2359300
  559.2 10.2 %copy-start.62 = (f32[8,4096]{1,0:T(8,128)S(1)}, f32[8,4096]{1,0:T(8,128)}, u32[]{:S(2)}) copy-start(f32[8,4096]{1,0:T(8,128)} %get-tuple-element.173) | copy-start | bytes 393220
  559.3 10.8 %copy-start.61 = (f32[32,1024]{1,0:T(8,128)S(1)}, f32[32,1024]{1,0:T(8,128)}, u32[]{:S(2)}) copy-start(f32[32,1024]{1,0:T(8,128)} %get-tuple-element.175) | copy-start | bytes 393220
  (42 other events, 98.6 us)

commit v2 on v0

v2 whole, which is shorter than its diff:
```python
import math
import types

import jax
import jax.numpy as jnp
from jax import lax
from jax.experimental import pallas as pl
from jax.experimental.pallas import tpu as pltpu
from jax.sharding import PartitionSpec as P

HEADS = 16
WINDOW = 1024
D = 1024
FF = 4096
HEAD = 64
CHIPS = 8
ROWS = 192
CHIP_ROWS = 2 * ROWS
LENGTH = CHIP_ROWS * CHIPS
HALF = 512
EPSILON = 1e-05
MASKED = -1e30
SCALE = 1.0 / math.sqrt(HEAD)
LOG2E = 1.4426950408889634
MESH = pl.DeviceIdType.MESH
BF = jnp.bfloat16
F32 = jnp.float32
CUBE = (4, 2, 2, 4)
X, Y, Z, CORE = range(4)


def bfloat(tensor):
    return tensor.astype(BF)


def widen(tensor):
    return tensor.astype(F32)


def place():
    seq, tok = lax.axis_index("seq"), lax.axis_index("tok")
    x = (tok // 8) * 2 + seq % 2
    return {X: x, Y: seq // 2, Z: (tok // 2) % 4, CORE: tok % 2}


def device(x, y, z, core):
    return (y * 2 + x % 2, (x // 2) * 8 + z * 2 + core)


def moved(here, axis, steps):
    there = dict(here)
    there[axis] = lax.rem(here[axis] + steps + 4, 4)
    return device(there[X], there[Y], there[Z], there[CORE])


def partner(here):
    return device(here[X], here[Y], here[Z], 1 - here[CORE])


def cube_index(here, whole, axis, value):
    index = []
    for name in (Y, X, Z):
        if name in whole:
            index += [slice(None)] * (2 if name == X else 1)
        else:
            at = value if name == axis else here[name]
            index += [at % 2, at // 2] if name == X else [at]
    return tuple(index)


def greet(targets):
    barrier = pltpu.get_barrier_semaphore()
    for target in targets:
        pl.semaphore_signal(barrier, inc=1, device_id=target, device_id_type=MESH)
    pl.semaphore_wait(barrier, len(targets))


def neighbours(here, steps):
    return [moved(here, axis, step) for axis in (X, Y, Z) for step in steps] + [partner(here)]


def group_device(here, number):
    seq = lax.axis_index("seq")
    return (seq, (number // 4) * 8 + (number % 4) * 2 + here[CORE])


def group_number(here):
    return (here[X] // 2) * 4 + here[Z]


def group(here):
    me = group_number(here)
    return [group_device(here, lax.rem(me + k, CHIPS)) for k in range(1, CHIPS)]


class Wire:
    def __init__(self, here, send, recv, local):
        self.send, self.recv, self.local = send, recv, local
        self.here, self.number, self.locals = here, 0, 0
        self.core, self.me = here[CORE], group_number(here)
        self.own = pl.ds(pl.multiple_of(self.core * ROWS, ROWS), ROWS)
        self.other = pl.ds(pl.multiple_of((1 - self.core) * ROWS, ROWS), ROWS)

    def to(self, source, target, device_id):
        copy = pltpu.make_async_remote_copy(
            src_ref=source,
            dst_ref=target,
            send_sem=self.send.at[self.number],
            recv_sem=self.recv.at[self.number],
            device_id=device_id,
            device_id_type=MESH,
        )
        self.number += 1
        copy.start()
        return copy

    def swap(self, source, target):
        return self.to(source, target, partner(self.here))

    def fetch(self, source, target):
        copy = pltpu.make_async_copy(source, target, self.local.at[self.locals])
        self.locals += 1
        copy.start()
        return copy

    def spread(self, stage, target):
        span = chunk_span(self.me)
        copies = []
        for k in range(1, CHIPS):
            to = lax.rem(self.me + k, CHIPS)
            copies.append(self.to(stage.at[to], target.at[:, span], group_device(self.here, to)))
        copies.append(self.fetch(stage.at[self.me], target.at[:, span]))
        return copies


def chunk_span(number):
    return pl.ds(pl.multiple_of(number * CHIP_ROWS, CHIP_ROWS), CHIP_ROWS)


EVERY = slice(None)
CUBE_ALL = (EVERY,) * 4
SIDES = (pl.ds(0, HALF // 2), pl.ds(HALF // 2, HALF // 2))
SIZES = {Y: (4,), X: (2, 2), Z: (4,)}
GATHER_ORDERS = ((X, Z, Y), (Y, X, Z), (Z, Y, X), (X, Z, Y))
SCATTER_ORDERS = ((Y, Z, X), (Z, X, Y), (X, Y, Z), (Y, Z, X))


def ring_gather(wire, parts):
    here = wire.here
    sent, kept = [], []
    for buffer, prefix, order, own, _, _ in parts:
        kept.append(wire.fetch(own, buffer.at[prefix + cube_index(here, (), None, None)]))
    for phase in range(2):
        copies = []
        for step in (1, -1, 2):
            for buffer, prefix, order, own, _, _ in parts:
                axis = order[phase]
                block = buffer.at[prefix + cube_index(here, order[:phase], axis, here[axis])]
                source = own if phase == 0 else block
                copies.append(wire.to(source, block, moved(here, axis, step)))
        yield
        for copy in copies:
            copy.wait_recv()
        sent += copies
        if phase == 0:
            for copy in kept:
                copy.wait()
    one, two = [], []
    for buffer, prefix, order, _, _, complete in parts:
        axis = order[2]
        block = buffer.at[prefix + cube_index(here, order[:2], axis, here[axis])]
        one.append([wire.to(block, block, moved(here, axis, step)) for step in (1, -1)])
    for _, _, order, _, _, complete in parts:
        complete(here[order[2]])
    yield
    for (buffer, prefix, order, _, cut, complete), pair in zip(parts, one):
        axis = order[2]
        for side, step in enumerate((1, -1)):
            pair[side].wait_recv()
            come = lax.rem(here[axis] - step + 4, 4)
            index = prefix + cube_index(here, order[:2], axis, come)
            if cut:
                index += (EVERY, SIDES[side])
            if cut or side == 0:
                block = buffer.at[index]
                two.append(wire.to(block, block, moved(here, axis, step)))
            complete(come)
        sent += pair
    yield
    for copy in two:
        copy.wait_recv()
    for _, _, order, _, _, complete in parts:
        complete(lax.rem(here[order[2]] + 2, 4))
    for copy in sent + two:
        copy.wait_send()


GATHER_COPIES = 3 + 3 + 4


def lengths_of(full):
    return tuple(n for name in (Y, X, Z) if name in full for n in SIZES[name])


def digits_of(i, lengths):
    digits = []
    for length in reversed(lengths):
        digits.append(lax.rem(i, length))
        i = lax.div(i, length)
    return tuple(digits[::-1])


def one_chip(here, full, axis, value, digits):
    digits, index = list(digits), []
    for name in (Y, X, Z):
        if name in full:
            index += [digits.pop(0) for _ in SIZES[name]]
        else:
            at = value if name == axis else here[name]
            index += [at % 2, at // 2] if name == X else [at]
    return tuple(index)


SCATTER_COPIES = (4, 3, 3)


def scatter_slots(order, rows, cut):
    wide = HALF if cut else 128
    dims = lengths_of(order[1:])
    slots = [
        pltpu.VMEM((2,) + dims + (rows, wide // 2 if cut else wide), BF),
        pltpu.VMEM((2,) + dims + (rows, wide), BF),
    ]
    return slots + [
        pltpu.VMEM((3,) + lengths_of(order[phase + 1 :]) + (rows, wide), BF) for phase in (1, 2)
    ]


def ring_scatter(wire, parts, phases):
    here = wire.here
    sent = []
    for phase in phases:
        ahead, arriving = [], []
        for buffer, prefix, order, cut, slots, _ in parts:
            axis, full = order[phase], order[phase + 1 :]
            row = []
            if phase == 0:
                far = prefix + cube_index(here, full, axis, lax.rem(here[axis] + 2, 4))
                for side, step in enumerate((1, -1)):
                    if cut or side == 0:
                        block = buffer.at[far + ((EVERY, SIDES[side]) if cut else ())]
                        row.append(wire.to(block, slots[0].at[side], moved(here, axis, step)))
                ahead.append(row)
            else:
                for k, step in enumerate((1, -1, 2)):
                    value = lax.rem(here[axis] + step + 4, 4)
                    block = buffer.at[prefix + cube_index(here, full, axis, value)]
                    row.append(
                        wire.to(block, slots[1 + phase].at[k], moved(here, axis, step))
                    )
                arriving.append(row)
            sent += row
        yield
        if phase == 0:
            for (buffer, prefix, order, cut, slots, _), row in zip(parts, ahead):
                axis, full = order[phase], order[phase + 1 :]
                pair = []
                for side, step in enumerate((1, -1)):
                    value = lax.rem(here[axis] + step + 4, 4)
                    if side < len(row):
                        row[side].wait_recv()
                        half = slots[0]
                        columns_ = SIDES[side] if cut else EVERY

                        def add(
                            i, _, buffer=buffer, prefix=prefix, axis=axis, full=full, value=value,
                            half=half, side=side, columns_=columns_,
                        ):
                            digits = digits_of(i, lengths_of(full))
                            at = prefix + one_chip(here, full, axis, value, digits)
                            at += (EVERY, columns_)
                            buffer[at] = bfloat(widen(buffer[at]) + widen(half[(side,) + digits]))
                            return 0

                        lax.fori_loop(0, math.prod(lengths_of(full)), add, 0)
                    block = buffer.at[prefix + cube_index(here, full, axis, value)]
                    pair.append(wire.to(block, slots[1].at[side], moved(here, axis, step)))
                arriving.append(pair)
                sent += pair
            yield
        for (buffer, prefix, order, _, slots, final), row in zip(parts, arriving):
            axis, full = order[phase], order[phase + 1 :]
            come = slots[1 + phase]
            for copy in row:
                copy.wait_recv()

            def total(
                i, _, buffer=buffer, prefix=prefix, axis=axis, full=full, come=come, final=final,
                count=len(row),
            ):
                digits = digits_of(i, lengths_of(full))
                at = prefix + one_chip(here, full, axis, here[axis], digits)
                value = widen(buffer[at])
                for k in range(count):
                    value = value + widen(come[(k,) + digits])
                if phase < 2:
                    buffer[at] = bfloat(value)
                else:
                    final(value)
                return 0

            lax.fori_loop(0, math.prod(lengths_of(full)), total, 0)
    for copy in sent:
        copy.wait_send()


def advance(stages, count=1):
    for _ in range(count):
        next(stages, None)


class Mail:
    def __init__(self, here, send, recv):
        self.here, self.me, self.send, self.recv = here, group_number(here), send, recv
        self.count = 0
        self.sent = []

    def to(self, number, source, target):
        copy = pltpu.make_async_remote_copy(
            src_ref=source,
            dst_ref=target,
            send_sem=self.send.at[self.count],
            recv_sem=self.recv.at[self.me],
            device_id=group_device(self.here, number),
            device_id_type=MESH,
        )
        self.count += 1
        copy.start()
        self.sent.append(copy)

    def finish(self, source, target):
        for k in range(1, CHIPS):
            sender = lax.rem(self.me + k, CHIPS)
            pltpu.make_async_remote_copy(
                src_ref=source,
                dst_ref=target,
                send_sem=self.send.at[0],
                recv_sem=self.recv.at[sender],
                device_id=group_device(self.here, sender),
                device_id_type=MESH,
            ).wait_recv()
        for copy in self.sent:
            copy.wait_send()


BLOCK = 256
SPAN = 1280
STEPS = LENGTH // BLOCK
SLOTS = 4
LAST_START = LENGTH - SPAN


def limits(bounds, first, count):
    places = first + lax.broadcasted_iota(jnp.int32, (1, count), 1)
    low = jnp.maximum(places - (WINDOW // 2 - 1), 0)
    high = jnp.minimum(places + WINDOW // 2, LENGTH)
    for bound in bounds:
        low = jnp.maximum(low, jnp.where(bound <= places, bound, 0))
        high = jnp.minimum(high, jnp.where(bound > places, bound, LENGTH))
    return low, high


def dot(former, latter):
    return jnp.dot(former, latter, preferred_element_type=F32)


def attend_steps(refs, mail, between):
    qkv, mixed_t, mixed, inverse = refs.qkv, refs.mixed_t, refs.mixed_head, refs.inverse
    live, end, bounds = LENGTH - refs.pads[0], 0, []
    for k in range(4):
        end = end + refs.lengths[0, k]
        bounds.append(jnp.minimum(end, live))
    kv, ones_v, chances, stage, local = refs.kv, refs.ones_v, refs.held, refs.mixed_stage, refs.attend_local
    me = mail.me
    kv[...] = jnp.concatenate([qkv[1], qkv[2]], axis=0).T
    ones_v[0:HEAD, :] = jnp.ones((HEAD, LENGTH), BF)
    ones_v[HEAD:, :] = qkv[2]
    kept = []

    def step(i):
        first = pl.multiple_of(i * BLOCK, BLOCK)
        start = pl.multiple_of(jnp.clip(first - 512, 0, LAST_START), BLOCK)
        queries = qkv[0, :, pl.ds(first, BLOCK)]
        padded = jnp.concatenate([queries, jnp.zeros_like(queries)], axis=0)
        scores = dot(kv[pl.ds(start, SPAN), :], padded)
        low, high = limits(bounds, first, BLOCK)
        places = start + lax.broadcasted_iota(jnp.int32, (SPAN, BLOCK), 0)
        scores = jnp.where((places >= low) & (places < high), scores, MASKED)
        highest = jnp.max(scores, axis=0, keepdims=True)
        raised = bfloat(jnp.exp2((scores - highest) * (SCALE * LOG2E)))
        chances[i] = raised
        out = dot(ones_v[:, pl.ds(start, SPAN)], raised)
        back = 1.0 / out[0:1]
        result = out[HEAD:] * back
        mixed[:, pl.ds(first, BLOCK)] = result
        stage[:, pl.ds(first, BLOCK)] = bfloat(result)
        inverse[:, pl.ds(first, BLOCK)] = back

    for slot in range(SLOTS):
        pair = lax.rem(me // 2 + 1 + slot, SLOTS)

        def run(t, _, pair=pair):
            step(pair * 3 + t)
            return 0

        lax.fori_loop(0, 3, run, 0)
        blocks = pl.ds(pair * 3, 3)
        copy = pltpu.make_async_copy(chances.at[blocks], refs.chances.at[blocks], local.at[slot])
        copy.start()
        kept.append(copy)
        if slot < SLOTS - 1:
            for number in (2 * pair, 2 * pair + 1):
                mail.to(number, stage.at[:, chunk_span(number)], mixed_t.at[me])
        else:
            number = me + 1 - 2 * (me % 2)
            mail.to(number, stage.at[:, chunk_span(number)], mixed_t.at[me])
            copy = pltpu.make_async_copy(
                stage.at[:, chunk_span(me)], mixed_t.at[me], local.at[SLOTS]
            )
            copy.start()
            kept.append(copy)
        between(slot)
    refs.keep(mixed, inverse)
    for copy in kept:
        copy.wait()
    mail.finish(stage.at[:, chunk_span(me)], mixed_t.at[me])


MIXED_T = dict(mixed_t=((CHIPS, HEAD, CHIP_ROWS), BF))
ATTEND_SAVED = dict(mixed_head=((HEAD, LENGTH), F32), inverse=((1, LENGTH), F32))
CHANCES = ((STEPS, SPAN, BLOCK), BF)
ATTEND_SCRATCH = dict(
    kv=((LENGTH, 2 * HEAD), BF), ones_v=((2 * HEAD, LENGTH), BF), held=CHANCES,
    mixed_stage=((HEAD, LENGTH), BF),
)
MAIL_SEMS = [pltpu.SemaphoreType.DMA((CHIPS - 1,)), pltpu.SemaphoreType.DMA((CHIPS,))]


def call(
    body, name, number, near, loaded, sources, outputs, saved, far, scratch, semaphores, scalars={}
):
    vmem, hbm = pl.BlockSpec(memory_space=pltpu.VMEM), pl.BlockSpec(memory_space=pltpu.HBM)
    smem = pl.BlockSpec(memory_space=pltpu.SMEM)
    scratch = dict(scratch)
    for key, value in loaded.items():
        scratch[key] = (value.shape, value.dtype)
    scratch.update(saved)
    specs = [*outputs.values(), *saved.values(), *far.values()]

    def size(shape, dtype):
        rows, lanes = (1,) * (2 - len(shape[-2:])) + tuple(shape[-2:])
        rows, lanes = -(-rows // 8) * 8, -(-lanes // 128) * 128
        return math.prod(shape[:-2]) * rows * lanes * jnp.dtype(dtype).itemsize

    held = [(value.shape, value.dtype) for value in near.values()] + list(outputs.values())
    held += [s if isinstance(s, tuple) else (s.shape, s.dtype) for s in scratch.values()]
    limit = sum(size(*spec) for spec in held) + 10 * 2**20

    def kernel(*values):
        values = list(values)

        def take(names):
            return {key: values.pop(0) for key in names}

        refs = types.SimpleNamespace(**take(scalars), **take(near))
        heres = take(loaded)
        for key, ref in take(sources).items():
            setattr(refs, key, ref)
        for key, ref in take(outputs).items():
            setattr(refs, key, ref)
        outs = take(saved)
        for names in (far, scratch):
            for key, ref in take(names).items():
                setattr(refs, key, ref)
        copies = values.pop(0)
        pending = [
            pltpu.make_async_copy(ref, getattr(refs, key), copies.at[k])
            for k, (key, ref) in enumerate(heres.items())
        ]
        for copy in pending:
            copy.start()
        kept = []

        def arrive():
            for copy in pending:
                copy.wait()

        def keep(*arrays):
            for k, (key, out) in enumerate(outs.items()):
                if any(getattr(refs, key) is array for array in arrays):
                    copy = pltpu.make_async_copy(
                        getattr(refs, key), out, copies.at[len(heres) + k]
                    )
                    copy.start()
                    kept.append(copy)

        refs.arrive, refs.keep = arrive, keep
        body(refs, values)
        for copy in kept:
            copy.wait()

    results = pl.pallas_call(
        kernel,
        out_shape=tuple(jax.ShapeDtypeStruct(*spec) for spec in specs),
        in_specs=[smem] * len(scalars)
        + [vmem] * len(near)
        + [hbm] * (len(loaded) + len(sources)),
        out_specs=(vmem,) * len(outputs) + (hbm,) * (len(saved) + len(far)),
        scratch_shapes=[
            pltpu.VMEM(*spec) if isinstance(spec, tuple) else spec for spec in scratch.values()
        ]
        + [dma(max(1, len(loaded) + len(saved)))]
        + list(semaphores),
        name=name,
        compiler_params=pltpu.CompilerParams(
            collective_id=number, has_side_effects=True, vmem_limit_bytes=max(limit, 58 * 2**20)
        ),
    )(*scalars.values(), *near.values(), *loaded.values(), *sources.values())
    return types.SimpleNamespace(**dict(zip([*outputs, *saved, *far], results)))


def dma(count):
    return pltpu.SemaphoreType.DMA((count,))


def attend(lengths, pads, qkv, number):
    def body(refs, semaphores):
        send, recv, refs.attend_local = semaphores
        here = place()
        greet(group(here))
        refs.arrive()
        attend_steps(refs, Mail(here, send, recv), lambda slot: None)

    return call(
        body, "attend", number, dict(qkv=qkv), {}, {}, MIXED_T, ATTEND_SAVED,
        dict(chances=CHANCES), ATTEND_SCRATCH, MAIL_SEMS + [dma(SLOTS + 1)],
        dict(lengths=lengths, pads=pads),
    )


PAD = 2 * BLOCK
PADDED = LENGTH + 2 * PAD


def attend_back_steps(refs, mail_q, mail_kv, between):
    qkv, mixed, inverse, d_mixed = refs.qkv, refs.mixed_head, refs.inverse, refs.d_mixed
    d_q_t, d_kv_t, chances, kv = refs.d_q_t, refs.d_kv_t, refs.held, refs.kv
    rows_q, rows_d, turned_d, shift = refs.rows_q, refs.rows_d, refs.turned_d, refs.shift
    total_q, stage_q, stage_kv = refs.total_q, refs.stage_q, refs.stage_kv
    me = mail_q.me
    kept = []
    for slot in range(SLOTS):
        blocks = pl.ds(slot * 3, 3)
        copy = pltpu.make_async_copy(
            refs.chances.at[blocks], chances.at[blocks], refs.attend_local.at[slot]
        )
        copy.start()
        kept.append(copy)
    kv[...] = jnp.concatenate([qkv[1], qkv[2]], axis=0).T
    scaled = bfloat(widen(d_mixed[...]) * inverse[...])
    inner = jnp.sum(widen(scaled) * mixed[...], axis=0, keepdims=True)
    for edge in (0, PAD + LENGTH):
        shift[:, edge : edge + PAD] = jnp.zeros((1, PAD), F32)
        turned_d[:, edge : edge + PAD] = jnp.zeros((2 * HEAD, PAD), BF)
        rows_q[edge : edge + PAD, :] = jnp.zeros((PAD, 2 * HEAD), BF)
        rows_d[edge : edge + PAD, :] = jnp.zeros((PAD, 2 * HEAD), BF)
    middle = slice(PAD, PAD + LENGTH)
    shift[:, middle] = inner
    turned_d[0:HEAD, middle] = jnp.zeros((HEAD, LENGTH), BF)
    turned_d[HEAD:, middle] = scaled
    both = jnp.concatenate([qkv[0], scaled], axis=0).T
    left = lax.broadcasted_iota(jnp.int32, both.shape, 1) < HEAD
    rows_q[middle, :] = jnp.where(left, both, jnp.zeros_like(both))
    rows_d[middle, :] = jnp.where(left, jnp.zeros_like(both), both)
    total_q[...] = jnp.zeros_like(total_q)
    between(-1)
    for copy in kept:
        copy.wait()

    def step(i):
        first = pl.multiple_of(i * BLOCK, BLOCK)
        keys = pl.ds(first, BLOCK)
        span = pl.ds(first, SPAN)
        tiles = []
        for t in range(5):
            block = jnp.clip(i - 2 + t, 0, STEPS - 1)
            start = jnp.clip(block * BLOCK - 512, 0, LAST_START)
            offset = pl.multiple_of(jnp.clip(first - start, 0, SPAN - BLOCK), BLOCK)
            tiles.append(chances[block, pl.ds(offset, BLOCK), :])
        weights = jnp.concatenate(tiles, axis=1)
        grad_weights = dot(kv[keys, :], turned_d[:, span])
        grad_scores = bfloat(widen(weights) * (grad_weights - shift[:, span]))
        total = dot(weights, rows_d[span, :]) + dot(grad_scores, rows_q[span, :])
        total_q[:, span] += dot(qkv[1, :, keys], grad_scores)
        turned = total.T
        stage_kv[0:HEAD, keys] = bfloat(turned[:HEAD] * SCALE)
        stage_kv[HEAD:, keys] = bfloat(turned[HEAD:])

    def send_queries(number):
        span = pl.ds(pl.multiple_of(number * CHIP_ROWS + PAD, 128), CHIP_ROWS)
        stage_q[number] = bfloat(total_q[:, span] * SCALE)
        mail_q.to(number, stage_q.at[number], d_q_t.at[me])

    near = me + 1 - 2 * (me % 2)
    for slot in range(SLOTS):
        pair = lax.rem(me // 2 + 1 + slot, SLOTS)

        def run(t, _, pair=pair):
            step(pair * 3 + t)
            return 0

        lax.fori_loop(0, 3, run, 0)
        if slot < SLOTS - 1:
            for number in (2 * pair, 2 * pair + 1):
                mail_kv.to(number, stage_kv.at[:, chunk_span(number)], d_kv_t.at[me])
        else:
            mail_kv.to(near, stage_kv.at[:, chunk_span(near)], d_kv_t.at[me])
        if slot == 2:
            complete = lax.rem(me // 2 + 2, SLOTS)
            send_queries(2 * complete)
            send_queries(2 * complete + 1)
        between(slot)
    for rest in (1, 3):
        pair = lax.rem(me // 2 + rest, SLOTS)
        send_queries(2 * pair)
        send_queries(2 * pair + 1)
    send_queries(near)
    span = pl.ds(pl.multiple_of(me * CHIP_ROWS + PAD, 128), CHIP_ROWS)
    d_q_t[me] = bfloat(total_q[:, span] * SCALE)
    d_kv_t[me] = stage_kv[:, chunk_span(me)]
    mail_kv.finish(stage_kv.at[:, chunk_span(me)], d_kv_t.at[me])
    mail_q.finish(stage_q.at[me], d_q_t.at[me])


BACK_SCRATCH = dict(
    held=CHANCES, kv=((LENGTH, 2 * HEAD), BF), rows_q=((PADDED, 2 * HEAD), BF),
    rows_d=((PADDED, 2 * HEAD), BF), turned_d=((2 * HEAD, PADDED), BF), shift=((1, PADDED), F32),
    total_q=((HEAD, PADDED), F32), stage_q=((CHIPS, HEAD, CHIP_ROWS), BF),
    stage_kv=((2 * HEAD, LENGTH), BF),
)
BACK_OUTPUTS = dict(
    d_q_t=((CHIPS, HEAD, CHIP_ROWS), BF), d_kv_t=((CHIPS, 2 * HEAD, CHIP_ROWS), BF)
)


def attend_back(near, loaded, chances, number):
    def body(refs, semaphores):
        send_q, recv_q, send_kv, recv_kv, refs.attend_local = semaphores
        here = place()
        greet(group(here))
        refs.arrive()
        attend_back_steps(
            refs, Mail(here, send_q, recv_q), Mail(here, send_kv, recv_kv), lambda slot: None
        )

    return call(
        body, "attend_back", number, near, loaded, dict(chances=chances), BACK_OUTPUTS, {}, {},
        BACK_SCRATCH, MAIL_SEMS + MAIL_SEMS + [dma(SLOTS)],
    )


REST_ROWS = 48


def rest_planes(here):
    return [
        (part,) + cube_index(here, SCATTER_ORDERS[part][1:], SCATTER_ORDERS[part][0], here[SCATTER_ORDERS[part][0]])
        for part in range(3)
    ]


def attend_back_scatter(near, loaded, chances, g_in, g_back, g_out, number):
    slots = [
        scatter_slots(SCATTER_ORDERS[part], REST_ROWS, True) for part in range(3)
    ]

    def body(refs, semaphores):
        send, recv, local, send_q, recv_q, send_kv, recv_kv, refs.attend_local = semaphores
        here = place()
        wire = Wire(here, send, recv, local)
        core = wire.core
        greet(neighbours(here, (1, -1)) + group(here))
        refs.arrive()
        mine = pl.ds(2 * core, 2)
        own_columns = pl.ds(pl.multiple_of(core * HALF, HALF), HALF)
        your_columns = pl.ds(pl.multiple_of((1 - core) * HALF, HALF), HALF)
        blocks = (EVERY,) * 3
        halves = (
            (refs.g_back, pl.ds(0, 48), refs.rest.at[(1, mine) + blocks]),
            (refs.g_back, pl.ds(48, 16), refs.rest.at[(2, mine) + blocks + (pl.ds(16, 16),)]),
            (refs.g_out, EVERY, refs.rest.at[(2, mine) + blocks + (pl.ds(32, 16),)]),
        )
        copies = [
            wire.swap(ref.at[CUBE_ALL + (rows, your_columns)], target)
            for ref, rows, target in halves
        ]
        copies += [
            wire.fetch(ref.at[CUBE_ALL + (rows, own_columns)], target)
            for ref, rows, target in halves
        ]
        for k in range(4):
            source = refs.g_in.at[CUBE_ALL + (EVERY, pl.ds(k * HALF, HALF))]
            part, low = ((0, 16 * k), (2, 0))[k // 3]
            copies.append(
                wire.fetch(source, refs.rest.at[(part,) + CUBE_ALL + (pl.ds(low, 16),)])
            )
        arrivals = [
            [getattr(refs, "slot_%d_%d" % (part, k)) for k in range(2)] for part in range(3)
        ]
        stages = ring_scatter(
            wire,
            [
                (refs.rest, (part,), SCATTER_ORDERS[part], True, arrivals[part], None)
                for part in range(3)
            ],
            (0,),
        )

        def between(slot):
            if slot == -1:
                for copy in copies:
                    copy.wait()
                advance(stages)
            elif slot == 0:
                advance(stages)

        attend_back_steps(
            refs, Mail(here, send_q, recv_q), Mail(here, send_kv, recv_kv), between
        )
        for _ in stages:
            pass
        kept = [
            wire.fetch(refs.rest.at[at], refs.rest_summed.at[at]) for at in rest_planes(here)
        ]
        for copy in kept:
            copy.wait()

    rest = ((3,) + CUBE + (REST_ROWS, HALF), BF)
    scratch = dict(BACK_SCRATCH, rest=rest)
    for part in range(3):
        for k in range(2):
            scratch["slot_%d_%d" % (part, k)] = slots[part][k]
    copies = 3 * SCATTER_COPIES[0] + 3
    return call(
        body, "attend_back_scatter", number, near, loaded,
        dict(chances=chances, g_in=g_in, g_back=g_back, g_out=g_out),
        BACK_OUTPUTS, {}, dict(rest_summed=rest), scratch,
        [dma(copies), dma(copies), dma(10)] + MAIL_SEMS + MAIL_SEMS + [dma(SLOTS)],
    )


def dot_nt(former, latter):
    return lax.dot_general(former, latter, (((1,), (1,)), ((), ())), preferred_element_type=F32)


QKV, OUT, IN, BACK = range(4)


class Weights:
    def __init__(self, refs, wire, names):
        core = wire.core
        mine = pl.ds(2 * core, 2)
        own = (mine,) + (EVERY,) * 3
        self.refs, self.pending = refs, {}
        for name in names:
            if name == QKV:
                pairs = [(refs.gqkv, refs.w_qkv)]
            elif name == OUT:
                pairs = [
                    (refs.rest_three.at[own + (pl.ds(32, 16),)], refs.w_out.at[core]),
                    (refs.yours_three.at[CUBE_ALL + (pl.ds(16, 16),)], refs.w_out.at[1 - core]),
                ]
            elif name == IN:
                pairs = [
                    (refs.rest_one.at[CUBE_ALL + (pl.ds(16 * k, 16),)], refs.w_in.at[k])
                    for k in range(3)
                ] + [(refs.rest_three.at[CUBE_ALL + (pl.ds(0, 16),)], refs.w_in.at[3])]
            else:
                blocks = (EVERY,) * 4
                low, high = blocks + (pl.ds(0, 48),), blocks + (pl.ds(48, 16),)
                pairs = [
                    (refs.rest_two.at[own], refs.w_back.at[(core,) + low]),
                    (refs.rest_three.at[own + (pl.ds(16, 16),)], refs.w_back.at[(core,) + high]),
                    (refs.yours_two, refs.w_back.at[(1 - core,) + low]),
                    (refs.yours_three.at[CUBE_ALL + (pl.ds(0, 16),)], refs.w_back.at[(1 - core,) + high]),
                ]
            self.pending[name] = [wire.fetch(*pair) for pair in pairs]

    def ready(self, name):
        for copy in self.pending.pop(name, []):
            copy.wait()

    def qkv(self, k):
        self.ready(QKV)
        return self.refs.w_qkv[k].reshape(D, HALF)

    def out(self, half):
        self.ready(OUT)
        return self.refs.w_out[half].reshape(HALF, HALF)

    def into(self, chunk):
        self.ready(IN)
        return self.refs.w_in[chunk].reshape(D, HALF)

    def back(self, half, chunk):
        self.ready(BACK)
        return self.refs.w_back[half, chunk // 2, chunk % 2].reshape(HALF, HALF)


def columns(k):
    return slice(k * HALF, k * HALF + HALF)


def vector(refs, k):
    return refs.vecs[k : k + 1, :]


def half_vector(refs, core, k):
    return refs.vecs[k : k + 1, pl.ds(pl.multiple_of(core * HALF, HALF), HALF)]


B_QUERY, B_VALUE, B_OUT, GAIN_ATTN, SHIFT_ATTN, B_BACK, GAIN_FFN, SHIFT_FFN = range(8)


def normalized(tensor):
    centred = tensor - jnp.mean(tensor, axis=-1, keepdims=True)
    factor = lax.rsqrt(jnp.mean(centred * centred, axis=-1, keepdims=True) + EPSILON)
    return centred * factor, factor


def normalize_back(grad_out, normed, factor, gain):
    grad_normed = grad_out * gain
    grad_input = factor * (
        grad_normed
        - jnp.mean(grad_normed, axis=-1, keepdims=True)
        - normed * jnp.mean(grad_normed * normed, axis=-1, keepdims=True)
    )
    return (
        grad_input,
        jnp.sum(grad_out * normed, axis=0, keepdims=True),
        jnp.sum(grad_out, axis=0, keepdims=True),
    )


def row_sum(tensor):
    return jnp.sum(widen(tensor), axis=0, keepdims=True)


def gelu_pair(v):
    root = math.sqrt(2.0 / math.pi)
    squared = v * v
    bent = jnp.tanh(root * v * (1.0 + 0.044715 * squared))
    half = 0.5 + 0.5 * bent
    slope = half + (0.5 * root) * v * (1.0 - bent * bent) * (1.0 + (3 * 0.044715) * squared)
    return v * half, slope


def summed_over_cores(refs, wire, number, fill):
    send, come, kept = refs.outgoing.at[number], refs.incoming.at[number], refs.kept
    fill(wire.other, send)
    copy = wire.swap(send, come)
    fill(wire.own, kept)
    copy.wait()
    return kept[...] + come[...]


def project_rows(refs, wire, weight, copy, between):
    entry, rows_of, stage = refs.entry, refs.qkv_rows, refs.qkv_stage
    biases = (half_vector(refs, wire.core, B_QUERY), None, half_vector(refs, wire.core, B_VALUE))

    def project(rows, k):
        result = dot(entry[rows, :], weight(k))
        if biases[k] is not None:
            result = result + biases[k]
        rows_of[k, rows, :] = bfloat(result)

    for k in range(3):
        project(wire.own, k)
    copy.wait()
    refs.keep(entry)
    copies = []
    for k in range(3):
        project(wire.other, k)
        stage[k] = rows_of[k].T.reshape(CHIPS, HEAD, CHIP_ROWS)
        copies += wire.spread(stage.at[k], refs.qkv.at[k])
        if k < 2:
            between()
    return copies


def part_project(refs, wire, weights, hidden):
    entry = refs.entry
    entry[wire.own, :] = bfloat(hidden)
    copy = wire.swap(entry.at[wire.own], entry.at[wire.own])
    return project_rows(refs, wire, weights.qkv, copy, lambda: None)


def part_post(refs, wire, weights):
    mixed = refs.mixed
    mixed[...] = refs.mixed_t[...].reshape(HALF, CHIP_ROWS).T
    refs.keep(mixed)

    def leave(rows, target):
        for half in range(2):
            target[:, columns(half)] = dot(mixed[rows, :], weights.out(half))

    branch = summed_over_cores(refs, wire, 0, leave)
    normed, factor = normalized(widen(refs.hidden[...]) + branch + vector(refs, B_OUT))
    refs.normed_one[...] = normed
    refs.factor_one[...] = factor
    refs.keep(refs.normed_one, refs.factor_one)
    first = normed * vector(refs, GAIN_ATTN) + vector(refs, SHIFT_ATTN)
    refs.first[...] = first
    entry_two, active, slope = refs.entry_two, refs.active, refs.slope
    entry_two[wire.own, :] = bfloat(first)
    copy = wire.swap(entry_two.at[wire.own], entry_two.at[wire.own])

    def inner(rows):
        for chunk in range(4):
            start = pl.multiple_of(wire.core * 2048 + chunk * HALF, HALF)
            before = dot(entry_two[rows, :], weights.into(chunk)) + refs.b_in[:, pl.ds(start, HALF)]
            value, steep = gelu_pair(before)
            active[rows, columns(chunk)] = bfloat(value)
            slope[rows, columns(chunk)] = bfloat(steep)

    inner(wire.own)
    copy.wait()
    refs.keep(entry_two)
    inner(wire.other)
    refs.keep(active, slope)

    def leave_two(rows, target):
        for half in range(2):
            total = dot(active[rows, columns(0)], weights.back(half, 0))
            for chunk in range(1, 4):
                total = total + dot(active[rows, columns(chunk)], weights.back(half, chunk))
            target[:, columns(half)] = total

    second = summed_over_cores(refs, wire, 1, leave_two)
    normed, factor = normalized(refs.first[...] + second + vector(refs, B_BACK))
    refs.normed_two[...] = normed
    refs.factor_two[...] = factor
    refs.keep(refs.normed_two, refs.factor_two)
    return normed * vector(refs, GAIN_FFN) + vector(refs, SHIFT_FFN)


def part_back_dense(refs, wire, weights, grad_out):
    d_branch, d_before, d_attn = refs.d_branch, refs.d_before, refs.d_attn
    sums = refs.sums
    d_second, g_gain, g_shift = normalize_back(
        grad_out, refs.normed_two[...], refs.factor_two[...], vector(refs, GAIN_FFN)
    )
    refs.d_second[...] = d_second
    d_branch[wire.own, :] = bfloat(d_second)
    copy = wire.swap(d_branch.at[wire.own], d_branch.at[wire.own])
    sums[GAIN_FFN : GAIN_FFN + 1, :] = g_gain
    sums[SHIFT_FFN : SHIFT_FFN + 1, :] = g_shift
    sums[B_BACK : B_BACK + 1, :] = row_sum(d_branch[wire.own, :])

    def inner(rows):
        for chunk in range(4):
            d_active = dot_nt(d_branch[rows, columns(0)], weights.back(0, chunk)) + dot_nt(
                d_branch[rows, columns(1)], weights.back(1, chunk)
            )
            d_before[rows, columns(chunk)] = bfloat(
                d_active * widen(refs.slope[rows, columns(chunk)])
            )

    inner(wire.own)
    copy.wait()
    refs.keep(d_branch)
    inner(wire.other)
    refs.keep(d_before)
    for chunk in range(4):
        start = pl.multiple_of(wire.core * 2048 + chunk * HALF, HALF)
        refs.sums_in[:, pl.ds(start, HALF)] = row_sum(d_before[:, columns(chunk)])

    def leave(rows, target):
        total = dot_nt(d_before[rows, columns(0)], weights.into(0))
        for chunk in range(1, 4):
            total = total + dot_nt(d_before[rows, columns(chunk)], weights.into(chunk))
        target[...] = total

    d_first = refs.d_second[...] + summed_over_cores(refs, wire, 2, leave)
    d_inner, g_gain, g_shift = normalize_back(
        d_first, refs.normed_one[...], refs.factor_one[...], vector(refs, GAIN_ATTN)
    )
    refs.d_inner_out[...] = d_inner
    refs.keep(refs.d_inner_out)
    d_attn[wire.own, :] = bfloat(d_inner)
    copy = wire.swap(d_attn.at[wire.own], d_attn.at[wire.own])
    sums[GAIN_ATTN : GAIN_ATTN + 1, :] = g_gain
    sums[SHIFT_ATTN : SHIFT_ATTN + 1, :] = g_shift
    sums[B_OUT : B_OUT + 1, :] = row_sum(d_attn[wire.own, :])
    rows_of, stage = refs.d_mixed_rows, refs.d_mixed_stage

    def enter(rows):
        rows_of[rows, :] = bfloat(
            dot_nt(d_attn[rows, columns(0)], weights.out(0))
            + dot_nt(d_attn[rows, columns(1)], weights.out(1))
        )

    enter(wire.own)
    copy.wait()
    refs.keep(d_attn, refs.sums, refs.sums_in)
    enter(wire.other)
    stage[...] = rows_of[...].T.reshape(CHIPS, HEAD, CHIP_ROWS)
    return wire.spread(stage, refs.d_mixed)


def turn_gradients(refs):
    rows_of = refs.d_qkv
    rows_of[0] = refs.d_q_t[...].reshape(HALF, CHIP_ROWS).T
    rows_of[1] = refs.d_kv_t[:, :HEAD, :].reshape(HALF, CHIP_ROWS).T
    rows_of[2] = refs.d_kv_t[:, HEAD:, :].reshape(HALF, CHIP_ROWS).T


def add_half(refs, wire, k, value):
    half = pl.ds(pl.multiple_of(wire.core * HALF, HALF), HALF)
    refs.sums[k : k + 1, half] = refs.sums[k : k + 1, half] + value


def part_back_project(refs, wire, weights):
    rows_of = refs.d_qkv

    def leave(rows, target):
        total = dot_nt(rows_of[0, rows, :], weights.qkv(0))
        for k in range(1, 3):
            total = total + dot_nt(rows_of[k, rows, :], weights.qkv(k))
        target[...] = total

    return refs.d_inner[...] + summed_over_cores(refs, wire, 3, leave)


ROW_F32 = ((ROWS, D), F32)
COLUMN_F32 = ((ROWS, 1), F32)
CHIP_BF = ((CHIP_ROWS, D), BF)
WIDE_BF = ((CHIP_ROWS, 2048), BF)
HEADS_BF = ((CHIP_ROWS, HALF), BF)
STAGE = (CHIPS, HEAD, CHIP_ROWS)
PROJECT, POST, BACK_DENSE, BACK_PROJECT = range(4)
PARTS = (
    (
        (QKV,),
        dict(entry=CHIP_BF),
        dict(qkv=((3, HEAD, LENGTH), BF)),
        dict(qkv_rows=((3, CHIP_ROWS, HALF), BF), qkv_stage=((3,) + STAGE, BF)),
        1 + 3 * 7,
        3,
    ),
    (
        (OUT, IN, BACK),
        dict(
            mixed=HEADS_BF, normed_one=ROW_F32, factor_one=COLUMN_F32, entry_two=CHIP_BF,
            active=WIDE_BF, slope=WIDE_BF, normed_two=ROW_F32, factor_two=COLUMN_F32,
        ),
        {},
        dict(first=ROW_F32),
        4,
        0,
    ),
    (
        (BACK, IN, OUT),
        dict(
            d_branch=CHIP_BF, d_before=WIDE_BF, d_attn=CHIP_BF, d_inner_out=ROW_F32,
            sums=((8, D), F32), sums_in=((1, FF), F32),
        ),
        dict(d_mixed=((HEAD, LENGTH), BF)),
        dict(d_second=ROW_F32, d_mixed_rows=HEADS_BF, d_mixed_stage=(STAGE, BF)),
        3 + 7,
        1,
    ),
    (
        (QKV,),
        dict(d_qkv=((3, CHIP_ROWS, HALF), BF)),
        {},
        {},
        1,
        0,
    ),
)
WEIGHT_SHAPES = (
    dict(w_qkv=((3,) + CUBE + (16, HALF), BF)),
    dict(w_out=((2, 2, 2, 2, 4, 16, HALF), BF)),
    dict(w_in=((4,) + CUBE + (16, HALF), BF)),
    dict(w_back=((2, 2, 2, 2, 4, 64, HALF), BF)),
)


WEIGHT_COPIES = (1, 2, 4, 4)


def dense(parts, number, gathered, near, loaded, extra, dropped=()):
    outputs, saved, weight_names = {}, dict(extra), []
    scratch = dict(outgoing=((4, ROWS, D), F32), incoming=((4, ROWS, D), F32), kept=ROW_F32)
    copies = locals_ = 0
    for part in parts:
        its_weights, its_saved, its_outputs, its_scratch, its_copies, its_locals = PARTS[part]
        weight_names += [name for name in its_weights if name not in weight_names]
        outputs.update(its_outputs)
        saved.update(its_saved)
        scratch.update(its_scratch)
        copies += its_copies
        locals_ += its_locals
    for name in dropped:
        scratch[name] = saved.pop(name)
    for name in weight_names:
        scratch.update(WEIGHT_SHAPES[name])
        locals_ += WEIGHT_COPIES[name]

    def body(refs, semaphores):
        here = place()
        wire = Wire(here, *semaphores)
        weights = Weights(refs, wire, weight_names)
        if BACK_DENSE in parts:
            refs.sums[...] = jnp.zeros((8, D), F32)
            refs.sums_in[...] = jnp.zeros((1, FF), F32)
        greet([partner(here)] + group(here))
        refs.arrive()
        pending = []
        value = None
        for part in parts:
            if part == PROJECT:
                pending += part_project(refs, wire, weights, value)
            elif part == POST:
                value = part_post(refs, wire, weights)
                refs.result[...] = value.astype(refs.result.dtype)
                refs.keep(refs.result)
            elif part == BACK_DENSE:
                if POST in parts:
                    value = widen(refs.cotangent[...])
                pending += part_back_dense(refs, wire, weights, value)
            else:
                turn_gradients(refs)
                refs.keep(refs.d_qkv)
                add_half(refs, wire, B_QUERY, row_sum(refs.d_qkv[0]))
                add_half(refs, wire, B_VALUE, row_sum(refs.d_qkv[2]))
                value = part_back_project(refs, wire, weights)
        for copy in pending:
            copy.wait()

    return call(
        body, "dense_%d" % number, number, near,
        dict(loaded, vecs=gathered.vecs, b_in=gathered.b_in),
        dict(
            gqkv=gathered.gqkv, rest_one=gathered.rest_one, rest_two=gathered.rest_two,
            rest_three=gathered.rest_three, yours_two=gathered.yours_two,
            yours_three=gathered.yours_three,
        ),
        outputs, saved, {}, scratch, [dma(copies), dma(copies), dma(locals_)],
    )


def opening(lengths, pads, shards, vectors, tokens, number):
    def body(refs, semaphores):
        send, recv, local, mail_send, mail_recv, refs.attend_local = semaphores
        here = place()
        wire = Wire(here, send, recv, local)
        core = wire.core
        greet(neighbours(here, (1, -1, 2)) + group(here))
        refs.arrive()
        tok = lax.axis_index("tok")
        lanes = lax.broadcasted_iota(jnp.int32, (1, 128), 1)
        line = refs.vectors[...]
        rows = []
        for k in range(8):
            turned = pltpu.roll(line, lax.rem(tok * 8 - 8 * k + 128, 128), 1)
            rows.append(jnp.where(lanes // 8 == tok, turned, 0.0))
        turned = pltpu.roll(line, lax.rem(lax.rem(tok, 4) * 32 + 64, 128), 1)
        turned = jnp.where(lanes // 32 == lax.rem(tok, 4), turned, 0.0)
        for k in range(4):
            rows.append(jnp.where(lax.div(tok, 4) == k, turned, jnp.zeros_like(turned)))
        rows.append(jnp.zeros((4, 128), F32))
        refs.small[...] = bfloat(jnp.concatenate(rows, axis=0))
        thin = [widen(ref[...]) for ref in (refs.w_query, refs.w_key, refs.w_value, refs.w_out)]
        wide, back = widen(refs.w_in[...]), refs.w_back[...]
        for half in range(2):
            span = columns(half)
            spread = [wide[:, columns(4 * half + k)] for k in range(4)]
            pieces = [thin[k][:, span] for k in range(3)] + spread[:3]
            refs.pack[half, 0:48, :] = bfloat(jnp.concatenate(pieces, axis=0))
            refs.pack[half, 48:80, :] = back[:, span]
            refs.pack[half, 80:96, :] = bfloat(
                jnp.concatenate([spread[3], thin[3][:, span]], axis=0)
            )
        swaps = [
            wire.swap(refs.pack.at[1 - core], refs.theirs),
            wire.swap(refs.small, refs.small_theirs),
        ]
        entry = refs.entry
        entry[wire.own, :] = refs.tokens[...]
        entry_copy = wire.swap(refs.tokens, entry.at[wire.own])
        for copy in swaps:
            copy.wait()

        def build(low, high):
            low, high = widen(low), widen(high)

            def both(row):
                return bfloat(jnp.concatenate([low[row : row + 8], high[row : row + 8]], axis=0))

            for k in range(3):
                refs.own_qkv[k] = both(8 * k)
                refs.own_rest[0, 16 * k : 16 * k + 16, :] = both(24 + 8 * k)
            back = bfloat(jnp.concatenate([low[48:80], high[48:80]], axis=0))
            refs.own_rest[1] = back[:48]
            refs.own_rest[2, 0:16, :] = both(80)
            refs.own_rest[2, 16:32, :] = back[48:]
            refs.own_rest[2, 32:48, :] = both(88)

        @pl.when(core == 0)
        def _():
            build(refs.pack[0], refs.theirs[...])

        @pl.when(core == 1)
        def _():
            build(refs.theirs[...], refs.pack[1])

        refs.own_small[...] = refs.small[...] + refs.small_theirs[...]

        def nothing(value):
            pass

        parts = [
            (refs.w_qkv, (k,), GATHER_ORDERS[k], refs.own_qkv.at[k], True, nothing)
            for k in range(3)
        ]
        parts.append((refs.all_small, (), GATHER_ORDERS[3], refs.own_small, False, nothing))
        first_stages = ring_gather(wire, parts)
        yours = pl.ds(2 * (1 - core), 2)
        passed = []

        def pass_two(value):
            passed.append(
                wire.swap(
                    refs.rest_two.at[yours, :, :, value], refs.yours_two.at[:, :, :, value]
                )
            )

        def pass_three(value):
            passed.append(
                wire.swap(
                    refs.rest_three.at[yours, value % 2, value // 2, :, pl.ds(16, 32)],
                    refs.yours_three.at[:, value % 2, value // 2],
                )
            )

        stages = ring_gather(
            wire,
            [
                (ref, (), GATHER_ORDERS[part], refs.own_rest.at[part], True, complete)
                for part, (ref, complete) in enumerate(
                    (
                        (refs.rest_one, nothing),
                        (refs.rest_two, pass_two),
                        (refs.rest_three, pass_three),
                    )
                )
            ],
        )
        for _ in range(2):
            advance(first_stages)
            advance(stages)
        for _ in first_stages:
            pass
        kept = wire.fetch(refs.w_qkv, refs.gqkv)
        for s in range(8):
            tile = jnp.zeros((16, 128), F32)
            for x_hi in range(2):
                for z in range(4):
                    tile = tile + widen(refs.all_small[s // 2, s % 2, x_hi, z])
            refs.vecs[:, 128 * s : 128 * s + 128] = tile[:8]
            for j in range(4):
                low = HALF * s + 128 * j
                refs.b_in[:, low : low + 128] = tile[8 + j : 9 + j]
        refs.keep(refs.vecs, refs.b_in)
        pending = project_rows(
            refs, wire, lambda k: refs.w_qkv[k].reshape(D, HALF), entry_copy, lambda: None
        )
        for copy in pending:
            copy.wait()
        refs.keep(refs.qkv)
        advance(stages)

        def between(slot):
            if slot == 2:
                advance(stages)

        attend_steps(refs, Mail(here, mail_send, mail_recv), between)
        for _ in stages:
            pass
        for copy in passed:
            copy.wait()
        kept.wait()

    scratch = dict(
        ATTEND_SCRATCH, pack=((2, 96, HALF), BF), small=((16, 128), BF), theirs=((96, HALF), BF),
        small_theirs=((16, 128), BF),
        own_qkv=((3, 16, HALF), BF), own_rest=((3, REST_ROWS, HALF), BF), own_small=((16, 128), BF),
        w_qkv=((3,) + CUBE + (16, HALF), BF), all_small=(CUBE + (16, 128), BF),
        qkv_rows=((3, CHIP_ROWS, HALF), BF), qkv_stage=((3,) + STAGE, BF),
    )
    rest = (CUBE + (REST_ROWS, HALF), BF)
    copies = 3 + 7 * GATHER_COPIES + 8 + 21
    return call(
        body, "opening", number, dict(vectors=vectors), dict(shards, tokens=tokens), {}, MIXED_T,
        dict(
            ATTEND_SAVED, entry=CHIP_BF, qkv=((3, HEAD, LENGTH), BF), vecs=((8, D), F32),
            b_in=((1, FF), F32),
        ),
        dict(
            chances=CHANCES, gqkv=((3,) + CUBE + (16, HALF), BF), rest_one=rest, rest_two=rest,
            rest_three=rest, yours_two=((2, 2, 2, 4, 48, HALF), BF),
            yours_three=((2, 2, 2, 4, 32, HALF), BF),
        ),
        scratch, [dma(copies), dma(copies), dma(11)] + MAIL_SEMS + [dma(SLOTS + 1)],
        dict(lengths=lengths, pads=pads),
    )


def closing(near, loaded, gqkv, rest_summed, number):
    def body(refs, semaphores):
        here = place()
        wire = Wire(here, *semaphores)
        core = wire.core
        planes = [
            wire.fetch(refs.rest_summed.at[at], refs.rest.at[at]) for at in rest_planes(here)
        ]
        weights = Weights(refs, wire, (QKV,))
        rest_slots = [
            [None] * 2 + [getattr(refs, "late_%d_%d" % (part, k)) for k in (2, 3)]
            for part in range(3)
        ]

        def keep_rest(part):
            def store(value):
                refs.sums_rest[part] = value

            return store

        rest_stages = ring_scatter(
            wire,
            [
                (refs.rest, (part,), SCATTER_ORDERS[part], True, rest_slots[part], keep_rest(part))
                for part in range(3)
            ],
            (1, 2),
        )
        greet(neighbours(here, (1, -1, 2)))
        refs.arrive()
        for copy in planes:
            copy.wait()
        advance(rest_stages)
        turn_gradients(refs)
        refs.sums[...] = refs.sums_three[...] + refs.sums_four[...]
        refs.sums_in[...] = refs.in_three[...] + refs.in_four[...]
        add_half(refs, wire, B_QUERY, row_sum(refs.d_qkv[0]))
        add_half(refs, wire, B_VALUE, row_sum(refs.d_qkv[2]))
        swaps = [wire.swap(refs.sums, refs.sums_come), wire.swap(refs.sums_in, refs.in_come)]
        for k in range(3):
            total = dot(refs.entry[...].T, refs.d_qkv[k])
            total = total + dot(refs.entry_later[...].T, refs.d_qkv_later[k])
            refs.gradients[k] = bfloat(total).reshape(CUBE + (16, HALF))
            if k == 1:
                advance(rest_stages)
        for copy in swaps:
            copy.wait()
        both = refs.sums[...] + refs.sums_come[...]
        both_in = refs.sums_in[...] + refs.in_come[...]
        for s in range(8):
            pieces = [both[:, 128 * s : 128 * s + 128]]
            for j in range(4):
                low = HALF * s + 128 * j
                pieces.append(both_in[:, low : low + 128])
            pieces.append(jnp.zeros((4, 128), F32))
            tile = bfloat(jnp.concatenate(pieces, axis=0))
            for x_hi in range(2):
                for z in range(4):
                    refs.small_sums[s // 2, s % 2, x_hi, z] = tile

        def keep(part):
            def store(value):
                if part == 3:
                    refs.tiny[...] = value
                else:
                    refs.final[part] = value

            return store

        arrivals = [
            [getattr(refs, "slot_%d_%d" % (part, k)) for k in range(4)] for part in range(4)
        ]
        parts = [
            (refs.gradients, (part,), SCATTER_ORDERS[part], True, arrivals[part], keep(part))
            for part in range(3)
        ]
        parts.append((refs.small_sums, (), SCATTER_ORDERS[3], False, arrivals[3], keep(3)))
        stages = ring_scatter(wire, parts, (0, 1, 2))
        advance(stages)
        for _ in rest_stages:
            pass
        advance(stages)
        refs.d_tokens[...] = bfloat(part_back_project(refs, wire, weights))
        for _ in stages:
            pass

        def finish(own):
            rest = refs.sums_rest
            rows = [refs.final[k, 8 * own : 8 * own + 8, :] for k in range(3)]
            rows.append(rest[2, 32 + 8 * own : 40 + 8 * own, :])
            for k in range(3):
                rows.append(rest[0, 16 * k + 8 * own : 16 * k + 8 * own + 8, :])
            rows.append(rest[2, 8 * own : 8 * own + 8, :])
            if own == 0:
                rows.append(rest[1, 0:32, :])
            else:
                rows += [rest[1, 32:48, :], rest[2, 16:32, :]]
            return jnp.concatenate(rows, axis=0)

        @pl.when(core == 0)
        def _():
            refs.leaving[...] = finish(1)
            refs.landed[0] = finish(0)

        @pl.when(core == 1)
        def _():
            refs.leaving[...] = finish(0)
            refs.landed[1] = finish(1)

        wire.swap(refs.leaving, refs.landed.at[core]).wait()
    few = ((8, D), F32)
    scratch = dict(
        outgoing=((4, ROWS, D), F32), incoming=((4, ROWS, D), F32), kept=ROW_F32,
        d_qkv=((3, CHIP_ROWS, HALF), BF), sums=few, sums_in=((1, FF), F32), sums_come=few,
        in_come=((1, FF), F32), gradients=((3,) + CUBE + (16, HALF), BF),
        small_sums=(CUBE + (16, 128), BF), final=((3, 16, HALF), F32),
        leaving=((96, HALF), F32), sums_rest=((3, REST_ROWS, HALF), F32),
        rest=((3,) + CUBE + (REST_ROWS, HALF), BF),
    )
    scratch.update(WEIGHT_SHAPES[QKV])
    for part in range(4):
        slots = scatter_slots(SCATTER_ORDERS[part], 16, part < 3)
        for k in range(4):
            scratch["slot_%d_%d" % (part, k)] = slots[k]
        if part < 3:
            slots = scatter_slots(SCATTER_ORDERS[part], REST_ROWS, True)
            for k in (2, 3):
                scratch["late_%d_%d" % (part, k)] = slots[k]
    copies = 4 * sum(SCATTER_COPIES) + 3 * sum(SCATTER_COPIES[1:]) + 4
    return call(
        body, "closing", number, near, loaded, dict(gqkv=gqkv, rest_summed=rest_summed),
        dict(
            d_tokens=((ROWS, D), BF), landed=((2, 96, HALF), F32), tiny=((16, 128), F32),
        ),
        {}, {}, scratch, [dma(copies), dma(copies), dma(4)],
    )


def unpack_kernel(
    result, d_tokens, landed, tiny, o_result, o_tokens, o_query, o_key, o_value, o_out, o_in, o_back,
    o_vectors,
):
    o_result[...] = result[...]
    o_tokens[...] = d_tokens[...]
    for column in (0, 1):
        span = columns(column)
        for piece, ref in enumerate((o_query, o_key, o_value, o_out)):
            ref[:, span] = landed[column, 8 * piece : 8 * piece + 8, :]
        for chunk in range(4):
            o_in[:, columns(4 * column + chunk)] = landed[
                column, 32 + 8 * chunk : 40 + 8 * chunk, :
            ]
        o_back[:, span] = landed[column, 64:96, :]
    tok = lax.axis_index("tok")
    o_vectors[0:8, :] = pltpu.roll(tiny[0:8, :], lax.rem(128 - tok * 8, 128), 1)
    wide = tiny[8:9, :]
    for k in range(1, 4):
        wide = jnp.where(lax.div(tok, 4) == k, tiny[8 + k : 9 + k, :], wide)
    wide = pltpu.roll(wide, lax.rem(128 - lax.rem(tok, 4) * 32, 128), 1)
    o_vectors[8:16, :] = jnp.broadcast_to(wide, (8, 128))


def unpack(result, d_tokens, landed, tiny):
    vmem = pl.BlockSpec(memory_space=pltpu.VMEM)
    few = ((8, D), F32)
    specs = (
        ((ROWS, D), BF), ((ROWS, D), BF), few, few, few, few, ((8, FF), F32), ((32, D), F32),
        ((16, 128), F32),
    )
    return pl.pallas_call(
        unpack_kernel,
        out_shape=tuple(jax.ShapeDtypeStruct(*spec) for spec in specs),
        in_specs=[vmem] * 4,
        out_specs=(vmem,) * len(specs),
        name="unpack",
        compiler_params=pltpu.CompilerParams(vmem_limit_bytes=16 * 2**20),
    )(result, d_tokens, landed, tiny)


def on_device(
    tokens, cotangent, doc_lengths, pad_counts, w_query, b_query, w_key, w_value, b_value, w_out,
    b_out, gain_attn, shift_attn, w_in, b_in, w_back, b_back, gain_ffn, shift_ffn,
):
    vectors = jnp.concatenate(
        [
            b_query, b_value, b_out, gain_attn, shift_attn, b_back, gain_ffn, shift_ffn, b_in,
            jnp.zeros((32,), BF),
        ]
    )
    one = opening(
        doc_lengths, pad_counts,
        dict(
            w_query=w_query, w_key=w_key, w_value=w_value, w_out=w_out, w_in=w_in, w_back=w_back
        ),
        widen(vectors)[None], tokens, 0,
    )
    two = dense(
        (POST, PROJECT), 2, one, dict(mixed_t=one.mixed_t), dict(hidden=tokens),
        dict(result=ROW_F32),
    )
    two_attend = attend(doc_lengths, pad_counts, two.qkv, 3)
    three = dense(
        (POST, BACK_DENSE), 4, one, dict(mixed_t=two_attend.mixed_t),
        dict(hidden=two.result, cotangent=cotangent), dict(result=((ROWS, D), BF)),
        ("normed_one", "factor_one", "normed_two", "factor_two", "slope"),
    )
    back_two = attend_back(
        dict(d_mixed=three.d_mixed),
        dict(qkv=two.qkv, mixed_head=two_attend.mixed_head, inverse=two_attend.inverse),
        two_attend.chances, 5,
    )
    four = dense(
        (BACK_PROJECT, BACK_DENSE), 6, one,
        dict(d_q_t=back_two.d_q_t, d_kv_t=back_two.d_kv_t),
        dict(
            d_inner=three.d_inner_out, normed_one=two.normed_one, factor_one=two.factor_one,
            normed_two=two.normed_two, factor_two=two.factor_two, slope=two.slope,
        ),
        {},
    )

    def gradient(one_former, one_latter, two_former, two_latter):
        former = jnp.concatenate([one_former, two_former], axis=0)
        latter = jnp.concatenate([one_latter, two_latter], axis=0)
        return bfloat(
            lax.dot_general(
                former, latter, (((0,), (0,)), ((), ())), preferred_element_type=F32
            )
        )

    half_cube = (2, 2, 2, 4)
    back_one = attend_back_scatter(
        dict(d_mixed=four.d_mixed),
        dict(qkv=one.qkv, mixed_head=one.mixed_head, inverse=one.inverse),
        one.chances,
        gradient(two.entry_two, four.d_before, three.entry_two, three.d_before).reshape(
            CUBE + (16, 2048)
        ),
        gradient(two.active, four.d_branch, three.active, three.d_branch).reshape(
            half_cube + (64, D)
        ),
        gradient(two.mixed, four.d_attn, three.mixed, three.d_attn).reshape(half_cube + (16, D)),
        7,
    )
    last = closing(
        dict(d_q_t=back_one.d_q_t, d_kv_t=back_one.d_kv_t),
        dict(
            d_inner=four.d_inner_out,
            entry=one.entry, entry_later=two.entry, d_qkv_later=four.d_qkv,
            sums_three=three.sums, sums_four=four.sums,
            in_three=three.sums_in, in_four=four.sums_in,
        ),
        one.gqkv, back_one.rest_summed, 8,
    )
    result, d_tokens, g_query, g_key, g_value, g_out, g_in, g_back, lines = unpack(
        three.result, last.d_tokens, last.landed, last.tiny
    )
    (
        g_b_query, g_b_value, g_b_out, g_gain_attn, g_shift_attn, g_b_back, g_gain_ffn, g_shift_ffn,
    ) = [lines[k, :8] for k in range(8)]
    return (
        result, d_tokens, g_query, g_b_query, g_key, g_value, g_b_value, g_out, g_b_out, g_gain_attn,
        g_shift_attn, g_in, lines[8, :32], g_back, g_b_back, g_gain_ffn, g_shift_ffn,
    )


def solution(mesh):
    both = ("seq", "tok")
    rows, vector = P(both, None), P(both)
    ins = (
        rows, rows, P("seq", None), P("seq"), rows, vector, rows, rows, vector, rows, vector, vector,
        vector, rows, vector, rows, vector, vector, vector,
    )
    outs = (
        rows, rows, rows, vector, rows, rows, vector, rows, vector, vector, vector, rows, vector,
        rows, vector, vector, vector,
    )
    return jax.shard_map(on_device, mesh=mesh, in_specs=ins, out_specs=outs, check_vma=False)
```

time: 5440 us -> 372 us (0.07)
  waiting for transfers between devices: 4800 us -> 0 us
  Pallas kernels: 0 us -> 346 us
  matrix products: 229 us -> 13.7 us
  blocking collectives: 140 us -> 0 us
  starting transfers between devices: 82.7 us -> 0 us
  local copies, waits for them, and re-layouts: 86.5 us -> 4.67 us
  other arithmetic: 71.5 us -> 0.52 us
    reduce_scatter x6 -> x0, waiting for transfers between devices: 3650 us -> none  [spread_layer(): lax.psum_scatter(gradients, ('seq', 'tok'), scatter_dimension=0, tiled=True)]
    all_gather x6 -> x0, waiting for transfers between devices: 1050 us -> none  [the longest x1 202 us: on_device(): lax.all_gather(w_query, ('seq', 'tok'), axis=0, tiled=True)]
    pallas_call x0 -> x9, Pallas kernels: none -> 346 us  [the longest x8 345 us: call(): pl.pallas_call(kernel, out_shape=tuple((jax.ShapeDtypeStruct(*spec) for s...]
    dot_general x48 -> x3, matrix products: 229 us -> 13.7 us  [gradient(): lax.dot_general(former, latter, (((0,), (0,)), ((), ())), preferred_eleme...]
    unnamed x2 -> x0, blocking collectives: 140 us -> none
    ppermute x24 -> x0, waiting for transfers between devices: 103 us -> none  [passed_along(): lax.ppermute(value, axis, [(source, source + steps) for source in range(i...]
    ppermute x24 -> x0, starting transfers between devices: 81.7 us -> none  [passed_along(): lax.ppermute(value, axis, [(source, source + steps) for source in range(i...]
  transfers between devices with their start and end apart: 36 -> 0, of which waited for: 24 -> 0; matrix products, arithmetic and copies ran while one was open for 4% -> 0% of each run, Pallas kernels for 0% -> 0%
where the time goes in v2:
time: 372 us; the launch traced here: 366 us
  Pallas kernels  346 us (93%)
  matrix products  13.7 us (4%)
  local copies, waits for them, and re-layouts  4.67 us (1%)
    pallas_call x8, Pallas kernels, call(): pl.pallas_call(kernel, out_shape=tuple((jax.ShapeDtypeStruct(*spec) for s...  345 us
    dot_general x3, matrix products, gradient(): lax.dot_general(former, latter, (((0,), (0,)), ((), ())), preferred_eleme...  13.7 us

profile of v2, /device:TPU:1, one launch (start us, length us, event | category | flops | bytes accessed | tf_op | source)
XLA Modules:
  0.0 366.5 jit_solution(5677795216938892774)
XLA Ops:
  1.3 0.9 concatenate.55
  2.2 0.5 convert_element_type.19.values_2_
  2.7 93.0 %opening.1 = (bf16[8,64,384]{2,1,0:T(8,128)(2,1)}, f32[64,3072]{1,0:T(8,128)}, f32[1,3072]{1,0:T(1,128)}, bf16[384,1024]{1,0:T(8,128)(2,1)}, bf16[3,64,3072]{2,1...) custom-call(s32[1,4]{1,0:T(1,128)} %values_0_.3, ...), custom_call_target="tpu_custom_call" | custom-call | tf_op jit(solution)/shard_map/opening/pallas_call | solution.py:512
  95.7 33.6 %dense_2.1 = (bf16[3,64,3072]{2,1,0:T(8,128)(2,1)}, f32[192,1024]{1,0:T(8,128)}, bf16[384,512]{1,0:T(8,128)(2,1)}, f32[192,1024]{1,0:T(8,128)}, f32[192,1]{1,0:T...) custom-call(bf16[8,64,384]{2,1,0:T(8,128)(2,1)} %get-tuple-element.8, ...), custom_call_target="tpu_custom_call" | custom-call | tf_op jit(solution)/shard_map/dense_2/pallas_call | solution.py:512
  129.4 21.2 %attend.1 = (bf16[8,64,384]{2,1,0:T(8,128)(2,1)}, f32[64,3072]{1,0:T(8,128)}, f32[1,3072]{1,0:T(1,128)}, bf16[12,1280,256]{2,1,0:T(8,128)(2,1)}) custom-call(s32[1,4]{1,0:T(1,128)} %values_0_.3, s32[1]{0:T(128)S(6)} %copy.36.values_1_, bf16[3,64,3072]{2,1,0:T(8,128)(2,1)} %get-tuple-element.91.values_2_.values_1_), custom_call_target="tpu_custom_call" | custom-call | tf_op jit(solution)/shard_map/attend/pallas_call | solution.py:512
  150.6 33.4 %dense_4.1 = (bf16[64,3072]{1,0:T(8,128)(2,1)}, bf16[192,1024]{1,0:T(8,128)(2,1)}, bf16[384,512]{1,0:T(8,128)(2,1)}, bf16[384,1024]{1,0:T(8,128)(2,1)}, bf16[384...) custom-call(bf16[8,64,384]{2,1,0:T(8,128)(2,1)} %get-tuple-element.9, ...), custom_call_target="tpu_custom_call" | custom-call | tf_op jit(solution)/shard_map/dense_4/pallas_call | solution.py:512
  183.9 28.9 %attend_back.1 = (bf16[8,64,384]{2,1,0:T(8,128)(2,1)}, bf16[8,128,384]{2,1,0:T(8,128)(2,1)}) custom-call(bf16[64,3072]{1,0:T(8,128)(2,1)} %get-tuple-element.95.values_0_, bf16[3,64,3072]{2,1,0:T(8,128)(2,1)} %get-tuple-element.91.values_2_.values_1_, f32[64,3072]{1,0:T(8,128)} %get-tuple-element.96.values_2_, f32[1,3072]{1,0:T(1,128)} %get-tuple-element.97.values_3_, ...), custom_call_target="tpu_custom_call" | custom-call | tf_op jit(solution)/shard_map/attend_back/pallas_call | solution.py:512
  212.8 0.0 copy-start.11
  212.9 0.0 copy-start.13
  212.9 0.0 copy-start.14
  212.9 31.5 %dense_6.1 = (bf16[64,3072]{1,0:T(8,128)(2,1)}, bf16[3,384,512]{2,1,0:T(8,128)(2,1)}, bf16[384,1024]{1,0:T(8,128)(2,1)}, bf16[384,2048]{1,0:T(8,128)(2,1)}, bf16...) custom-call(bf16[8,64,384]{2,1,0:T(8,128)(2,1)} %get-tuple-element.99.values_0_, ...), custom_call_target="tpu_custom_call" | custom-call | tf_op jit(solution)/shard_map/dense_6/pallas_call | solution.py:512
  244.4 0.0 copy-done.11
  244.4 0.0 copy-done.13
  244.4 0.0 copy-done.14
  244.4 0.0 copy-start.4
  244.4 0.0 copy-start.6
  244.5 0.0 copy-start.10
  244.5 0.0 copy-start.12
  244.5 3.3 fusion.16
  247.8 0.0 copy-done.4
  247.8 0.0 copy-done.6
  247.8 0.0 copy-done.10
  247.8 0.0 copy-done.12
  247.8 0.0 copy-start.5
  247.8 0.0 copy-start.7
  247.8 0.0 copy-start.8
  247.8 0.0 copy-start.9
  247.9 5.3 %convolution_convert_fusion = bf16[2048,1024]{1,0:T(8,128)(2,1)} fusion(bf16[384,2048]{1,0:T(8,128)(2,1)S(1)} %copy-done.6, bf16[384,2048]{1,0:T(8,128)(2,1)S(1)} %copy-done.4, bf16[384,1024]{1,0:T(8,128)(2,1)S(1)} %copy-done.10, bf16[384,1024]{1,0:T(8,128)(2,1)S(1)} %copy-done.12), kind=kOutput, calls=%fused_computation | convolution fusion | flops 3232759808 | bytes 8912896 | tf_op jit(solution)/shard_map/dot_general | solution.py:1556
  253.1 0.0 copy-done.5
  253.1 0.0 copy-done.7
  253.1 0.0 copy-done.8
  253.1 0.0 copy-done.9
  253.1 5.2 %convolution_convert_fusion.1 = bf16[1024,2048]{1,0:T(8,128)(2,1)} fusion(bf16[384,2048]{1,0:T(8,128)(2,1)S(1)} %copy-done.5, bf16[384,2048]{1,0:T(8,128)(2,1)S(1)} %copy-done.7, bf16[384,1024]{1,0:T(8,128)(2,1)S(1)} %copy-done.9, bf16[384,1024]{1,0:T(8,128)(2,1)S(1)} %copy-done.8), kind=kOutput, calls=%fused_computation.1 | convolution fusion | flops 3232759808 | bytes 8912896 | tf_op jit(solution)/shard_map/dot_general | solution.py:1556
  258.3 55.1 %attend_back_scatter.1 = (bf16[8,64,384]{2,1,0:T(8,128)(2,1)}, bf16[8,128,384]{2,1,0:T(8,128)(2,1)}, bf16[3,4,2,2,4,48,512]{6,5,4,3,2,1,0:T(8,128)(2,1)}) custom-call(bf16[64,3072]{1,0:T(8,128)(2,1)} %get-tuple-element.107.values_0_, bf16[3,64,3072]{2,1,0:T(8,128)(2,1)} %get-tuple-element.108.values_1_, f32[64,3072]{1,0:T(8,128)} %get-tuple-element.109.values_2_, ...), custom_call_target="tpu_custom_call" | custom-call | tf_op jit(solution)/shard_map/attend_back_scatter/pallas_call | solution.py:512
  313.5 0.0 copy-start
  313.5 48.0 %closing.1 = (bf16[192,1024]{1,0:T(8,128)(2,1)}, f32[2,96,512]{2,1,0:T(8,128)}, f32[16,128]{1,0:T(8,128)}) custom-call(bf16[8,64,384]{2,1,0:T(8,128)(2,1)} %get-tuple-element.124.values_0_, bf16[8,128,384]{2,1,0:T(8,128)(2,1)} %get-tuple-element.125.values_1_, f32[192,1024]{1,0:T(8,128)} %get-tuple-element.126.values_2_, ...), custom_call_target="tpu_custom_call" | custom-call | tf_op jit(solution)/shard_map/closing/pallas_call | solution.py:512
  361.5 0.0 copy-done
  361.5 0.0 copy-start.1
  361.5 1.0 copy-done.1
  362.5 0.0 copy-start.2
  362.5 1.0 copy-done.2
  363.5 0.0 copy-start.3
  363.5 0.7 copy-done.3
  364.2 1.0 unpack.1
  365.2 0.5 slice_bitcast_fusion.3
  365.7 0.5 slice_bitcast_fusion
  (1 shorter events, 0.0 us)
Async XLA Ops:
  212.8 31.6 %copy-start.11 = (bf16[384,1024]{1,0:T(8,128)(2,1)S(1)}, bf16[384,1024]{1,0:T(8,128)(2,1)}, u32[]{:S(2)}) copy-start(bf16[384,1024]{1,0:T(8,128)(2,1)} %get-tuple-element.123) | copy-start | bytes 2359300
  212.9 31.6 %copy-start.13 = (bf16[384,512]{1,0:T(8,128)(2,1)S(1)}, bf16[384,512]{1,0:T(8,128)(2,1)}, u32[]{:S(2)}) copy-start(bf16[384,512]{1,0:T(8,128)(2,1)} %get-tuple-element.120) | copy-start | bytes 1179652
  212.9 31.6 %copy-start.14 = (bf16[384,512]{1,0:T(8,128)(2,1)S(1)}, bf16[384,512]{1,0:T(8,128)(2,1)}, u32[]{:S(2)}) copy-start(bf16[384,512]{1,0:T(8,128)(2,1)} %get-tuple-element.121) | copy-start | bytes 1179652
  244.4 3.4 copy-start.4
  244.4 3.4 copy-start.6
  244.5 3.3 copy-start.10
  244.5 3.3 copy-start.12
  247.8 5.3 %copy-start.5 = (bf16[384,2048]{1,0:T(8,128)(2,1)S(1)}, bf16[384,2048]{1,0:T(8,128)(2,1)}, u32[]{:S(2)}) copy-start(bf16[384,2048]{1,0:T(8,128)(2,1)} %get-tuple-element.115) | copy-start | bytes 4718596
  247.8 5.3 %copy-start.7 = (bf16[384,2048]{1,0:T(8,128)(2,1)S(1)}, bf16[384,2048]{1,0:T(8,128)(2,1)}, u32[]{:S(2)}) copy-start(bf16[384,2048]{1,0:T(8,128)(2,1)} %get-tuple-element.114) | copy-start | bytes 4718596
  247.8 5.3 %copy-start.8 = (bf16[384,1024]{1,0:T(8,128)(2,1)S(1)}, bf16[384,1024]{1,0:T(8,128)(2,1)}, u32[]{:S(2)}) copy-start(bf16[384,1024]{1,0:T(8,128)(2,1)} %get-tuple-element.112) | copy-start | bytes 2359300
  247.8 5.3 %copy-start.9 = (bf16[384,1024]{1,0:T(8,128)(2,1)S(1)}, bf16[384,1024]{1,0:T(8,128)(2,1)}, u32[]{:S(2)}) copy-start(bf16[384,1024]{1,0:T(8,128)(2,1)} %get-tuple-element.113) | copy-start | bytes 2359300
  313.5 48.1 %copy-start = (bf16[192,1024]{1,0:T(8,128)(2,1)S(1)}, bf16[192,1024]{1,0:T(8,128)(2,1)}, u32[]{:S(2)}) copy-start(bf16[192,1024]{1,0:T(8,128)(2,1)} %get-tuple-element.94.result) | copy-start | bytes 1179652
  361.5 1.0 copy-start.1
  362.5 1.0 copy-start.2
  363.5 0.7 copy-start.3

commit v3 on v2

--- a/solution.py
+++ b/solution.py
@@ -139,7 +139,12 @@
 
 EVERY = slice(None)
 CUBE_ALL = (EVERY,) * 4
-SIDES = (pl.ds(0, HALF // 2), pl.ds(HALF // 2, HALF // 2))
+
+
+def side_columns(width, side):
+    return pl.ds(side * (width // 2), width // 2)
+
+
 SIZES = {Y: (4,), X: (2, 2), Z: (4,)}
 GATHER_ORDERS = ((X, Z, Y), (Y, X, Z), (Z, Y, X), (X, Z, Y))
 SCATTER_ORDERS = ((Y, Z, X), (Z, X, Y), (X, Y, Z), (Y, Z, X))
@@ -180,7 +185,7 @@
             come = lax.rem(here[axis] - step + 4, 4)
             index = prefix + cube_index(here, order[:2], axis, come)
             if cut:
-                index += (EVERY, SIDES[side])
+                index += (EVERY, side_columns(cut, side))
             if cut or side == 0:
                 block = buffer.at[index]
                 two.append(wire.to(block, block, moved(here, axis, step)))
@@ -224,8 +229,7 @@
 SCATTER_COPIES = (4, 3, 3)
 
 
-def scatter_slots(order, rows, cut):
-    wide = HALF if cut else 128
+def scatter_slots(order, rows, wide, cut):
     dims = lengths_of(order[1:])
     slots = [
         pltpu.VMEM((2,) + dims + (rows, wide // 2 if cut else wide), BF),
@@ -248,7 +252,7 @@
                 far = prefix + cube_index(here, full, axis, lax.rem(here[axis] + 2, 4))
                 for side, step in enumerate((1, -1)):
                     if cut or side == 0:
-                        block = buffer.at[far + ((EVERY, SIDES[side]) if cut else ())]
+                        block = buffer.at[far + ((EVERY, side_columns(cut, side)) if cut else ())]
                         row.append(wire.to(block, slots[0].at[side], moved(here, axis, step)))
                 ahead.append(row)
             else:
@@ -270,7 +274,7 @@
                     if side < len(row):
                         row[side].wait_recv()
                         half = slots[0]
-                        columns_ = SIDES[side] if cut else EVERY
+                        columns_ = side_columns(cut, side) if cut else EVERY
 
                         def add(
                             i, _, buffer=buffer, prefix=prefix, axis=axis, full=full, value=value,
@@ -533,23 +537,20 @@
     return pltpu.SemaphoreType.DMA((count,))
 
 
-def attend(lengths, pads, qkv, number):
-    def body(refs, semaphores):
-        send, recv, refs.attend_local = semaphores
-        here = place()
-        greet(group(here))
-        refs.arrive()
-        attend_steps(refs, Mail(here, send, recv), lambda slot: None)
-
-    return call(
-        body, "attend", number, dict(qkv=qkv), {}, {}, MIXED_T, ATTEND_SAVED,
-        dict(chances=CHANCES), ATTEND_SCRATCH, MAIL_SEMS + [dma(SLOTS + 1)],
-        dict(lengths=lengths, pads=pads),
-    )
-
-
 PAD = 2 * BLOCK
 PADDED = LENGTH + 2 * PAD
+
+
+def fetch_chances(refs):
+    copies = []
+    for slot in range(SLOTS):
+        blocks = pl.ds(slot * 3, 3)
+        copy = pltpu.make_async_copy(
+            refs.chances.at[blocks], refs.held.at[blocks], refs.attend_local.at[slot]
+        )
+        copy.start()
+        copies.append(copy)
+    refs.early = copies
 
 
 def attend_back_steps(refs, mail_q, mail_kv, between):
@@ -558,14 +559,6 @@
     rows_q, rows_d, turned_d, shift = refs.rows_q, refs.rows_d, refs.turned_d, refs.shift
     total_q, stage_q, stage_kv = refs.total_q, refs.stage_q, refs.stage_kv
     me = mail_q.me
-    kept = []
-    for slot in range(SLOTS):
-        blocks = pl.ds(slot * 3, 3)
-        copy = pltpu.make_async_copy(
-            refs.chances.at[blocks], chances.at[blocks], refs.attend_local.at[slot]
-        )
-        copy.start()
-        kept.append(copy)
     kv[...] = jnp.concatenate([qkv[1], qkv[2]], axis=0).T
     scaled = bfloat(widen(d_mixed[...]) * inverse[...])
     inner = jnp.sum(widen(scaled) * mixed[...], axis=0, keepdims=True)
@@ -583,9 +576,9 @@
     rows_q[middle, :] = jnp.where(left, both, jnp.zeros_like(both))
     rows_d[middle, :] = jnp.where(left, jnp.zeros_like(both), both)
     total_q[...] = jnp.zeros_like(total_q)
+    for copy in refs.early:
+        copy.wait()
     between(-1)
-    for copy in kept:
-        copy.wait()
 
     def step(i):
         first = pl.multiple_of(i * BLOCK, BLOCK)
@@ -653,110 +646,7 @@
 )
 
 
-def attend_back(near, loaded, chances, number):
-    def body(refs, semaphores):
-        send_q, recv_q, send_kv, recv_kv, refs.attend_local = semaphores
-        here = place()
-        greet(group(here))
-        refs.arrive()
-        attend_back_steps(
-            refs, Mail(here, send_q, recv_q), Mail(here, send_kv, recv_kv), lambda slot: None
-        )
-
-    return call(
-        body, "attend_back", number, near, loaded, dict(chances=chances), BACK_OUTPUTS, {}, {},
-        BACK_SCRATCH, MAIL_SEMS + MAIL_SEMS + [dma(SLOTS)],
-    )
-
-
-REST_ROWS = 48
-
-
-def rest_planes(here):
-    return [
-        (part,) + cube_index(here, SCATTER_ORDERS[part][1:], SCATTER_ORDERS[part][0], here[SCATTER_ORDERS[part][0]])
-        for part in range(3)
-    ]
-
-
-def attend_back_scatter(near, loaded, chances, g_in, g_back, g_out, number):
-    slots = [
-        scatter_slots(SCATTER_ORDERS[part], REST_ROWS, True) for part in range(3)
-    ]
-
-    def body(refs, semaphores):
-        send, recv, local, send_q, recv_q, send_kv, recv_kv, refs.attend_local = semaphores
-        here = place()
-        wire = Wire(here, send, recv, local)
-        core = wire.core
-        greet(neighbours(here, (1, -1)) + group(here))
-        refs.arrive()
-        mine = pl.ds(2 * core, 2)
-        own_columns = pl.ds(pl.multiple_of(core * HALF, HALF), HALF)
-        your_columns = pl.ds(pl.multiple_of((1 - core) * HALF, HALF), HALF)
-        blocks = (EVERY,) * 3
-        halves = (
-            (refs.g_back, pl.ds(0, 48), refs.rest.at[(1, mine) + blocks]),
-            (refs.g_back, pl.ds(48, 16), refs.rest.at[(2, mine) + blocks + (pl.ds(16, 16),)]),
-            (refs.g_out, EVERY, refs.rest.at[(2, mine) + blocks + (pl.ds(32, 16),)]),
-        )
-        copies = [
-            wire.swap(ref.at[CUBE_ALL + (rows, your_columns)], target)
-            for ref, rows, target in halves
-        ]
-        copies += [
-            wire.fetch(ref.at[CUBE_ALL + (rows, own_columns)], target)
-            for ref, rows, target in halves
-        ]
-        for k in range(4):
-            source = refs.g_in.at[CUBE_ALL + (EVERY, pl.ds(k * HALF, HALF))]
-            part, low = ((0, 16 * k), (2, 0))[k // 3]
-            copies.append(
-                wire.fetch(source, refs.rest.at[(part,) + CUBE_ALL + (pl.ds(low, 16),)])
-            )
-        arrivals = [
-            [getattr(refs, "slot_%d_%d" % (part, k)) for k in range(2)] for part in range(3)
-        ]
-        stages = ring_scatter(
-            wire,
-            [
-                (refs.rest, (part,), SCATTER_ORDERS[part], True, arrivals[part], None)
-                for part in range(3)
-            ],
-            (0,),
-        )
-
-        def between(slot):
-            if slot == -1:
-                for copy in copies:
-                    copy.wait()
-                advance(stages)
-            elif slot == 0:
-                advance(stages)
-
-        attend_back_steps(
-            refs, Mail(here, send_q, recv_q), Mail(here, send_kv, recv_kv), between
-        )
-        for _ in stages:
-            pass
-        kept = [
-            wire.fetch(refs.rest.at[at], refs.rest_summed.at[at]) for at in rest_planes(here)
-        ]
-        for copy in kept:
-            copy.wait()
-
-    rest = ((3,) + CUBE + (REST_ROWS, HALF), BF)
-    scratch = dict(BACK_SCRATCH, rest=rest)
-    for part in range(3):
-        for k in range(2):
-            scratch["slot_%d_%d" % (part, k)] = slots[part][k]
-    copies = 3 * SCATTER_COPIES[0] + 3
-    return call(
-        body, "attend_back_scatter", number, near, loaded,
-        dict(chances=chances, g_in=g_in, g_back=g_back, g_out=g_out),
-        BACK_OUTPUTS, {}, dict(rest_summed=rest), scratch,
-        [dma(copies), dma(copies), dma(10)] + MAIL_SEMS + MAIL_SEMS + [dma(SLOTS)],
-    )
+REST = ((64, HALF), (80, HALF // 2), (80, HALF // 2))
 
 
 def dot_nt(former, latter):
@@ -775,25 +665,20 @@
         for name in names:
             if name == QKV:
                 pairs = [(refs.gqkv, refs.w_qkv)]
-            elif name == OUT:
-                pairs = [
-                    (refs.rest_three.at[own + (pl.ds(32, 16),)], refs.w_out.at[core]),
-                    (refs.yours_three.at[CUBE_ALL + (pl.ds(16, 16),)], refs.w_out.at[1 - core]),
-                ]
             elif name == IN:
                 pairs = [
                     (refs.rest_one.at[CUBE_ALL + (pl.ds(16 * k, 16),)], refs.w_in.at[k])
-                    for k in range(3)
-                ] + [(refs.rest_three.at[CUBE_ALL + (pl.ds(0, 16),)], refs.w_in.at[3])]
+                    for k in range(4)
+                ]
             else:
-                blocks = (EVERY,) * 4
-                low, high = blocks + (pl.ds(0, 48),), blocks + (pl.ds(48, 16),)
-                pairs = [
-                    (refs.rest_two.at[own], refs.w_back.at[(core,) + low]),
-                    (refs.rest_three.at[own + (pl.ds(16, 16),)], refs.w_back.at[(core,) + high]),
-                    (refs.yours_two, refs.w_back.at[(1 - core,) + low]),
-                    (refs.yours_three.at[CUBE_ALL + (pl.ds(0, 16),)], refs.w_back.at[(1 - core,) + high]),
-                ]
+                rows, target = (pl.ds(0, 64), refs.w_back) if name == BACK else (pl.ds(64, 16), refs.w_out)
+                pairs = []
+                for part, (ref, come) in enumerate(
+                    ((refs.rest_two, refs.yours_two), (refs.rest_three, refs.yours_three))
+                ):
+                    span = (EVERY,) * 5 + (side_columns(HALF, part),)
+                    pairs.append((ref.at[own + (rows,)], target.at[(core,) + span]))
+                    pairs.append((come.at[CUBE_ALL + (rows,)], target.at[(1 - core,) + span]))
             self.pending[name] = [wire.fetch(*pair) for pair in pairs]
 
     def ready(self, name):
@@ -865,8 +750,9 @@
     return v * half, slope
 
 
-def summed_over_cores(refs, wire, number, fill):
-    send, come, kept = refs.outgoing.at[number], refs.incoming.at[number], refs.kept
+def summed_over_cores(refs, wire, fill):
+    send, come, kept = refs.outgoing.at[refs.round], refs.incoming.at[refs.round], refs.kept
+    refs.round += 1
     fill(wire.other, send)
     copy = wire.swap(send, come)
     fill(wire.own, kept)
@@ -888,13 +774,12 @@
         project(wire.own, k)
     copy.wait()
     refs.keep(entry)
+    between()
     copies = []
     for k in range(3):
         project(wire.other, k)
         stage[k] = rows_of[k].T.reshape(CHIPS, HEAD, CHIP_ROWS)
         copies += wire.spread(stage.at[k], refs.qkv.at[k])
-        if k < 2:
-            between()
     return copies
 
 
@@ -907,14 +792,13 @@
 
 def part_post(refs, wire, weights):
     mixed = refs.mixed
-    mixed[...] = refs.mixed_t[...].reshape(HALF, CHIP_ROWS).T
-    refs.keep(mixed)
+    mixed[...] = refs.mixed_t_in[...].reshape(HALF, CHIP_ROWS).T
 
     def leave(rows, target):
         for half in range(2):
             target[:, columns(half)] = dot(mixed[rows, :], weights.out(half))
 
-    branch = summed_over_cores(refs, wire, 0, leave)
+    branch = summed_over_cores(refs, wire, leave)
     normed, factor = normalized(widen(refs.hidden[...]) + branch + vector(refs, B_OUT))
     refs.normed_one[...] = normed
     refs.factor_one[...] = factor
@@ -946,7 +830,7 @@
                 total = total + dot(active[rows, columns(chunk)], weights.back(half, chunk))
             target[:, columns(half)] = total
 
-    second = summed_over_cores(refs, wire, 1, leave_two)
+    second = summed_over_cores(refs, wire, leave_two)
     normed, factor = normalized(refs.first[...] + second + vector(refs, B_BACK))
     refs.normed_two[...] = normed
     refs.factor_two[...] = factor
@@ -991,7 +875,7 @@
             total = total + dot_nt(d_before[rows, columns(chunk)], weights.into(chunk))
         target[...] = total
 
-    d_first = refs.d_second[...] + summed_over_cores(refs, wire, 2, leave)
+    d_first = refs.d_second[...] + summed_over_cores(refs, wire, leave)
     d_inner, g_gain, g_shift = normalize_back(
         d_first, refs.normed_one[...], refs.factor_one[...], vector(refs, GAIN_ATTN)
     )
@@ -1039,7 +923,7 @@
             total = total + dot_nt(rows_of[k, rows, :], weights.qkv(k))
         target[...] = total
 
-    return refs.d_inner[...] + summed_over_cores(refs, wire, 3, leave)
+    return refs.d_inner[...] + summed_over_cores(refs, wire, leave)
 
 
 ROW_F32 = ((ROWS, D), F32)
@@ -1048,12 +932,15 @@
 WIDE_BF = ((CHIP_ROWS, 2048), BF)
 HEADS_BF = ((CHIP_ROWS, HALF), BF)
 STAGE = (CHIPS, HEAD, CHIP_ROWS)
-PROJECT, POST, BACK_DENSE, BACK_PROJECT = range(4)
+PROJECT, POST, BACK_DENSE, BACK_PROJECT, ATTEND, ATTEND_BACK, GRADIENTS = range(7)
+WHOLE_GRADIENTS = dict(
+    g_in=(CUBE + (16, 2048), BF), g_back=((2, 2, 2, 4, 64, D), BF), g_out=((2, 2, 2, 4, 16, D), BF)
+)
 PARTS = (
     (
         (QKV,),
-        dict(entry=CHIP_BF),
-        dict(qkv=((3, HEAD, LENGTH), BF)),
+        dict(entry=CHIP_BF, qkv=((3, HEAD, LENGTH), BF)),
+        {},
         dict(qkv_rows=((3, CHIP_ROWS, HALF), BF), qkv_stage=((3,) + STAGE, BF)),
         1 + 3 * 7,
         3,
@@ -1061,11 +948,11 @@
     (
         (OUT, IN, BACK),
         dict(
-            mixed=HEADS_BF, normed_one=ROW_F32, factor_one=COLUMN_F32, entry_two=CHIP_BF,
+            normed_one=ROW_F32, factor_one=COLUMN_F32, entry_two=CHIP_BF,
             active=WIDE_BF, slope=WIDE_BF, normed_two=ROW_F32, factor_two=COLUMN_F32,
         ),
         {},
-        dict(first=ROW_F32),
+        dict(first=ROW_F32, mixed=HEADS_BF),
         4,
         0,
     ),
@@ -1088,6 +975,9 @@
         1,
         0,
     ),
+    ((), ATTEND_SAVED, MIXED_T, ATTEND_SCRATCH, 0, 0),
+    ((), {}, BACK_OUTPUTS, BACK_SCRATCH, 0, 0),
+    ((), WHOLE_GRADIENTS, {}, {}, 0, 0),
 )
 WEIGHT_SHAPES = (
     dict(w_qkv=((3,) + CUBE + (16, HALF), BF)),
@@ -1097,12 +987,34 @@
 )
 
 
-WEIGHT_COPIES = (1, 2, 4, 4)
-
-
-def dense(parts, number, gathered, near, loaded, extra, dropped=()):
-    outputs, saved, weight_names = {}, dict(extra), []
-    scratch = dict(outgoing=((4, ROWS, D), F32), incoming=((4, ROWS, D), F32), kept=ROW_F32)
+WEIGHT_COPIES = (1, 4, 4, 4)
+
+
+def weight_gradients(refs, mixed_t, add):
+    def store(ref, at, value):
+        value = value.reshape(ref[at].shape)
+        ref[at] = bfloat(value + widen(ref[at])) if add else bfloat(value)
+
+    turned = refs.entry_two[...].T
+    for chunk in range(4):
+        value = dot(turned, refs.d_before[:, columns(chunk)])
+        store(refs.g_in, CUBE_ALL + (EVERY, columns(chunk)), value)
+    refs.keep(refs.g_in)
+    for chunk in range(4):
+        value = dot(refs.active[:, columns(chunk)].T, refs.d_branch[...])
+        store(refs.g_back, (chunk // 2, chunk % 2), value)
+    refs.keep(refs.g_back)
+    store(refs.g_out, CUBE_ALL, dot(mixed_t.reshape(HALF, CHIP_ROWS), refs.d_attn[...]))
+    refs.keep(refs.g_out)
+
+
+def dense(
+    parts, number, gathered, near, loaded, extra, dropped=(), sources={}, scalars={}, added={}
+):
+    outputs, saved, far, weight_names, sems = {}, dict(extra), {}, [], []
+    rounds = 2 * (POST in parts) + (BACK_DENSE in parts) + (BACK_PROJECT in parts)
+    sums = ((rounds, ROWS, D), F32)
+    scratch = dict(outgoing=sums, incoming=sums, kept=ROW_F32)
     copies = locals_ = 0
     for part in parts:
         its_weights, its_saved, its_outputs, its_scratch, its_copies, its_locals = PARTS[part]
@@ -1113,18 +1025,32 @@
         copies += its_copies
         locals_ += its_locals
     for name in dropped:
-        scratch[name] = saved.pop(name)
+        scratch[name] = {**saved, **outputs}[name]
+        saved.pop(name, None)
+        outputs.pop(name, None)
     for name in weight_names:
         scratch.update(WEIGHT_SHAPES[name])
         locals_ += WEIGHT_COPIES[name]
+    if ATTEND in parts:
+        far.update(chances=CHANCES)
+        sems = MAIL_SEMS + [dma(SLOTS + 1)]
+    if ATTEND_BACK in parts:
+        sems = MAIL_SEMS + MAIL_SEMS + [dma(SLOTS)]
 
     def body(refs, semaphores):
         here = place()
-        wire = Wire(here, *semaphores)
+        wire = Wire(here, *semaphores[:3])
+        refs.round = 0
         weights = Weights(refs, wire, weight_names)
+        partial = [
+            wire.fetch(getattr(refs, key + LATER), getattr(refs, key)) for key in added
+        ]
         if BACK_DENSE in parts:
             refs.sums[...] = jnp.zeros((8, D), F32)
             refs.sums_in[...] = jnp.zeros((1, FF), F32)
+        if ATTEND_BACK in parts:
+            refs.attend_local = semaphores[-1]
+            fetch_chances(refs)
         greet([partner(here)] + group(here))
         refs.arrive()
         pending = []
@@ -1140,12 +1066,30 @@
                 if POST in parts:
                     value = widen(refs.cotangent[...])
                 pending += part_back_dense(refs, wire, weights, value)
-            else:
+            elif part == BACK_PROJECT:
                 turn_gradients(refs)
                 refs.keep(refs.d_qkv)
                 add_half(refs, wire, B_QUERY, row_sum(refs.d_qkv[0]))
                 add_half(refs, wire, B_VALUE, row_sum(refs.d_qkv[2]))
                 value = part_back_project(refs, wire, weights)
+            elif part == GRADIENTS:
+                for copy in partial:
+                    copy.wait()
+                weight_gradients(refs, refs.mixed_t_in[...], bool(added))
+            else:
+                for copy in pending:
+                    copy.wait()
+                pending = []
+                if part == ATTEND:
+                    send, recv, refs.attend_local = semaphores[3:]
+                    refs.keep(refs.qkv)
+                    attend_steps(refs, Mail(here, send, recv), lambda slot: None)
+                else:
+                    send, recv, send_two, recv_two, _ = semaphores[3:]
+                    attend_back_steps(
+                        refs, Mail(here, send, recv), Mail(here, send_two, recv_two),
+                        lambda slot: None,
+                    )
         for copy in pending:
             copy.wait()
 
@@ -1153,12 +1097,16 @@
         body, "dense_%d" % number, number, near,
         dict(loaded, vecs=gathered.vecs, b_in=gathered.b_in),
         dict(
-            gqkv=gathered.gqkv, rest_one=gathered.rest_one, rest_two=gathered.rest_two,
+            sources, gqkv=gathered.gqkv, rest_one=gathered.rest_one, rest_two=gathered.rest_two,
             rest_three=gathered.rest_three, yours_two=gathered.yours_two,
             yours_three=gathered.yours_three,
+            **{key + LATER: value for key, value in added.items()},
         ),
-        outputs, saved, {}, scratch, [dma(copies), dma(copies), dma(locals_)],
-    )
+        outputs, saved, far, scratch, [dma(copies), dma(copies), dma(locals_ + 3)] + sems, scalars,
+    )
+
+
+LATER = "_later"
 
 
 def opening(lengths, pads, shards, vectors, tokens, number):
@@ -1211,12 +1159,13 @@
 
             for k in range(3):
                 refs.own_qkv[k] = both(8 * k)
-                refs.own_rest[0, 16 * k : 16 * k + 16, :] = both(24 + 8 * k)
+                refs.own_one[16 * k : 16 * k + 16, :] = both(24 + 8 * k)
+            refs.own_one[48:64, :] = both(80)
             back = bfloat(jnp.concatenate([low[48:80], high[48:80]], axis=0))
-            refs.own_rest[1] = back[:48]
-            refs.own_rest[2, 0:16, :] = both(80)
-            refs.own_rest[2, 16:32, :] = back[48:]
-            refs.own_rest[2, 32:48, :] = both(88)
+            out = both(88)
+            for ref, span in ((refs.own_two, slice(0, 256)), (refs.own_three, slice(256, 512))):
+                ref[0:64, :] = back[:, span]
+                ref[64:80, :] = out[:, span]
 
         @pl.when(core == 0)
         def _():
@@ -1232,10 +1181,10 @@
             pass
 
         parts = [
-            (refs.w_qkv, (k,), GATHER_ORDERS[k], refs.own_qkv.at[k], True, nothing)
+            (refs.w_qkv, (k,), GATHER_ORDERS[k], refs.own_qkv.at[k], HALF, nothing)
             for k in range(3)
         ]
-        parts.append((refs.all_small, (), GATHER_ORDERS[3], refs.own_small, False, nothing))
+        parts.append((refs.all_small, (), GATHER_ORDERS[3], refs.own_small, 0, nothing))
         first_stages = ring_gather(wire, parts)
         yours = pl.ds(2 * (1 - core), 2)
         passed = []
@@ -1250,27 +1199,24 @@
         def pass_three(value):
             passed.append(
                 wire.swap(
-                    refs.rest_three.at[yours, value % 2, value // 2, :, pl.ds(16, 32)],
+                    refs.rest_three.at[yours, value % 2, value // 2],
                     refs.yours_three.at[:, value % 2, value // 2],
                 )
             )
 
+        long_stages = ring_gather(
+            wire, [(refs.rest_one, (), GATHER_ORDERS[0], refs.own_one, HALF, nothing)]
+        )
         stages = ring_gather(
             wire,
             [
-                (ref, (), GATHER_ORDERS[part], refs.own_rest.at[part], True, complete)
-                for part, (ref, complete) in enumerate(
-                    (
-                        (refs.rest_one, nothing),
-                        (refs.rest_two, pass_two),
-                        (refs.rest_three, pass_three),
-                    )
-                )
+                (refs.rest_two, (), GATHER_ORDERS[1], refs.own_two, HALF // 2, pass_two),
+                (refs.rest_three, (), GATHER_ORDERS[2], refs.own_three, HALF // 2, pass_three),
             ],
         )
-        for _ in range(2):
-            advance(first_stages)
-            advance(stages)
+        for ring in (first_stages, long_stages, stages, first_stages, first_stages, long_stages):
+            advance(ring)
+        advance(stages)
         for _ in first_stages:
             pass
         kept = wire.fetch(refs.w_qkv, refs.gqkv)
@@ -1285,7 +1231,7 @@
                 refs.b_in[:, low : low + 128] = tile[8 + j : 9 + j]
         refs.keep(refs.vecs, refs.b_in)
         pending = project_rows(
-            refs, wire, lambda k: refs.w_qkv[k].reshape(D, HALF), entry_copy, lambda: None
+            refs, wire, lambda k: refs.w_qkv[k].reshape(D, HALF), entry_copy, lambda: advance(long_stages)
         )
         for copy in pending:
             copy.wait()
@@ -1294,9 +1240,13 @@
 
         def between(slot):
             if slot == 2:
+                advance(long_stages)
+            elif slot == 3:
                 advance(stages)
 
         attend_steps(refs, Mail(here, mail_send, mail_recv), between)
+        for _ in long_stages:
+            pass
         for _ in stages:
             pass
         for copy in passed:
@@ -1306,11 +1256,12 @@
     scratch = dict(
         ATTEND_SCRATCH, pack=((2, 96, HALF), BF), small=((16, 128), BF), theirs=((96, HALF), BF),
         small_theirs=((16, 128), BF),
-        own_qkv=((3, 16, HALF), BF), own_rest=((3, REST_ROWS, HALF), BF), own_small=((16, 128), BF),
+        own_qkv=((3, 16, HALF), BF), own_one=((64, HALF), BF), own_two=((80, HALF // 2), BF), own_three=((80, HALF // 2), BF), own_small=((16, 128), BF),
         w_qkv=((3,) + CUBE + (16, HALF), BF), all_small=(CUBE + (16, 128), BF),
         qkv_rows=((3, CHIP_ROWS, HALF), BF), qkv_stage=((3,) + STAGE, BF),
     )
-    rest = (CUBE + (REST_ROWS, HALF), BF)
+    narrow = (CUBE + (80, HALF // 2), BF)
+    come = ((2, 2, 2, 4, 80, HALF // 2), BF)
     copies = 3 + 7 * GATHER_COPIES + 8 + 21
     return call(
         body, "opening", number, dict(vectors=vectors), dict(shards, tokens=tokens), {}, MIXED_T,
@@ -1319,47 +1270,84 @@
             b_in=((1, FF), F32),
         ),
         dict(
-            chances=CHANCES, gqkv=((3,) + CUBE + (16, HALF), BF), rest_one=rest, rest_two=rest,
-            rest_three=rest, yours_two=((2, 2, 2, 4, 48, HALF), BF),
-            yours_three=((2, 2, 2, 4, 32, HALF), BF),
+            chances=CHANCES, gqkv=((3,) + CUBE + (16, HALF), BF), rest_one=(CUBE + (64, HALF), BF),
+            rest_two=narrow, rest_three=narrow, yours_two=come, yours_three=come,
         ),
         scratch, [dma(copies), dma(copies), dma(11)] + MAIL_SEMS + [dma(SLOTS + 1)],
         dict(lengths=lengths, pads=pads),
     )
 
 
-def closing(near, loaded, gqkv, rest_summed, number):
+def closing(near, loaded, sources, number):
+    rest_slots = [scatter_slots(order, *REST[k], True) for k, order in enumerate(SCATTER_ORDERS[:3])]
+
     def body(refs, semaphores):
+        send, recv, local, send_q, recv_q, send_kv, recv_kv, refs.attend_local = semaphores
         here = place()
-        wire = Wire(here, *semaphores)
+        wire = Wire(here, send, recv, local)
         core = wire.core
-        planes = [
-            wire.fetch(refs.rest_summed.at[at], refs.rest.at[at]) for at in rest_planes(here)
+        refs.round = 0
+        fetch_chances(refs)
+        weights = Weights(refs, wire, (QKV,))
+        greet(neighbours(here, (1, -1, 2)) + group(here))
+        mine = pl.ds(2 * core, 2)
+        blocks = (EVERY,) * 3
+        halves = [
+            (ref, (mine,) + blocks + (rows,), gradient, side)
+            for side, ref in enumerate((refs.rest_two, refs.rest_three))
+            for rows, gradient in ((pl.ds(0, 64), refs.g_back), (pl.ds(64, 16), refs.g_out))
         ]
-        weights = Weights(refs, wire, (QKV,))
-        rest_slots = [
-            [None] * 2 + [getattr(refs, "late_%d_%d" % (part, k)) for k in (2, 3)]
-            for part in range(3)
+
+        def part_columns(half, side):
+            low = pl.multiple_of(half * HALF + side * (HALF // 2), HALF // 2)
+            return CUBE_ALL + (EVERY, pl.ds(low, HALF // 2))
+
+        copies = [
+            wire.swap(gradient.at[part_columns(1 - core, side)], ref.at[at])
+            for ref, at, gradient, side in halves
         ]
+        copies += [
+            wire.fetch(gradient.at[part_columns(core, side)], ref.at[at])
+            for ref, at, gradient, side in halves
+        ]
+        for k in range(4):
+            source = refs.g_in.at[CUBE_ALL + (EVERY, pl.ds(k * HALF, HALF))]
+            copies.append(wire.fetch(source, refs.rest_one.at[CUBE_ALL + (pl.ds(16 * k, 16),)]))
+        refs.arrive()
 
         def keep_rest(part):
             def store(value):
-                refs.sums_rest[part] = value
+                (refs.sums_one, refs.sums_two, refs.sums_six)[part][...] = value
 
             return store
 
+        rest_arrivals = [
+            [getattr(refs, "rest_%d_%d" % (part, k)) for k in range(4)] for part in range(3)
+        ]
         rest_stages = ring_scatter(
             wire,
             [
-                (refs.rest, (part,), SCATTER_ORDERS[part], True, rest_slots[part], keep_rest(part))
-                for part in range(3)
+                (ref, (), SCATTER_ORDERS[part], REST[part][1], rest_arrivals[part], keep_rest(part))
+                for part, ref in enumerate((refs.rest_one, refs.rest_two, refs.rest_three))
             ],
-            (1, 2),
+            (0, 1, 2),
         )
-        greet(neighbours(here, (1, -1, 2)))
-        refs.arrive()
-        for copy in planes:
-            copy.wait()
+
+        def between(slot):
+            if slot == -1:
+                for copy in copies:
+                    copy.wait()
+                advance(rest_stages)
+                turned = refs.entry_later[...].T
+                for k in range(3):
+                    total = dot(turned, refs.d_qkv_later[k])
+                    refs.gradients[k] = bfloat(total).reshape(CUBE + (16, HALF))
+            elif slot == 0:
+                advance(rest_stages)
+
+        attend_back_steps(
+            refs, Mail(here, send_q, recv_q), Mail(here, send_kv, recv_kv), between
+        )
         advance(rest_stages)
         turn_gradients(refs)
         refs.sums[...] = refs.sums_three[...] + refs.sums_four[...]
@@ -1367,10 +1355,10 @@
         add_half(refs, wire, B_QUERY, row_sum(refs.d_qkv[0]))
         add_half(refs, wire, B_VALUE, row_sum(refs.d_qkv[2]))
         swaps = [wire.swap(refs.sums, refs.sums_come), wire.swap(refs.sums_in, refs.in_come)]
+        turned = refs.entry[...].T
         for k in range(3):
-            total = dot(refs.entry[...].T, refs.d_qkv[k])
-            total = total + dot(refs.entry_later[...].T, refs.d_qkv_later[k])
-            refs.gradients[k] = bfloat(total).reshape(CUBE + (16, HALF))
+            total = dot(turned, refs.d_qkv[k]).reshape(CUBE + (16, HALF))
+            refs.gradients[k] = bfloat(widen(refs.gradients[k]) + total)
             if k == 1:
                 advance(rest_stages)
         for copy in swaps:
@@ -1401,10 +1389,10 @@
             [getattr(refs, "slot_%d_%d" % (part, k)) for k in range(4)] for part in range(4)
         ]
         parts = [
-            (refs.gradients, (part,), SCATTER_ORDERS[part], True, arrivals[part], keep(part))
+            (refs.gradients, (part,), SCATTER_ORDERS[part], HALF, arrivals[part], keep(part))
             for part in range(3)
         ]
-        parts.append((refs.small_sums, (), SCATTER_ORDERS[3], False, arrivals[3], keep(3)))
+        parts.append((refs.small_sums, (), SCATTER_ORDERS[3], 0, arrivals[3], keep(3)))
         stages = ring_scatter(wire, parts, (0, 1, 2))
         advance(stages)
         for _ in rest_stages:
@@ -1415,16 +1403,15 @@
             pass
 
         def finish(own):
-            rest = refs.sums_rest
+            def both(low, count):
+                span = slice(low, low + count)
+                return jnp.concatenate([refs.sums_two[span, :], refs.sums_six[span, :]], axis=1)
+
             rows = [refs.final[k, 8 * own : 8 * own + 8, :] for k in range(3)]
-            rows.append(rest[2, 32 + 8 * own : 40 + 8 * own, :])
-            for k in range(3):
-                rows.append(rest[0, 16 * k + 8 * own : 16 * k + 8 * own + 8, :])
-            rows.append(rest[2, 8 * own : 8 * own + 8, :])
-            if own == 0:
-                rows.append(rest[1, 0:32, :])
-            else:
-                rows += [rest[1, 32:48, :], rest[2, 16:32, :]]
+            rows.append(both(64 + 8 * own, 8))
+            for k in range(4):
+                rows.append(refs.sums_one[16 * k + 8 * own : 16 * k + 8 * own + 8, :])
+            rows.append(both(32 * own, 32))
             return jnp.concatenate(rows, axis=0)
 
         @pl.when(core == 0)
@@ -1440,29 +1427,30 @@
         wire.swap(refs.leaving, refs.landed.at[core]).wait()
     few = ((8, D), F32)
     scratch = dict(
-        outgoing=((4, ROWS, D), F32), incoming=((4, ROWS, D), F32), kept=ROW_F32,
-        d_qkv=((3, CHIP_ROWS, HALF), BF), sums=few, sums_in=((1, FF), F32), sums_come=few,
+        BACK_SCRATCH, **BACK_OUTPUTS, outgoing=((1, ROWS, D), F32), incoming=((1, ROWS, D), F32),
+        kept=ROW_F32, d_qkv=((3, CHIP_ROWS, HALF), BF), sums=few, sums_in=((1, FF), F32), sums_come=few,
         in_come=((1, FF), F32), gradients=((3,) + CUBE + (16, HALF), BF),
         small_sums=(CUBE + (16, 128), BF), final=((3, 16, HALF), F32),
-        leaving=((96, HALF), F32), sums_rest=((3, REST_ROWS, HALF), F32),
-        rest=((3,) + CUBE + (REST_ROWS, HALF), BF),
+        leaving=((96, HALF), F32), sums_one=(REST[0], F32), sums_two=(REST[1], F32),
+        sums_six=(REST[2], F32), rest_one=(CUBE + REST[0], BF), rest_two=(CUBE + REST[1], BF),
+        rest_three=(CUBE + REST[2], BF),
     )
     scratch.update(WEIGHT_SHAPES[QKV])
     for part in range(4):
-        slots = scatter_slots(SCATTER_ORDERS[part], 16, part < 3)
+        slots = scatter_slots(SCATTER_ORDERS[part], 16, HALF if part < 3 else 128, part < 3)
         for k in range(4):
             scratch["slot_%d_%d" % (part, k)] = slots[k]
-        if part < 3:
-            slots = scatter_slots(SCATTER_ORDERS[part], REST_ROWS, True)
-            for k in (2, 3):
-                scratch["late_%d_%d" % (part, k)] = slots[k]
-    copies = 4 * sum(SCATTER_COPIES) + 3 * sum(SCATTER_COPIES[1:]) + 4
+    for part in range(3):
+        for k in range(4):
+            scratch["rest_%d_%d" % (part, k)] = rest_slots[part][k]
+    copies = 7 * sum(SCATTER_COPIES) + 8
     return call(
-        body, "closing", number, near, loaded, dict(gqkv=gqkv, rest_summed=rest_summed),
+        body, "closing", number, near, loaded, sources,
         dict(
             d_tokens=((ROWS, D), BF), landed=((2, 96, HALF), F32), tiny=((16, 128), F32),
         ),
-        {}, {}, scratch, [dma(copies), dma(copies), dma(4)],
+        {}, {}, scratch,
+        [dma(copies), dma(copies), dma(9)] + MAIL_SEMS + MAIL_SEMS + [dma(SLOTS)],
     )
 
 
@@ -1525,62 +1513,43 @@
         widen(vectors)[None], tokens, 0,
     )
     two = dense(
-        (POST, PROJECT), 2, one, dict(mixed_t=one.mixed_t), dict(hidden=tokens),
-        dict(result=ROW_F32),
-    )
-    two_attend = attend(doc_lengths, pad_counts, two.qkv, 3)
+        (POST, PROJECT, ATTEND), 2, one, dict(mixed_t_in=one.mixed_t), dict(hidden=tokens),
+        dict(result=ROW_F32), scalars=dict(lengths=doc_lengths, pads=pad_counts),
+    )
     three = dense(
-        (POST, BACK_DENSE), 4, one, dict(mixed_t=two_attend.mixed_t),
-        dict(hidden=two.result, cotangent=cotangent), dict(result=((ROWS, D), BF)),
-        ("normed_one", "factor_one", "normed_two", "factor_two", "slope"),
-    )
-    back_two = attend_back(
-        dict(d_mixed=three.d_mixed),
-        dict(qkv=two.qkv, mixed_head=two_attend.mixed_head, inverse=two_attend.inverse),
-        two_attend.chances, 5,
+        (POST, BACK_DENSE, GRADIENTS, ATTEND_BACK), 4, one, dict(mixed_t_in=two.mixed_t),
+        dict(
+            hidden=two.result, cotangent=cotangent, qkv=two.qkv, mixed_head=two.mixed_head,
+            inverse=two.inverse,
+        ),
+        dict(result=((ROWS, D), BF)),
+        (
+            "normed_one", "factor_one", "entry_two", "active", "slope", "normed_two",
+            "factor_two", "d_branch", "d_before", "d_attn", "d_mixed",
+        ),
+        dict(chances=two.chances),
     )
     four = dense(
-        (BACK_PROJECT, BACK_DENSE), 6, one,
-        dict(d_q_t=back_two.d_q_t, d_kv_t=back_two.d_kv_t),
+        (BACK_PROJECT, BACK_DENSE, GRADIENTS), 6, one, dict(d_q_t=three.d_q_t, d_kv_t=three.d_kv_t),
         dict(
             d_inner=three.d_inner_out, normed_one=two.normed_one, factor_one=two.factor_one,
             normed_two=two.normed_two, factor_two=two.factor_two, slope=two.slope,
+            entry_two=two.entry_two, active=two.active, mixed_t_in=one.mixed_t,
         ),
-        {},
-    )
-
-    def gradient(one_former, one_latter, two_former, two_latter):
-        former = jnp.concatenate([one_former, two_former], axis=0)
-        latter = jnp.concatenate([one_latter, two_latter], axis=0)
-        return bfloat(
-            lax.dot_general(
-                former, latter, (((0,), (0,)), ((), ())), preferred_element_type=F32
-            )
-        )
-
-    half_cube = (2, 2, 2, 4)
-    back_one = attend_back_scatter(
+        {}, ("d_branch", "d_before", "d_attn"),
+        added=dict(g_in=three.g_in, g_back=three.g_back, g_out=three.g_out),
+    )
+    last = closing(
         dict(d_mixed=four.d_mixed),
-        dict(qkv=one.qkv, mixed_head=one.mixed_head, inverse=one.inverse),
-        one.chances,
-        gradient(two.entry_two, four.d_before, three.entry_two, three.d_before).reshape(
-            CUBE + (16, 2048)
+        dict(
+            qkv=one.qkv, mixed_head=one.mixed_head, inverse=one.inverse, d_inner=four.d_inner_out,
+            entry=one.entry, entry_later=two.entry, d_qkv_later=four.d_qkv, sums_three=three.sums,
+            sums_four=four.sums, in_three=three.sums_in, in_four=four.sums_in,
         ),
-        gradient(two.active, four.d_branch, three.active, three.d_branch).reshape(
-            half_cube + (64, D)
+        dict(
+            chances=one.chances, gqkv=one.gqkv, g_in=four.g_in, g_back=four.g_back, g_out=four.g_out
         ),
-        gradient(two.mixed, four.d_attn, three.mixed, three.d_attn).reshape(half_cube + (16, D)),
-        7,
-    )
-    last = closing(
-        dict(d_q_t=back_one.d_q_t, d_kv_t=back_one.d_kv_t),
-        dict(
-            d_inner=four.d_inner_out,
-            entry=one.entry, entry_later=two.entry, d_qkv_later=four.d_qkv,
-            sums_three=three.sums, sums_four=four.sums,
-            in_three=three.sums_in, in_four=four.sums_in,
-        ),
-        one.gqkv, back_one.rest_summed, 8,
+        8,
     )
     result, d_tokens, g_query, g_key, g_value, g_out, g_in, g_back, lines = unpack(
         three.result, last.d_tokens, last.landed, last.tiny

time: 372 us -> 337 us (0.906)
  Pallas kernels: 346 us -> 325 us
  matrix products: 13.7 us -> 0 us
    pallas_call x8 -> x5, Pallas kernels: 345 us -> 324 us  [call(): pl.pallas_call(kernel, out_shape=tuple((jax.ShapeDtypeStruct(*spec) for s...]
    dot_general x3 -> x0, matrix products: 13.7 us -> none  [gradient(): lax.dot_general(former, latter, (((0,), (0,)), ((), ())), preferred_eleme...]
where the time goes in v3:
time: 337 us; the launch traced here: 332 us
  Pallas kernels  325 us (96%)
  local copies, waits for them, and re-layouts  4.63 us (1%)
    pallas_call x5, Pallas kernels, call(): pl.pallas_call(kernel, out_shape=tuple((jax.ShapeDtypeStruct(*spec) for s...  324 us

profile of v3, /device:TPU:1, one launch (start us, length us, event | category | flops | bytes accessed | tf_op | source)
XLA Modules:
  0.0 331.9 jit_solution(2147929915155168567)
XLA Ops:
  1.3 0.9 concatenate.37
  2.2 0.5 convert_element_type.10.values_2_
  2.7 90.7 %opening.1 = (bf16[8,64,384]{2,1,0:T(8,128)(2,1)}, f32[64,3072]{1,0:T(8,128)}, f32[1,3072]{1,0:T(1,128)}, bf16[384,1024]{1,0:T(8,128)(2,1)}, bf16[3,64,3072]{2,1...) custom-call(s32[1,4]{1,0:T(1,128)} %values_0_.3, ...), custom_call_target="tpu_custom_call" | custom-call | tf_op jit(solution)/shard_map/opening/pallas_call | solution.py:516
  93.5 48.0 %dense_2.1 = (bf16[8,64,384]{2,1,0:T(8,128)(2,1)}, f32[192,1024]{1,0:T(8,128)}, f32[192,1024]{1,0:T(8,128)}, f32[192,1]{1,0:T(8,128)}, bf16[384,1024]{1,0:T(8,12...) custom-call(s32[1,4]{1,0:T(1,128)} %values_0_.3, ...), custom_call_target="tpu_custom_call" | custom-call | tf_op jit(solution)/shard_map/dense_2/pallas_call | solution.py:516
  141.4 55.3 %dense_4.1 = (bf16[8,64,384]{2,1,0:T(8,128)(2,1)}, bf16[8,128,384]{2,1,0:T(8,128)(2,1)}, bf16[192,1024]{1,0:T(8,128)(2,1)}, f32[192,1024]{1,0:T(8,128)}, f32[8,1...) custom-call(bf16[8,64,384]{2,1,0:T(8,128)(2,1)} %get-tuple-element.8, ...), custom_call_target="tpu_custom_call" | custom-call | tf_op jit(solution)/shard_map/dense_4/pallas_call | solution.py:516
  196.7 29.0 %dense_6.1 = (bf16[64,3072]{1,0:T(8,128)(2,1)}, bf16[3,384,512]{2,1,0:T(8,128)(2,1)}, f32[192,1024]{1,0:T(8,128)}, f32[8,1024]{1,0:T(8,128)}, f32[1,4096]{1,0:T(...) custom-call(bf16[8,64,384]{2,1,0:T(8,128)(2,1)} %get-tuple-element.9, ...), custom_call_target="tpu_custom_call" | custom-call | tf_op jit(solution)/shard_map/dense_6/pallas_call | solution.py:516
  225.8 0.0 copy-start
  225.8 101.0 %closing.1 = (bf16[192,1024]{1,0:T(8,128)(2,1)}, f32[2,96,512]{2,1,0:T(8,128)}, f32[16,128]{1,0:T(8,128)}) custom-call(bf16[64,3072]{1,0:T(8,128)(2,1)} %get-tuple-element.103.values_0_, bf16[3,64,3072]{2,1,0:T(8,128)(2,1)} %get-tuple-element.104.values_1_, f32[64,3072]{1,0:T(8,128)} %get-tuple-element.105.values_2_, ...), custom_call_target="tpu_custom_call" | custom-call | tf_op jit(solution)/shard_map/closing/pallas_call | solution.py:516
  326.9 0.0 copy-done
  326.9 0.0 copy-start.1
  326.9 1.0 copy-done.1
  327.9 0.0 copy-start.2
  327.9 1.0 copy-done.2
  328.9 0.0 copy-start.3
  328.9 0.7 copy-done.3
  329.6 1.0 unpack.1
  330.6 0.5 slice_bitcast_fusion.3
  331.1 0.5 slice_bitcast_fusion
  (1 shorter events, 0.0 us)
Async XLA Ops:
  225.8 101.1 %copy-start = (bf16[192,1024]{1,0:T(8,128)(2,1)S(1)}, bf16[192,1024]{1,0:T(8,128)(2,1)}, u32[]{:S(2)}) copy-start(bf16[192,1024]{1,0:T(8,128)(2,1)} %get-tuple-element.89.result) | copy-start | bytes 1179652
  326.9 1.0 copy-start.1
  327.9 1.0 copy-start.2
  328.9 0.7 copy-start.3
